TPU v7x, 32 devices: a whole 2x2x4 slice. The times are simulated.
32 devices in a mesh: dp: 8 (over z, y), mp: 4 (over x, core).
Axes of the slice: x: 2, y: 2, z: 4, core: 2. Of those that a mesh axis runs over, the one named last changes fastest.
Arguments:
- hidden: bfloat16 [8192, 1152], P('dp'), may hold values from -6 to 6
- segment_ids: int32 [8, 1024], P('dp'), may hold values from 0 to 2, never falling along the last dimension, each value on 1 to 768 neighbouring positions
- w_query: bfloat16 [1152, 1024], P(None, 'mp'), may hold values from -0.1875 to 0.1875
- w_key: bfloat16 [1152, 256], replicated, may hold values from -0.1875 to 0.1875
- w_value: bfloat16 [1152, 256], replicated, may hold values from -0.1875 to 0.1875
- w_out: bfloat16 [1024, 1152], P('mp'), may hold values from -0.1875 to 0.1875
- w_gate: bfloat16 [1152, 6912], P(None, 'mp'), may hold values from -0.1875 to 0.1875
- w_up: bfloat16 [1152, 6912], P(None, 'mp'), may hold values from -0.1875 to 0.1875
- w_down: bfloat16 [6912, 1152], P('mp'), may hold values from -0.078125 to 0.078125
- gain_in: float32 [1152], replicated, may hold values from 0.25 to 1.75
- gain_post_attn: float32 [1152], replicated, may hold values from 0.25 to 1.75
- gain_pre_ffn: float32 [1152], replicated, may hold values from 0.25 to 1.75
- gain_post_ffn: float32 [1152], replicated, may hold values from 0.25 to 1.75
- gain_query: float32 [256], replicated, may hold values from 0.25 to 1.75
- gain_key: float32 [256], replicated, may hold values from 0.25 to 1.75
- cotangent: bfloat16 [8192, 1152], P('dp'), may hold values from -6 to 6
Outputs:
- output: bfloat16 [8192, 1152], P('dp')
- grad_hidden: bfloat16 [8192, 1152], P('dp')
- grad_w_query: float32 [1152, 1024], P(None, 'mp')
- grad_w_key: float32 [1152, 256], replicated
- grad_w_value: float32 [1152, 256], replicated
- grad_w_out: float32 [1024, 1152], P('mp')
- grad_w_gate: float32 [1152, 6912], P(None, 'mp')
- grad_w_up: float32 [1152, 6912], P(None, 'mp')
- grad_w_down: float32 [6912, 1152], P('mp')
- grad_gain_in: float32 [1152], replicated
- grad_gain_post_attn: float32 [1152], replicated
- grad_gain_pre_ffn: float32 [1152], replicated
- grad_gain_post_ffn: float32 [1152], replicated
- grad_gain_query: float32 [256], replicated
- grad_gain_key: float32 [256], replicated
Inputs may be any that keep to these rules, and one draw needn't show every extreme that they name: `segment_ids`: in each row (1024 tokens of one group) document numbers never fall, each of the 3 documents has a token, and the longest has exactly 768 tokens.
All inputs are finite; a program needn't handle non-finite values.
Results may differ from a plain program's by a relative error of at most 0.017.
Values sent between devices are 32-bit elements; how exact they have to be, the bound alone decides.
A program may use at most 192 MiB of HBM per device.

v0:
```python
import jax
import jax.numpy as jnp
from jax import lax
from jax.sharding import PartitionSpec as P

HD = 256
BLOCK = 512


epsilon = 1e-06
rope_base = 1000000.0
gelu_coeff = 0.7978845608028654
score_scale = 0.0625
masked_value = -1e30


def rms_norm(values, gain_vec):
    return (
        values * lax.rsqrt(jnp.mean(values * values, axis=-1, keepdims=True) + epsilon) * gain_vec
    )


def gelu_tanh(values):
    return (
        0.5 * values * (1.0 + jnp.tanh(gelu_coeff * (values + 0.044715 * values * values * values)))
    )


def rotate(values, cosine, sine_table):
    half_dim = values.shape[-1] // 2
    first_half = values[..., :half_dim]
    second_half = values[..., half_dim:]
    return jnp.concatenate(
        [
            first_half * cosine - second_half * sine_table,
            second_half * cosine + first_half * sine_table,
        ],
        axis=-1,
    )


def rope_tables(segment_row):
    row_count = segment_row.shape[0]
    earlier = jnp.sum((segment_row[None, :] < segment_row[:, None]).astype(jnp.int32), axis=1)
    position = jnp.arange(row_count, dtype=jnp.int32) - earlier
    exponent = jnp.arange(HD // 2, dtype=jnp.float32) * (2.0 / HD)
    frequency = rope_base ** (-exponent)
    angles = position.astype(jnp.float32)[:, None] * frequency[None, :]
    return (jnp.cos(angles), jnp.sin(angles))


def matmul(left, right):
    return jnp.dot(left, right, preferred_element_type=jnp.float32)


def left_dot(left, right):
    return lax.dot_general(
        left, right, (((0,), (0,)), ((), ())), preferred_element_type=jnp.float32
    )


def right_dot(left, right):
    return lax.dot_general(
        left, right, (((1,), (1,)), ((), ())), preferred_element_type=jnp.float32
    )


def per_device(
    hidden,
    segment_ids,
    w_query,
    w_key,
    w_value,
    w_out,
    w_gate,
    w_up,
    w_down,
    gain_in,
    gain_post_attn,
    gain_pre_ffn,
    gain_post_ffn,
    gain_query,
    gain_key,
    cotangent,
):
    row_total = hidden.shape[0]
    head_local = w_query.shape[1] // HD
    segment_row = segment_ids[0]
    cosine, sine_table = rope_tables(segment_row)
    hidden_full = hidden.astype(jnp.float32)
    normed_full, norm_in_back = jax.vjp(rms_norm, hidden_full, gain_in)
    normed_in = normed_full.astype(jnp.bfloat16)
    query_raw = matmul(normed_in, w_query)
    key_raw = matmul(normed_in, w_key)
    value_raw = matmul(normed_in, w_value)

    def query_path(raw_rows, gain_vec):
        shaped = raw_rows.reshape(row_total, head_local, HD)
        return rotate(rms_norm(shaped, gain_vec), cosine[:, None, :], sine_table[:, None, :])

    def key_path(raw_rows, gain_vec):
        return rotate(rms_norm(raw_rows, gain_vec), cosine, sine_table)

    query_rot, query_back = jax.vjp(query_path, query_raw, gain_query)
    key_rot, key_back = jax.vjp(key_path, key_raw, gain_key)
    queries = query_rot.astype(jnp.bfloat16)
    key_rows = key_rot.astype(jnp.bfloat16)
    value_rows = value_raw.astype(jnp.bfloat16)
    positions_all = jnp.arange(row_total, dtype=jnp.int32)
    block_count = row_total // BLOCK

    def block_scores(block_index):
        start = block_index * BLOCK
        stop = start + BLOCK
        raw_scores = (
            jnp.einsum(
                "rhd,kd->hrk",
                queries[start:stop],
                key_rows[:stop],
                preferred_element_type=jnp.float32,
            )
            * score_scale
        )
        allowed = (segment_row[start:stop, None] == segment_row[None, :stop]) & (
            positions_all[None, :stop] <= positions_all[start:stop, None]
        )
        return (jnp.where(allowed[None], raw_scores, masked_value), start, stop)

    context_blocks = []
    log_totals = []
    for block_index in range(block_count):
        scores, start, stop = block_scores(block_index)
        peak = jnp.max(scores, axis=-1, keepdims=True)
        expo_scores = jnp.exp(scores - peak)
        row_totals = jnp.sum(expo_scores, axis=-1, keepdims=True)
        probs = expo_scores / row_totals
        log_totals.append(peak + jnp.log(row_totals))
        context_blocks.append(
            jnp.einsum(
                "hrk,kd->rhd",
                probs.astype(jnp.bfloat16),
                value_rows[:stop],
                preferred_element_type=jnp.float32,
            )
        )
    context = (
        jnp.concatenate(context_blocks, axis=0)
        .reshape(row_total, head_local * HD)
        .astype(jnp.bfloat16)
    )
    attn = lax.psum(matmul(context, w_out), "mp")
    post_attn, post_attn_back = jax.vjp(rms_norm, attn, gain_post_attn)
    resid = hidden_full + post_attn
    mid_full, mid_back = jax.vjp(rms_norm, resid, gain_pre_ffn)
    normed_mid = mid_full.astype(jnp.bfloat16)
    gate = matmul(normed_mid, w_gate)
    up_proj = matmul(normed_mid, w_up)

    def gated(gate_vals, up_vals):
        return gelu_tanh(gate_vals) * up_vals

    act_full, gated_back = jax.vjp(gated, gate, up_proj)
    activated = act_full.astype(jnp.bfloat16)
    mlp_out = lax.psum(matmul(activated, w_down), "mp")
    post_ffn, post_ffn_back = jax.vjp(rms_norm, mlp_out, gain_post_ffn)
    output = (resid + post_ffn).astype(jnp.bfloat16)
    grad_out = cotangent.astype(jnp.float32)
    d_mlp, grad_gain_post_ffn = post_ffn_back(grad_out)
    d_mlp_low = d_mlp.astype(jnp.bfloat16)
    grad_w_down = left_dot(activated, d_mlp_low)
    d_act = right_dot(d_mlp_low, w_down)
    d_gate, d_up = gated_back(d_act)
    d_gate_low = d_gate.astype(jnp.bfloat16)
    d_up_low = d_up.astype(jnp.bfloat16)
    grad_w_gate = left_dot(normed_mid, d_gate_low)
    grad_w_up = left_dot(normed_mid, d_up_low)
    d_mid = lax.psum(right_dot(d_gate_low, w_gate) + right_dot(d_up_low, w_up), "mp")
    d_resid_norm, grad_gain_pre_ffn = mid_back(d_mid)
    d_resid = grad_out + d_resid_norm
    d_attn, grad_gain_post_attn = post_attn_back(d_resid)
    d_attn_low = d_attn.astype(jnp.bfloat16)
    grad_w_out = left_dot(context, d_attn_low)
    d_context = right_dot(d_attn_low, w_out).astype(jnp.bfloat16).reshape(row_total, head_local, HD)
    d_query_blocks = []
    d_keys = jnp.zeros((row_total, HD), jnp.float32)
    d_values = jnp.zeros((row_total, HD), jnp.float32)
    for block_index in range(block_count):
        scores, start, stop = block_scores(block_index)
        probs = jnp.exp(scores - log_totals[block_index])
        probs_low = probs.astype(jnp.bfloat16)
        grad_block = d_context[start:stop]
        d_probs = jnp.einsum(
            "rhd,kd->hrk", grad_block, value_rows[:stop], preferred_element_type=jnp.float32
        )
        row_inner = jnp.sum(probs * d_probs, axis=-1, keepdims=True)
        d_scores = (probs * (d_probs - row_inner)).astype(jnp.bfloat16)
        d_query_blocks.append(
            jnp.einsum("hrk,kd->rhd", d_scores, key_rows[:stop], preferred_element_type=jnp.float32)
            * score_scale
        )
        d_keys = d_keys.at[:stop].add(
            jnp.einsum(
                "hrk,rhd->kd", d_scores, queries[start:stop], preferred_element_type=jnp.float32
            )
            * score_scale
        )
        d_values = d_values.at[:stop].add(
            jnp.einsum("hrk,rhd->kd", probs_low, grad_block, preferred_element_type=jnp.float32)
        )
    d_queries = jnp.concatenate(d_query_blocks, axis=0)
    d_query_raw, grad_query_part = query_back(d_queries)
    d_query_low = d_query_raw.astype(jnp.bfloat16)
    grad_w_query = left_dot(normed_in, d_query_low)
    d_in_part = right_dot(d_query_low, w_query)
    key_value_part = jnp.concatenate([d_keys, d_values], axis=1)
    d_in_sum, key_value_sum, grad_gain_query = lax.psum(
        (d_in_part, key_value_part, grad_query_part), "mp"
    )
    d_keys_sum = key_value_sum[:, :HD]
    d_values_sum = key_value_sum[:, HD:]
    d_key_raw, grad_gain_key = key_back(d_keys_sum)
    d_key_low = d_key_raw.astype(jnp.bfloat16)
    d_value_low = d_values_sum.astype(jnp.bfloat16)
    grad_w_key = left_dot(normed_in, d_key_low)
    grad_w_value = left_dot(normed_in, d_value_low)
    d_in = d_in_sum + right_dot(d_key_low, w_key) + right_dot(d_value_low, w_value)
    d_hidden_norm, grad_gain_in = norm_in_back(d_in)
    grad_hidden = (d_resid + d_hidden_norm).astype(jnp.bfloat16)
    summed_parts = (
        lax.psum_scatter(grad_w_query, "dp", scatter_dimension=0, tiled=True),
        lax.psum_scatter(grad_w_key, "dp", scatter_dimension=0, tiled=True),
        lax.psum_scatter(grad_w_value, "dp", scatter_dimension=0, tiled=True),
        lax.psum_scatter(grad_w_out, "dp", scatter_dimension=1, tiled=True),
        lax.psum_scatter(grad_w_gate, "dp", scatter_dimension=0, tiled=True),
        lax.psum_scatter(grad_w_up, "dp", scatter_dimension=0, tiled=True),
        lax.psum_scatter(grad_w_down, "dp", scatter_dimension=1, tiled=True),
        lax.psum_scatter(grad_gain_in, "dp", scatter_dimension=0, tiled=True),
        lax.psum_scatter(grad_gain_post_attn, "dp", scatter_dimension=0, tiled=True),
        lax.psum_scatter(grad_gain_pre_ffn, "dp", scatter_dimension=0, tiled=True),
        lax.psum_scatter(grad_gain_post_ffn, "dp", scatter_dimension=0, tiled=True),
        lax.psum_scatter(grad_gain_query, "dp", scatter_dimension=0, tiled=True),
        lax.psum_scatter(grad_gain_key, "dp", scatter_dimension=0, tiled=True),
    )
    (
        grad_w_query,
        grad_w_key,
        grad_w_value,
        grad_w_out,
        grad_w_gate,
        grad_w_up,
        grad_w_down,
        grad_gain_in,
        grad_gain_post_attn,
        grad_gain_pre_ffn,
        grad_gain_post_ffn,
        grad_gain_query,
        grad_gain_key,
    ) = (
        lax.all_gather(summed_parts[0], "dp", axis=0, tiled=True),
        lax.all_gather(summed_parts[1], "dp", axis=0, tiled=True),
        lax.all_gather(summed_parts[2], "dp", axis=0, tiled=True),
        lax.all_gather(summed_parts[3], "dp", axis=1, tiled=True),
        lax.all_gather(summed_parts[4], "dp", axis=0, tiled=True),
        lax.all_gather(summed_parts[5], "dp", axis=0, tiled=True),
        lax.all_gather(summed_parts[6], "dp", axis=1, tiled=True),
        lax.all_gather(summed_parts[7], "dp", axis=0, tiled=True),
        lax.all_gather(summed_parts[8], "dp", axis=0, tiled=True),
        lax.all_gather(summed_parts[9], "dp", axis=0, tiled=True),
        lax.all_gather(summed_parts[10], "dp", axis=0, tiled=True),
        lax.all_gather(summed_parts[11], "dp", axis=0, tiled=True),
        lax.all_gather(summed_parts[12], "dp", axis=0, tiled=True),
    )
    return (
        output,
        grad_hidden,
        grad_w_query,
        grad_w_key,
        grad_w_value,
        grad_w_out,
        grad_w_gate,
        grad_w_up,
        grad_w_down,
        grad_gain_in,
        grad_gain_post_attn,
        grad_gain_pre_ffn,
        grad_gain_post_ffn,
        grad_gain_query,
        grad_gain_key,
    )


def solution(mesh):
    in_specs = (
        P("dp", None),
        P("dp", None),
        P(None, "mp"),
        P(),
        P(),
        P("mp", None),
        P(None, "mp"),
        P(None, "mp"),
        P("mp", None),
        P(),
        P(),
        P(),
        P(),
        P(),
        P(),
        P("dp", None),
    )
    out_specs = (
        P("dp", None),
        P("dp", None),
        P(None, "mp"),
        P(),
        P(),
        P("mp", None),
        P(None, "mp"),
        P(None, "mp"),
        P("mp", None),
        P(),
        P(),
        P(),
        P(),
        P(),
        P(),
    )
    return jax.shard_map(
        per_device, mesh=mesh, in_specs=in_specs, out_specs=out_specs, check_vma=False
    )
```

profile of v0, /device:TPU:0, one launch (start us, length us, event | category | flops | bytes accessed | tf_op | source)
XLA Modules:
  0.0 1817.3 jit_solution(17818812958873160346)
XLA Ops:
  28.9 96.6 %all-reduce.26.cloned.1.call-done = f32[1024,1152]{1,0:T(8,128)} async-done(((f32[1024,1152]{1,0:T(8,128)}), f32[1024,1152]{1,0:T(8,128)}) %all-reduce.26.cloned.1.call-update) | async-done | bytes 4718608 | tf_op jit(solution)/shard_map/psum | solution.py:151
  141.0 7.8 multiply_convert_fusion.1
  150.5 6.7 fusion.115
  157.4 94.3 %all-reduce.28.cloned.1.call-done = f32[1024,1152]{1,0:T(8,128)} async-done(((f32[1024,1152]{1,0:T(8,128)}), f32[1024,1152]{1,0:T(8,128)}) %all-reduce.28.cloned.1.call-update) | async-done | bytes 4718608 | tf_op jit(solution)/shard_map/psum | solution.py:164
  263.8 14.1 multiply_convert_fusion
  283.2 6.7 convolution_add_fusion.2
  291.3 93.0 %all-reduce.30.cloned.1.call-done = f32[1024,1152]{1,0:T(8,128)} async-done(((f32[1024,1152]{1,0:T(8,128)}), f32[1024,1152]{1,0:T(8,128)}) %all-reduce.30.cloned.1.call-update) | async-done | bytes 4718608 | tf_op jit(solution)/shard_map/psum | solution.py:177
  384.3 5.6 multiply_reduce_fusion
  390.1 5.5 multiply_reduce_fusion.1
  418.1 122.4 %all-reduce.32.cloned.1.call-done = (f32[1024,1152]{1,0:T(8,128)}, f32[1024,512]{0,1:T(8,128)}) async-done(((f32[1024,1152]{1,0:T(8,128)}, f32[1024,512]{0,1:T(8,128)}), (f32[1024,1152]{1,0:T(8,128)}, f32[1024,512]{0,1:T(8,128)})) %all-reduce.32.cloned.1.call-update) | async-done | bytes 6815760 | tf_op jit(solution)/shard_map/psum | solution.py:216
  551.2 10.5 fusion.120
  563.4 8.6 fusion.121
  573.7 8.6 fusion.122
  582.3 26.3 %reduce-scatter.8.cloned.1.call-done = f32[144,256]{1,0:T(8,128)} async-done(((f32[1152,256]{1,0:T(8,128)}), f32[144,256]{1,0:T(8,128)}) %reduce-scatter.8.cloned.1.call-update) | async-done | bytes 147472 | tf_op jit(solution)/shard_map/reduce_scatter | solution.py:230
  608.7 66.8 %reduce-scatter.14.cloned.1.call-done = f32[256,144]{0,1:T(8,128)} async-done(((f32[256,1152]{0,1:T(8,128)}), f32[256,144]{0,1:T(8,128)}) %reduce-scatter.14.cloned.1.call-update) | async-done | bytes 147472 | tf_op jit(solution)/shard_map/reduce_scatter | solution.py:233
  675.6 67.1 %reduce-scatter.10.cloned.1.call-done = f32[144,256]{1,0:T(8,128)} async-done(((f32[1152,256]{1,0:T(8,128)}), f32[144,256]{1,0:T(8,128)}) %reduce-scatter.10.cloned.1.call-update) | async-done | bytes 147472 | tf_op jit(solution)/shard_map/reduce_scatter | solution.py:231
  742.7 66.9 %reduce-scatter.12.cloned.1.call-done = f32[144,256]{1,0:T(8,128)} async-done(((f32[1152,256]{1,0:T(8,128)}), f32[144,256]{1,0:T(8,128)}) %reduce-scatter.12.cloned.1.call-update) | async-done | bytes 147472 | tf_op jit(solution)/shard_map/reduce_scatter | solution.py:232
  809.7 149.4 %reduce-scatter.16.cloned.1.call-done = f32[144,1728]{1,0:T(8,128)} async-done(((f32[1152,1728]{1,0:T(8,128)}), f32[144,1728]{1,0:T(8,128)}) %reduce-scatter.16.cloned.1.call-update) | async-done | bytes 995344 | tf_op jit(solution)/shard_map/reduce_scatter | solution.py:234
  959.2 149.3 %reduce-scatter.18.cloned.1.call-done = f32[144,1728]{1,0:T(8,128)} async-done(((f32[1152,1728]{1,0:T(8,128)}), f32[144,1728]{1,0:T(8,128)}) %reduce-scatter.18.cloned.1.call-update) | async-done | bytes 995344 | tf_op jit(solution)/shard_map/reduce_scatter | solution.py:235
  1108.8 149.2 %reduce-scatter.20.cloned.1.call-done = f32[1728,144]{0,1:T(8,128)} async-done(((f32[1728,1152]{0,1:T(8,128)}), f32[1728,144]{0,1:T(8,128)}) %reduce-scatter.20.cloned.1.call-update) | async-done | bytes 995344 | tf_op jit(solution)/shard_map/reduce_scatter | solution.py:236
  1268.6 35.7 %all-reduce.19 = (f32[1152]{0:T(1024)S(1)}, f32[1152]{0:T(1024)S(1)}, f32[1152]{0:T(1024)S(1)}, f32[1152]{0:T(1024)S(1)}, f32[256]{0:T(256)S(1)}, /*index=5*/f32[256]{0:T(256)S(1)}) all-reduce(f32[1152]{0:T(1024)S(1)} %get-tuple-element.130, f32[1152]{0:T(1024)S(1)} %get-tuple-element.126, ...), channel_id=9, replica_groups=mesh['dp'=8,'mp'=4] {'dp'}, use_global_device_ids=true, to_apply=%region_32.33.clone | all-reduce | flops 5120 | bytes 40960
  1304.4 5.6 psum.48
  1311.1 34.2 %all-reduce.18 = (f32[1152]{0:T(1024)}, f32[1152]{0:T(1024)}, f32[1152]{0:T(1024)}, f32[1152]{0:T(1024)}, f32[256]{0:T(256)}, /*index=5*/f32[256]{0:T(256)}) all-reduce(f32[1152]{0:T(1024)S(1)} %dynamic-slice_dynamic-update-slice_fusion.3, f32[1152]{0:T(1024)S(1)} %dynamic-slice_dynamic-update-slice_fusion.2, ...), channel_id=1, replica_groups=mesh['dp'=8,'mp'=4] {'dp'}, use_global_device_ids=true, to_apply=%add.6 | all-reduce | flops 5120 | bytes 40960
  1345.3 5.5 fusion.17
  1353.5 31.8 %all-gather.10.cloned.1.call-done = f32[1152,256]{1,0:T(8,128)} async-done(((f32[144,256]{1,0:T(8,128)}), f32[1152,256]{1,0:T(8,128)}) %all-gather.10.cloned.1.call-update) | async-done | bytes 1179664 | tf_op jit(solution)/shard_map/all_gather | solution.py:260
  1385.3 41.9 %all-gather.12.cloned.1.call-done = f32[1152,256]{1,0:T(8,128)} async-done(((f32[144,256]{1,0:T(8,128)}), f32[1152,256]{1,0:T(8,128)}) %all-gather.12.cloned.1.call-update) | async-done | bytes 1179664 | tf_op jit(solution)/shard_map/all_gather | solution.py:261
  1427.2 124.1 %all-gather.16.cloned.1.call-done = f32[1152,1728]{1,0:T(8,128)} async-done(((f32[144,1728]{1,0:T(8,128)}), f32[1152,1728]{1,0:T(8,128)}) %all-gather.16.cloned.1.call-update) | async-done | bytes 7962640 | tf_op jit(solution)/shard_map/all_gather | solution.py:263
  1551.2 8.8 copy.40
  1560.1 114.7 %all-gather.18.cloned.1.call-done = f32[1152,1728]{1,0:T(8,128)} async-done(((f32[144,1728]{1,0:T(8,128)}), f32[1152,1728]{1,0:T(8,128)}) %all-gather.18.cloned.1.call-update) | async-done | bytes 7962640 | tf_op jit(solution)/shard_map/all_gather | solution.py:264
  1674.7 8.8 copy.41
  1683.5 114.7 %all-gather.20.cloned.1.call-done = f32[1728,1152]{0,1:T(8,128)} async-done(((f32[1728,144]{0,1:T(8,128)}), f32[1728,1152]{0,1:T(8,128)}) %all-gather.20.cloned.1.call-update) | async-done | bytes 7962640 | tf_op jit(solution)/shard_map/all_gather | solution.py:265
  1798.2 8.8 copy.42
  (285 shorter events, 109.0 us)
Async XLA Ops:
  7.2 118.3 %all-reduce.26.cloned.1.call-start = ((), (), s32[]{:S(2)}) async-start(), calls=%async_computation.7 | async-start | bytes 9437184 | tf_op jit(solution)/shard_map/psum | solution.py:151
  7.3 11.3 copy-start.59
  13.4 10.3 copy-start.36
  18.4 382.9 %copy-start.27 = (bf16[1024,1,128]{0,2,1:T(8,128)(2,1)}, bf16[1024,1,128]{0,2,1:T(8,128)(2,1)S(1)}, u32[]{:S(2)}) copy-start(bf16[1024,1,128]{0,2,1:T(8,128)(2,1)S(1)} %get-tuple-element.161) | copy-start | bytes 786436
  18.4 382.9 %copy-start.29 = (bf16[1024,1,128]{0,2,1:T(8,128)(2,1)}, bf16[1024,1,128]{0,2,1:T(8,128)(2,1)S(1)}, u32[]{:S(2)}) copy-start(bf16[1024,1,128]{0,2,1:T(8,128)(2,1)S(1)} %get-tuple-element.162) | copy-start | bytes 786436
  28.6 99.8 %copy-start.47 = (f32[1152]{0:T(1024)S(1)}, f32[1152]{0:T(1024)}, u32[]{:S(2)}) copy-start(f32[1152]{0:T(1024)} %param.38) | copy-start | bytes 13828
  28.7 223.0 %all-reduce.28.cloned.1.call-start = ((), (), s32[]{:S(2)}) async-start(), calls=%async_computation.8 | async-start | bytes 9437184 | tf_op jit(solution)/shard_map/psum | solution.py:164
  157.3 97.3 %copy-start.54 = (f32[1152]{0:T(1024)S(1)}, f32[1152]{0:T(1024)}, u32[]{:S(2)}) copy-start(f32[1152]{0:T(1024)} %param.40) | copy-start | bytes 13828
  157.3 226.9 %all-reduce.30.cloned.1.call-start = ((), (), s32[]{:S(2)}) async-start(), calls=%async_computation.9 | async-start | bytes 9437184 | tf_op jit(solution)/shard_map/psum | solution.py:177
  263.8 14.1 copy-start.22
  263.8 14.1 copy-start.72
  289.9 250.6 %all-reduce.32.cloned.1.call-start = ((), (), s32[]{:S(2)}) async-start(), calls=%async_computation.24 | async-start | bytes 13631488 | tf_op jit(solution)/shard_map/psum | solution.py:216
  384.3 11.3 slice-start
  412.0 196.7 %reduce-scatter.8.cloned.1.call-start = ((), (), s32[]{:S(2)}) async-start(), calls=%async_computation.10 | async-start | bytes 1327104 | tf_op jit(solution)/shard_map/reduce_scatter | solution.py:230
  413.9 130.5 %copy-start.58 = (f32[256]{0:T(256)S(1)}, f32[256]{0:T(256)}, u32[]{:S(2)}) copy-start(f32[256]{0:T(256)} %param.42) | copy-start | bytes 3076
  413.9 261.6 %reduce-scatter.14.cloned.1.call-start = ((), (), s32[]{:S(2)}) async-start(), calls=%async_computation.16 | async-start | bytes 1327104 | tf_op jit(solution)/shard_map/reduce_scatter | solution.py:233
  417.9 324.8 %reduce-scatter.10.cloned.1.call-start = ((), (), s32[]{:S(2)}) async-start(), calls=%async_computation.12 | async-start | bytes 1327104 | tf_op jit(solution)/shard_map/reduce_scatter | solution.py:231
  548.1 261.6 %reduce-scatter.12.cloned.1.call-start = ((), (), s32[]{:S(2)}) async-start(), calls=%async_computation.14 | async-start | bytes 1327104 | tf_op jit(solution)/shard_map/reduce_scatter | solution.py:232
  551.2 408.0 %reduce-scatter.16.cloned.1.call-start = ((), (), s32[]{:S(2)}) async-start(), calls=%async_computation.18 | async-start | bytes 9289728 | tf_op jit(solution)/shard_map/reduce_scatter | solution.py:234
  561.8 546.7 %reduce-scatter.18.cloned.1.call-start = ((), (), s32[]{:S(2)}) async-start(), calls=%async_computation.20 | async-start | bytes 9289728 | tf_op jit(solution)/shard_map/reduce_scatter | solution.py:235
  572.0 686.0 %reduce-scatter.20.cloned.1.call-start = ((), (), s32[]{:S(2)}) async-start(), calls=%async_computation.22 | async-start | bytes 9289728 | tf_op jit(solution)/shard_map/reduce_scatter | solution.py:236
  582.3 675.8 %copy-start.68 = (u32[32]{0:T(128)S(1)}, u32[32]{0:T(128)}, u32[]{:S(2)}) copy-start(u32[32]{0:T(128)} %constant.180) | copy-start | bytes 388
  582.3 768.5 %all-gather.8.cloned.1.call-start = ((), (), s32[]{:S(2)}) async-start(), calls=%async_computation.11 | async-start | bytes 1327104 | tf_op jit(solution)/shard_map/all_gather | solution.py:259
  608.7 742.2 %all-gather.14.cloned.1.call-start = ((), (), s32[]{:S(2)}) async-start(), calls=%async_computation.17 | async-start | bytes 1327104 | tf_op jit(solution)/shard_map/all_gather | solution.py:262
  675.5 709.8 %all-gather.10.cloned.1.call-start = ((), (), s32[]{:S(2)}) async-start(), calls=%async_computation.13 | async-start | bytes 1327104 | tf_op jit(solution)/shard_map/all_gather | solution.py:260
  742.7 684.5 %all-gather.12.cloned.1.call-start = ((), (), s32[]{:S(2)}) async-start(), calls=%async_computation.15 | async-start | bytes 1327104 | tf_op jit(solution)/shard_map/all_gather | solution.py:261
  809.7 741.6 %all-gather.16.cloned.1.call-start = ((), (), s32[]{:S(2)}) async-start(), calls=%async_computation.19 | async-start | bytes 9289728 | tf_op jit(solution)/shard_map/all_gather | solution.py:263
  959.2 715.5 %all-gather.18.cloned.1.call-start = ((), (), s32[]{:S(2)}) async-start(), calls=%async_computation.21 | async-start | bytes 9289728 | tf_op jit(solution)/shard_map/all_gather | solution.py:264
  1108.5 689.7 %all-gather.20.cloned.1.call-start = ((), (), s32[]{:S(2)}) async-start(), calls=%async_computation.23 | async-start | bytes 9289728 | tf_op jit(solution)/shard_map/all_gather | solution.py:265
  1265.1 80.2 %copy-start.52 = (f32[1024]{0:T(1024)S(1)}, f32[1024]{0:T(1024)}, u32[]{:S(2)}) copy-start(f32[1024]{0:T(1024)} %copy-done.51) | copy-start | bytes 12292
  1683.5 123.4 %copy-start.33 = (f32[1152,256]{1,0:T(8,128)S(1)}, f32[1152,256]{1,0:T(8,128)}, u32[]{:S(2)}) copy-start(f32[1152,256]{1,0:T(8,128)} %all-gather.8.cloned.1.call-done) | copy-start | bytes 3538948
  1683.5 124.5 %copy-start.34 = (f32[1152,256]{1,0:T(8,128)S(1)}, f32[1152,256]{1,0:T(8,128)}, u32[]{:S(2)}) copy-start(f32[1152,256]{1,0:T(8,128)} %all-gather.10.cloned.1.call-done) | copy-start | bytes 3538948
  (64 other events, 209.7 us)
Sparse Core Ops, SparseCore 0:
  28.8 96.7 all-reduce.25
  157.4 94.1 all-reduce.27
  290.0 94.1 all-reduce.29
  412.1 128.4 all-reduce.31
  544.4 64.2 reduce-scatter.7
  612.4 63.0 reduce-scatter.13
  679.5 63.1 reduce-scatter.9
  746.6 63.0 reduce-scatter.11
  813.3 145.7 reduce-scatter.15
  962.7 145.7 reduce-scatter.17
  1112.2 145.7 reduce-scatter.19
  1260.0 40.4 all-gather.7
  1302.7 40.5 all-gather.13
  1345.4 39.8 all-gather.9
  1387.3 39.8 all-gather.11
  1429.2 121.9 all-gather.15
  1553.3 121.3 all-gather.17
  1676.8 121.3 all-gather.19
where the time goes:
time: 1830 us; the launch traced here: 1820 us
  waiting for transfers between devices  1510 us (83%)
  matrix products  106 us (6%)
  blocking collectives  75.6 us (4%)
  other arithmetic  57.5 us (3%)
  local copies, waits for them, and re-layouts  49.8 us (3%)
  between operations  18.4 us (1%)
    reduce_scatter x1, waiting for transfers between devices, per_device(): lax.psum_scatter(grad_w_gate, 'dp', scatter_dimension=0, tiled=True)  149 us
    reduce_scatter x1, waiting for transfers between devices, per_device(): lax.psum_scatter(grad_w_up, 'dp', scatter_dimension=0, tiled=True)  149 us
    reduce_scatter x1, waiting for transfers between devices, per_device(): lax.psum_scatter(grad_w_down, 'dp', scatter_dimension=1, tiled=True)  149 us
    all_gather x1, waiting for transfers between devices, per_device(): lax.all_gather(summed_parts[4], 'dp', axis=0, tiled=True)  124 us
    psum x1, waiting for transfers between devices, per_device(): lax.psum((d_in_part, key_value_part, grad_query_part), 'mp')  122 us
    all_gather x1, waiting for transfers between devices, per_device(): lax.all_gather(summed_parts[6], 'dp', axis=1, tiled=True)  115 us
    all_gather x1, waiting for transfers between devices, per_device(): lax.all_gather(summed_parts[5], 'dp', axis=0, tiled=True)  115 us
    psum x1, waiting for transfers between devices, per_device(): attn = lax.psum(matmul(context, w_out), 'mp')  96.6 us
  transfers between devices with their start and end apart: 18, of which 16 were waited for; matrix products, arithmetic and copies ran while one was open for 4% of the time, Pallas kernels for 0%

commit v1 on v0

v1 whole, which is shorter than its diff:
```python
import functools

import jax
import jax.numpy as jnp
from jax import lax
from jax.experimental import pallas as pl
from jax.experimental.pallas import tpu as pltpu
from jax.sharding import PartitionSpec as P

HD = 256
BLOCK = 512
LINE = 4
PAIR = 2

epsilon = 1e-06
rope_base = 1000000.0
gelu_coeff = 0.7978845608028654
score_scale = 0.0625
masked_value = -1e30

MESH = pl.DeviceIdType.MESH
DMA = pltpu.SemaphoreType.DMA


def send_to(src, dst, sent, arrived, dp, mp):
    return pltpu.make_async_remote_copy(
        src_ref=src, dst_ref=dst, send_sem=sent, recv_sem=arrived, device_id=(dp, mp), device_id_type=MESH
    )


def wait_bytes(ref, sem):
    pltpu.make_async_copy(ref, ref, sem).wait()


def span(start, k, r):
    return pl.ds(pl.multiple_of(start + k * r, r), r)


class Place:
    def __init__(self):
        dp, mp = lax.axis_index("dp"), lax.axis_index("mp")
        self.dp, self.mp = dp, mp
        self.y = lax.rem(dp, 2)
        z = lax.rem(dp // 2, LINE)
        self.core = lax.rem(mp, 2)
        self.pair = dp + 1 - 2 * self.y
        self.mid = (z == 1) | (z == 2)
        self.end = (z == 0) | (z == LINE - 1)
        self.chain = jnp.where((z == 0) | (z == 2), dp + 2, dp - 2)
        self.across = jnp.where(z == 1, dp + 2, dp - 2)
        self.sibling = mp + 1 - 2 * self.core
        self.far = lax.rem(mp + 2, 4)


def greet(peers):
    barrier = pltpu.get_barrier_semaphore()
    for cond, dp, mp in peers:

        def signal(dp=dp, mp=mp):
            pl.semaphore_signal(barrier, inc=1, device_id=(dp, mp), device_id_type=MESH)

        signal() if cond is None else pl.when(cond)(signal)
    pl.semaphore_wait(barrier, sum(1 if cond is None else cond.astype(jnp.int32) for cond, _, _ in peers))


def within(k, n, body):
    pl.when((k >= 0) & (k < n))(lambda: body(k))


class LineSum:
    lag_mid, lag_end = 2, 5

    @staticmethod
    def scratch(h, c, r, presum):
        n = h // r
        sems = [DMA((n,)), DMA((n,)), DMA, DMA, DMA, DMA, DMA]
        pre = [pltpu.VMEM((h, c), jnp.float32), DMA((n,)), DMA] if presum else []
        return [pltpu.VMEM((h, c), jnp.float32)] * 2 + sems + pre

    def __init__(self, at, own, out, r, presum, refs):
        self.at, self.own, self.out, self.r, self.presum = at, own, out, r, presum
        self.r1, self.r2, self.r1s, self.r2s, self.s1, self.s2, self.ys, self.yr, self.ls = refs[:9]
        if presum:
            self.r0, self.r0s, self.s0 = refs[9:]
        self.h = out.shape[1]
        self.n = self.h // r
        self.steps = self.n + self.lag_end
        self.base = at.y * self.h if presum else 0

    def rows(self, k):
        return span(0, k, self.r)

    def start(self):
        at = self.at
        if self.presum:
            theirs = (1 - at.y) * self.h

            def give(k, _):
                src = self.own.at[span(theirs, k, self.r)]
                send_to(src, self.r0.at[self.rows(k)], self.s0, self.r0s.at[k], at.pair, at.mp).start()
                return 0

            lax.fori_loop(0, self.n, give, 0)
        else:

            @pl.when(at.end)
            def _():
                def give(k, _):
                    q = self.rows(k)
                    send_to(self.own.at[q], self.r1.at[q], self.s1, self.r1s.at[k], at.chain, at.mp).start()
                    return 0

                lax.fori_loop(0, self.n, give, 0)

    def local(self, k):
        if not self.presum:
            return self.own[self.rows(k), :]
        q = self.rows(k)
        send_to(self.r0.at[q], self.r0.at[q], self.s0, self.r0s.at[k], self.at.pair, self.at.mp).wait_recv()
        return self.own[span(self.base, k, self.r), :] + self.r0[q, :]

    def give_total(self, k):
        at, q = self.at, self.rows(k)
        send_to(self.r2.at[q], self.out.at[at.y, q], self.ys, self.yr, at.pair, at.mp).start()
        pltpu.make_async_copy(self.r2.at[q], self.out.at[at.y, q], self.ls).start()

    def first(self, k):
        at, q = self.at, self.rows(k)
        local = self.local(k)
        send_to(self.r1.at[q], self.r1.at[q], self.s1, self.r1s.at[k], at.chain, at.mp).wait_recv()
        self.r1[q, :] = self.r1[q, :] + local
        send_to(self.r1.at[q], self.r2.at[q], self.s1, self.r2s.at[k], at.across, at.mp).start()

    def second(self, k):
        at, q = self.at, self.rows(k)
        send_to(self.r2.at[q], self.r2.at[q], self.s2, self.r2s.at[k], at.across, at.mp).wait_recv()
        self.r2[q, :] = self.r2[q, :] + self.r1[q, :]
        send_to(self.r2.at[q], self.r2.at[q], self.s2, self.r2s.at[k], at.chain, at.mp).start()
        self.give_total(k)

    def outer(self, k):
        at, q = self.at, self.rows(k)
        self.r0[q, :] = self.local(k)
        send_to(self.r0.at[q], self.r1.at[q], self.s1, self.r1s.at[k], at.chain, at.mp).start()

    def last(self, k):
        at, q = self.at, self.rows(k)
        send_to(self.r2.at[q], self.r2.at[q], self.s2, self.r2s.at[k], at.chain, at.mp).wait_recv()
        self.give_total(k)

    def step(self, k):
        @pl.when(self.at.mid)
        def _():
            within(k, self.n, self.first)
            within(k - self.lag_mid, self.n, self.second)

        @pl.when(self.at.end)
        def _():
            if self.presum:
                within(k, self.n, self.outer)
            within(k - self.lag_end, self.n, self.last)

    def finish(self):
        at = self.at
        wait_bytes(self.r1, self.s1)

        @pl.when(at.mid)
        def _():
            wait_bytes(self.r2, self.s2)

        if self.presum:
            wait_bytes(self.r0, self.s0)
        whole = send_to(self.r2, self.out.at[1 - at.y], self.ys, self.yr, at.pair, at.mp)
        whole.wait_send()
        whole.wait_recv()
        wait_bytes(self.r2, self.ls)


class MpSum:
    lag, lag_pair = 2, 4

    @staticmethod
    def scratch(rows, c, r, derive=False):
        n = rows // 2 // r
        half = pltpu.VMEM((rows // 2, c), jnp.float32)
        more = [half, DMA((n,)), DMA, DMA, DMA, DMA, DMA, DMA] if derive else []
        return [half, half, DMA((n,)), DMA((n,)), DMA, DMA, DMA, DMA, DMA] + more

    def __init__(self, at, p, out, r, refs, derive=None, der=None):
        self.at, self.p, self.out, self.r = at, p, out, r
        self.a, self.b, self.as_, self.bs, self.s1, self.s2, self.os, self.or_, self.ls = refs[:9]
        self.derive, self.der = derive, der
        if derive is not None:
            self.e, self.ps, self.es, self.er, self.el, self.ys, self.fs, self.fr = refs[9:]
        self.h = p.shape[0] // 2
        self.n = self.h // r
        self.mine, self.theirs = at.core * self.h, (1 - at.core) * self.h
        self.steps = self.n + self.lag + (self.lag_pair if derive is not None else 0)

    def start(self):
        at = self.at

        def give(k, _):
            src = self.p.at[span(self.theirs, k, self.r)]
            send_to(src, self.a.at[span(0, k, self.r)], self.s1, self.as_.at[k], at.dp, at.sibling).start()
            return 0

        lax.fori_loop(0, self.n, give, 0)

    def first(self, k):
        at, q = self.at, span(0, k, self.r)
        send_to(self.a.at[q], self.a.at[q], self.s1, self.as_.at[k], at.dp, at.sibling).wait_recv()
        self.a[q, :] = self.a[q, :] + self.p[span(self.mine, k, self.r), :]
        send_to(self.a.at[q], self.b.at[q], self.s2, self.bs.at[k], at.dp, at.far).start()

    def second(self, k):
        at, q, o = self.at, span(0, k, self.r), span(self.mine, k, self.r)
        send_to(self.b.at[q], self.b.at[q], self.s2, self.bs.at[k], at.dp, at.far).wait_recv()
        total = self.b[q, :] + self.a[q, :]
        self.b[q, :] = total
        send_to(self.b.at[q], self.out.at[o], self.os, self.or_, at.dp, at.sibling).start()
        pltpu.make_async_copy(self.b.at[q], self.out.at[o], self.ls).start()
        if self.derive is not None:
            self.e[q, :] = self.derive(total, o)
            send_to(self.e.at[q], self.der.at[1, o], self.ys, self.ps.at[k], at.pair, at.mp).start()
            send_to(self.e.at[q], self.der.at[0, o], self.es, self.er, at.dp, at.sibling).start()
            pltpu.make_async_copy(self.e.at[q], self.der.at[0, o], self.el).start()

    def third(self, k):
        at, o = self.at, span(self.mine, k, self.r)
        send_to(self.e.at[span(0, k, self.r)], self.der.at[1, o], self.ys, self.ps.at[k], at.pair, at.mp).wait_recv()
        send_to(self.der.at[1, o], self.der.at[1, o], self.fs, self.fr, at.dp, at.sibling).start()

    def step(self, k):
        within(k, self.n, self.first)
        within(k - self.lag, self.n, self.second)
        if self.derive is not None:
            within(k - self.lag - self.lag_pair, self.n, self.third)

    def finish(self):
        wait_bytes(self.a, self.s1)
        wait_bytes(self.a, self.s2)
        wait_bytes(self.b, self.os)
        wait_bytes(self.b, self.or_)
        wait_bytes(self.b, self.ls)
        if self.derive is not None:
            for sem in (self.es, self.er, self.el, self.ys, self.fs, self.fr):
                wait_bytes(self.e, sem)


def run_engines(engines):
    for engine, _ in engines:
        engine.start()
    steps = max(engine.steps + offset for engine, offset in engines)

    def body(t, _):
        for engine, offset in engines:
            engine.step(t - offset)
        return 0

    lax.fori_loop(0, steps, body, 0)
    for engine, _ in engines:
        engine.finish()


def vmem_spec():
    return pl.BlockSpec(memory_space=pltpu.VMEM)


def any_spec():
    return pl.BlockSpec(memory_space=pl.ANY)


def comm_params(collective_id, mib):
    return pltpu.CompilerParams(collective_id=collective_id, has_side_effects=True, vmem_limit_bytes=mib * 2**20)


def sums_kernel(lines, sums, *refs):
    at = Place()
    refs = list(refs)

    def take(count):
        got, refs[:count] = refs[:count], []
        return got

    own = take(len(lines))
    parts = take(len(sums))
    outs = take(len(lines))
    totals = take(len(sums))
    peers = []
    if lines:
        peers += [(None, at.pair, at.mp), (None, at.chain, at.mp), (at.mid, at.across, at.mp)]
    if sums:
        peers += [(None, at.dp, at.sibling), (None, at.dp, at.far)]
    greet(peers)
    engines = []
    offset = 0
    for p, total, r in zip(parts, totals, sums):
        engines.append((MpSum(at, p, total, r, take(9)), offset))
        offset += p.shape[0] // 2 // r
    offset = 0
    for x, out, (r, presum) in zip(own, outs, lines):
        engines.append((LineSum(at, x, out, r, presum, take(12 if presum else 9)), offset))
        offset += out.shape[1] // r
    run_engines(engines)


def sums_call(collective_id, mib, line_parts, mp_parts):
    lines = tuple((r, presum) for _, r, presum in line_parts)
    sums = tuple(r for _, r in mp_parts)
    outs, scratch = [], []
    for x, r, presum in line_parts:
        h = x.shape[0] // 2 if presum else x.shape[0]
        outs.append(jax.ShapeDtypeStruct((2, h, x.shape[1]), jnp.float32))
    for p, r in mp_parts:
        outs.append(jax.ShapeDtypeStruct(p.shape, jnp.float32))
        scratch += MpSum.scratch(*p.shape, r)
    for x, r, presum in line_parts:
        scratch += LineSum.scratch(x.shape[0] // 2 if presum else x.shape[0], x.shape[1], r, presum)
    args = [x for x, _, _ in line_parts] + [p for p, _ in mp_parts]
    return pl.pallas_call(
        functools.partial(sums_kernel, lines, sums),
        out_shape=outs,
        in_specs=[vmem_spec()] * len(args),
        out_specs=[any_spec()] * len(outs),
        scratch_shapes=scratch,
        compiler_params=comm_params(collective_id, mib),
        name="sums_%d" % collective_id,
    )(*args)


def attn_derive(hidden, gain_post, gain_pre):
    def derive(total, rows):
        scale = lax.rsqrt(jnp.mean(total * total, axis=-1, keepdims=True) + epsilon)
        resid = hidden[rows, :].astype(jnp.float32) + total * scale * gain_post[...]
        return resid * lax.rsqrt(jnp.mean(resid * resid, axis=-1, keepdims=True) + epsilon) * gain_pre[...]

    return derive


def mlp_derive(cotangent, gain):
    def derive(total, rows):
        scale = lax.rsqrt(jnp.mean(total * total, axis=-1, keepdims=True) + epsilon)
        ge = cotangent[rows, :].astype(jnp.float32) * gain[...]
        return scale * ge - total * (scale * scale * scale) * jnp.mean(ge * total, axis=-1, keepdims=True)

    return derive


def derive_kernel(make, n_aux, r, p, *refs):
    aux, (total, der), scratch = refs[:n_aux], refs[n_aux : n_aux + 2], refs[n_aux + 2 :]
    at = Place()
    greet([(None, at.dp, at.sibling), (None, at.dp, at.far), (None, at.pair, at.mp)])
    run_engines([(MpSum(at, p, total, r, scratch, make(*aux), der), 0)])


def derive_call(collective_id, make, p, r, aux):
    return pl.pallas_call(
        functools.partial(derive_kernel, make, len(aux), r),
        out_shape=[jax.ShapeDtypeStruct(p.shape, jnp.float32), jax.ShapeDtypeStruct((2,) + p.shape, jnp.float32)],
        in_specs=[vmem_spec()] * (1 + len(aux)),
        out_specs=[any_spec()] * 2,
        scratch_shapes=MpSum.scratch(*p.shape, r, True),
        compiler_params=comm_params(collective_id, 40),
        name="derive_%d" % collective_id,
    )(p, *aux)


def rms_norm(values, gain_vec):
    return values * lax.rsqrt(jnp.mean(values * values, axis=-1, keepdims=True) + epsilon) * gain_vec


def gelu_tanh(values):
    return 0.5 * values * (1.0 + jnp.tanh(gelu_coeff * (values + 0.044715 * values * values * values)))


def rotate(values, cosine, sine_table):
    half_dim = values.shape[-1] // 2
    first_half = values[..., :half_dim]
    second_half = values[..., half_dim:]
    return jnp.concatenate(
        [first_half * cosine - second_half * sine_table, second_half * cosine + first_half * sine_table], axis=-1
    )


def rope_tables(segment_row):
    row_count = segment_row.shape[0]
    earlier = jnp.sum((segment_row[None, :] < segment_row[:, None]).astype(jnp.int32), axis=1)
    position = jnp.arange(row_count, dtype=jnp.int32) - earlier
    exponent = jnp.arange(HD // 2, dtype=jnp.float32) * (2.0 / HD)
    frequency = rope_base ** (-exponent)
    angles = position.astype(jnp.float32)[:, None] * frequency[None, :]
    return (jnp.cos(angles), jnp.sin(angles))


def matmul(left, right):
    return jnp.dot(left, right, preferred_element_type=jnp.float32)


def left_dot(left, right):
    return lax.dot_general(left, right, (((0,), (0,)), ((), ())), preferred_element_type=jnp.float32)


def right_dot(left, right):
    return lax.dot_general(left, right, (((1,), (1,)), ((), ())), preferred_element_type=jnp.float32)


def per_device(
    rest_groups,
    hidden,
    segment_ids,
    w_query,
    w_key,
    w_value,
    w_out,
    w_gate,
    w_up,
    w_down,
    gain_in,
    gain_post_attn,
    gain_pre_ffn,
    gain_post_ffn,
    gain_query,
    gain_key,
    cotangent,
):
    row_total, width = hidden.shape
    head_local = w_query.shape[1] // HD
    y = lax.rem(lax.axis_index("dp"), 2)
    segment_row = segment_ids[0]
    cosine, sine_table = rope_tables(segment_row)
    hidden_full = hidden.astype(jnp.float32)
    normed_full, norm_in_back = jax.vjp(rms_norm, hidden_full, gain_in)
    normed_in = normed_full.astype(jnp.bfloat16)
    query_raw = matmul(normed_in, w_query)
    key_raw = matmul(normed_in, w_key)
    value_raw = matmul(normed_in, w_value)

    def query_path(raw_rows, gain_vec):
        shaped = raw_rows.reshape(row_total, head_local, HD)
        return rotate(rms_norm(shaped, gain_vec), cosine[:, None, :], sine_table[:, None, :])

    def key_path(raw_rows, gain_vec):
        return rotate(rms_norm(raw_rows, gain_vec), cosine, sine_table)

    query_rot, query_back = jax.vjp(query_path, query_raw, gain_query)
    key_rot, key_back = jax.vjp(key_path, key_raw, gain_key)
    queries = query_rot.astype(jnp.bfloat16)
    key_rows = key_rot.astype(jnp.bfloat16)
    value_rows = value_raw.astype(jnp.bfloat16)
    positions_all = jnp.arange(row_total, dtype=jnp.int32)
    block_count = row_total // BLOCK

    def block_scores(block_index):
        start = block_index * BLOCK
        stop = start + BLOCK
        raw_scores = (
            jnp.einsum("rhd,kd->hrk", queries[start:stop], key_rows[:stop], preferred_element_type=jnp.float32)
            * score_scale
        )
        allowed = (segment_row[start:stop, None] == segment_row[None, :stop]) & (
            positions_all[None, :stop] <= positions_all[start:stop, None]
        )
        return (jnp.where(allowed[None], raw_scores, masked_value), start, stop)

    context_blocks = []
    log_totals = []
    for block_index in range(block_count):
        scores, start, stop = block_scores(block_index)
        peak = jnp.max(scores, axis=-1, keepdims=True)
        expo_scores = jnp.exp(scores - peak)
        row_totals = jnp.sum(expo_scores, axis=-1, keepdims=True)
        probs = expo_scores / row_totals
        log_totals.append(peak + jnp.log(row_totals))
        context_blocks.append(
            jnp.einsum(
                "hrk,kd->rhd", probs.astype(jnp.bfloat16), value_rows[:stop], preferred_element_type=jnp.float32
            )
        )
    context = jnp.concatenate(context_blocks, axis=0).reshape(row_total, head_local * HD).astype(jnp.bfloat16)
    attn, mid_all = derive_call(
        1, attn_derive, matmul(context, w_out), 32, (hidden, gain_post_attn[None], gain_pre_ffn[None])
    )
    post_attn, post_attn_back = jax.vjp(rms_norm, attn, gain_post_attn)
    resid = hidden_full + post_attn
    mid_full, mid_back = jax.vjp(rms_norm, resid, gain_pre_ffn)
    mid_all = mid_all.reshape(2 * row_total, width).astype(jnp.bfloat16)
    gate = matmul(mid_all, w_gate)
    up_proj = matmul(mid_all, w_up)

    def gated(gate_vals, up_vals):
        return gelu_tanh(gate_vals) * up_vals

    act_full, gated_back = jax.vjp(gated, gate, up_proj)
    activated = act_full.astype(jnp.bfloat16)
    mlp_out, d_mlp_all = derive_call(
        2, mlp_derive, matmul(activated[:row_total], w_down), 32, (cotangent, gain_post_ffn[None])
    )
    grad_out = cotangent.astype(jnp.float32)
    post_ffn, post_ffn_back = jax.vjp(rms_norm, mlp_out, gain_post_ffn)
    output = (resid + post_ffn).astype(jnp.bfloat16)
    _, grad_gain_post_ffn = post_ffn_back(grad_out)
    d_mlp_all = d_mlp_all.reshape(2 * row_total, width).astype(jnp.bfloat16)
    units = w_down.shape[0]
    act_half = lax.dynamic_slice(activated, (0, y * (units // 2)), (2 * row_total, units // 2))
    part_down = left_dot(act_half, d_mlp_all)
    d_act = right_dot(d_mlp_all, w_down)
    d_gate, d_up = gated_back(d_act)
    d_gate_low = d_gate.astype(jnp.bfloat16)
    d_up_low = d_up.astype(jnp.bfloat16)
    d_mid_part = right_dot(d_gate_low[:row_total], w_gate) + right_dot(d_up_low[:row_total], w_up)
    grad_down, d_mid = sums_call(3, 48, [(part_down, 32, False)], [(d_mid_part, 32)])
    chosen = jnp.where(y == 0, d_gate_low, d_up_low)
    part_chosen = left_dot(mid_all, chosen)

    d_resid_norm, grad_gain_pre_ffn = mid_back(d_mid)
    d_resid = grad_out + d_resid_norm
    d_attn, grad_gain_post_attn = post_attn_back(d_resid)
    d_attn_low = d_attn.astype(jnp.bfloat16)
    part_out = left_dot(context, d_attn_low)
    d_context = right_dot(d_attn_low, w_out).astype(jnp.bfloat16).reshape(row_total, head_local, HD)
    d_query_blocks = []
    d_keys = jnp.zeros((row_total, HD), jnp.float32)
    d_values = jnp.zeros((row_total, HD), jnp.float32)
    for block_index in range(block_count):
        scores, start, stop = block_scores(block_index)
        probs = jnp.exp(scores - log_totals[block_index])
        probs_low = probs.astype(jnp.bfloat16)
        grad_block = d_context[start:stop]
        d_probs = jnp.einsum("rhd,kd->hrk", grad_block, value_rows[:stop], preferred_element_type=jnp.float32)
        row_inner = jnp.sum(probs * d_probs, axis=-1, keepdims=True)
        d_scores = (probs * (d_probs - row_inner)).astype(jnp.bfloat16)
        d_query_blocks.append(
            jnp.einsum("hrk,kd->rhd", d_scores, key_rows[:stop], preferred_element_type=jnp.float32) * score_scale
        )
        d_keys = d_keys.at[:stop].add(
            jnp.einsum("hrk,rhd->kd", d_scores, queries[start:stop], preferred_element_type=jnp.float32)
            * score_scale
        )
        d_values = d_values.at[:stop].add(
            jnp.einsum("hrk,rhd->kd", probs_low, grad_block, preferred_element_type=jnp.float32)
        )
    d_queries = jnp.concatenate(d_query_blocks, axis=0)
    d_query_raw, grad_query_part = query_back(d_queries)
    d_query_low = d_query_raw.astype(jnp.bfloat16)
    part_query = left_dot(normed_in, d_query_low)
    d_in_part = right_dot(d_query_low, w_query)
    extra = jnp.zeros((32, 2 * HD), jnp.float32).at[0, :HD].set(grad_query_part)
    key_value_part = jnp.concatenate([jnp.concatenate([d_keys, d_values], axis=1), extra], axis=0)
    grad_chosen, grad_query, grad_out_w, key_value_sum, d_in_sum = sums_call(
        4,
        56,
        [(part_chosen, 16, False), (part_query, 64, True), (part_out, 16, True)],
        [(key_value_part, 16), (d_in_part, 16)],
    )
    grad_gain_query = key_value_sum[row_total, :HD]
    d_keys_sum = key_value_sum[:row_total, :HD]
    d_values_sum = key_value_sum[:row_total, HD:]
    d_key_raw, grad_gain_key = key_back(d_keys_sum)
    d_key_low = d_key_raw.astype(jnp.bfloat16)
    d_value_low = d_values_sum.astype(jnp.bfloat16)
    part_key_value = left_dot(normed_in, jnp.concatenate([d_key_low, d_value_low], axis=1))
    d_in = d_in_sum + right_dot(d_key_low, w_key) + right_dot(d_value_low, w_value)
    d_hidden_norm, grad_gain_in = norm_in_back(d_in)
    grad_hidden = (d_resid + d_hidden_norm).astype(jnp.bfloat16)
    gains = (grad_gain_in, grad_gain_post_attn, grad_gain_pre_ffn, grad_gain_post_ffn, grad_gain_query, grad_gain_key)
    flat = jnp.concatenate(gains)
    flat = jnp.pad(flat, (0, 64 * 2 * HD - flat.shape[0])).reshape(64, 2 * HD)
    (last,) = sums_call(5, 32, [(jnp.concatenate([part_key_value, flat], axis=0), 32, True)], [])
    last = last.reshape(-1, 2 * HD)
    flat = last[width:].reshape(-1)
    cuts = [0]
    for gain in gains:
        cuts.append(cuts[-1] + gain.shape[0])
    gains = [flat[a:b] for a, b in zip(cuts, cuts[1:])]
    grads = [
        grad_query.reshape(width, head_local * HD),
        last[:width, :HD],
        last[:width, HD:],
        grad_out_w.reshape(head_local * HD, width),
        grad_chosen[0],
        grad_chosen[1],
        grad_down.reshape(units, width),
    ] + gains
    if rest_groups is not None:
        grads = [lax.psum(grad, "dp", axis_index_groups=rest_groups) for grad in grads]
    return (output, grad_hidden, *grads)


def solution(mesh):
    dp_size = mesh.shape["dp"]
    span_size = LINE * PAIR
    rest_groups = None
    if dp_size > span_size:
        rest_groups = [list(range(i, dp_size, span_size)) for i in range(span_size)]
    rows, columns, whole = P("dp", None), P(None, "mp"), P()
    in_specs = (rows, rows, columns, whole, whole, P("mp", None), columns, columns, P("mp", None)) + (whole,) * 6 + (rows,)
    out_specs = (rows, rows, columns, whole, whole, P("mp", None), columns, columns, P("mp", None)) + (whole,) * 6
    return jax.shard_map(
        functools.partial(per_device, rest_groups), mesh=mesh, in_specs=in_specs, out_specs=out_specs, check_vma=False
    )
```

time: 1830 us -> 785 us (0.43)
  waiting for transfers between devices: 1510 us -> 0 us
  Pallas kernels: 0 us -> 532 us
  blocking collectives: 75.6 us -> 0 us
  matrix products: 106 us -> 136 us
    reduce_scatter x7 -> x0, waiting for transfers between devices: 675 us -> none  [the longest x1 149 us: per_device(): lax.psum_scatter(grad_w_gate, 'dp', scatter_dimension=0, tiled=True)]
    pallas_call x0 -> x5, Pallas kernels: none -> 532 us  [the longest x3 405 us: sums_call(): pl.pallas_call(functools.partial(sums_kernel, lines, sums), out_shape=out...]
    all_gather x7 -> x0, waiting for transfers between devices: 427 us -> none  [the longest x1 124 us: per_device(): lax.all_gather(summed_parts[4], 'dp', axis=0, tiled=True)]
    psum x4 -> x0, waiting for transfers between devices: 406 us -> none  [the longest x1 122 us: per_device(): lax.psum((d_in_part, key_value_part, grad_query_part), 'mp')]
    unnamed x2 -> x0, blocking collectives: 69.9 us -> none
    dot_general x7, matrix products: 25.2 us -> 48.9 us  [matmul(): return jnp.dot(left, right, preferred_element_type=jnp.float32)]
    dot_general x7 -> x5, matrix products: 38.3 us -> 29.7 us  [left_dot(): lax.dot_general(left, right, (((0,), (0,)), ((), ())), preferred_element_...]
    unnamed x177 -> x182, local copies, waits for them, and re-layouts: 49.7 us -> 41.2 us
  transfers between devices with their start and end apart: 18 -> 0, of which waited for: 16 -> 0; matrix products, arithmetic and copies ran while one was open for 4% -> 0% of each run, Pallas kernels for 0% -> 0%
where the time goes in v1:
time: 785 us; the launch traced here: 776 us
  Pallas kernels  532 us (68%)
  matrix products  136 us (17%)
  local copies, waits for them, and re-layouts  62.2 us (8%)
  other arithmetic  43.3 us (6%)
    pallas_call x3, Pallas kernels, sums_call(): pl.pallas_call(functools.partial(sums_kernel, lines, sums), out_shape=out...  405 us
    pallas_call x2, Pallas kernels, derive_call(): pl.pallas_call(functools.partial(derive_kernel, make, len(aux), r), out_s...  127 us
    dot_general x7, matrix products, right_dot(): lax.dot_general(left, right, (((1,), (1,)), ((), ())), preferred_element_...  52 us
    dot_general x7, matrix products, matmul(): return jnp.dot(left, right, preferred_element_type=jnp.float32)  48.9 us
    unnamed x182, local copies, waits for them, and re-layouts  41.2 us
    dot_general x5, matrix products, left_dot(): lax.dot_general(left, right, (((0,), (0,)), ((), ())), preferred_element_...  29.7 us

profile of v1, /device:TPU:0, one launch (start us, length us, event | category | flops | bytes accessed | tf_op | source)
XLA Modules:
  0.0 775.6 jit_solution(13483459267749786935)
XLA Ops:
  0.7 2.3 fusion.17
  3.5 3.5 convolution_convert_fusion.1
  9.4 2.3 fusion.77
  13.8 2.5 copy.41
  17.8 2.4 fusion.71
  25.5 64.3 %derive_1.1 = (f32[1024,1152]{1,0:T(8,128)S(1)}, f32[2,1024,1152]{2,1,0:T(8,128)}) custom-call(f32[1024,1152]{1,0:T(8,128)S(1)} %fusion.91.p, bf16[1024,1152]{1,0:T(8,128)(2,1)S(1)} %copy-done.2, f32[1,1152]{1,0:T(1,128)S(1)} %broadcast_in_dim.28.refs_1_, f32[1,1152]{1,0:T(1,128)S(1)} %broadcast_in_dim.29.refs_2_), custom_call_target="tpu_custom_call" | custom-call | tf_op jit(solution)/shard_map/derive_1/pallas_call | solution.py:358
  91.9 4.3 convert_element_type.107
  96.7 12.0 %fusion.135 = f32[2048,1728]{0,1:T(8,128)} fusion(bf16[2048,1152]{1,0:T(8,128)(2,1)S(1)} %bitcast.152, bf16[1152,1728]{0,1:T(8,128)(2,1)S(1)} %copy-done.72), kind=kOutput, calls=%fused_computation.229 | convolution fusion | flops 8153726976 | bytes 22855680 | tf_op jit(solution)/shard_map/dot_general | solution.py:397
  108.7 21.1 %multiply_convert_fusion.1 = (bf16[2048,1728]{0,1:T(8,128)(2,1)}, f32[2048,1728]{0,1:T(8,128)}) fusion(f32[2048,1728]{0,1:T(8,128)} %fusion.135, bf16[2048,1152]{1,0:T(8,128)(2,1)S(1)} %bitcast.153, bf16[1152,1728]{0,1:T(8,128)(2,1)} %param.37), kind=kOutput, calls=%fused_computation.11 | convolution fusion | flops 8189116416 | bytes 44089344 | tf_op jit(solution)/shard_map/dot_general | solution.py:397
  129.8 8.3 %fusion.22.p = f32[1024,1152]{1,0:T(8,128)S(1)} fusion(bf16[1728,1152]{1,0:T(8,128)(2,1)} %param.38, bf16[2048,1728]{0,1:T(8,128)(2,1)} %get-tuple-element.191), kind=kOutput, calls=%fused_computation.53 | convolution fusion | flops 4076863488 | bytes 12238848 | tf_op jit(solution)/shard_map/dot_general | solution.py:397
  138.1 62.7 %derive_2.1 = (f32[1024,1152]{1,0:T(8,128)S(1)}, f32[2,1024,1152]{2,1,0:T(8,128)}) custom-call(f32[1024,1152]{1,0:T(8,128)S(1)} %fusion.22.p, bf16[1024,1152]{1,0:T(8,128)(2,1)S(1)} %copy-done.4, f32[1,1152]{1,0:T(1,128)S(1)} %broadcast_in_dim.30.refs_1_), custom_call_target="tpu_custom_call" | custom-call | tf_op jit(solution)/shard_map/derive_2/pallas_call | solution.py:358
  203.0 6.3 convert_element_type.112
  209.4 8.3 %fusion.24.refs_0_ = f32[864,1152]{1,0:T(8,128)S(1)} fusion(bf16[2048,1152]{1,0:T(8,128)(2,1)} %bitcast.155, bf16[2048,1728]{0,1:T(8,128)(2,1)} %get-tuple-element.191, s32[]{:T(128)S(6)} %select_n.23), kind=kOutput, calls=%fused_computation.55 | convolution fusion | flops 4076863488 | bytes 12238852 | tf_op jit(solution)/shard_map/dot_general | solution.py:401
  217.7 28.4 %multiply_convert_fusion = (bf16[2048,1728]{0,1:T(8,128)(2,1)}, bf16[2048,1728]{0,1:T(8,128)(2,1)}) fusion(f32[2048,1728]{0,1:T(8,128)} %fusion.135, f32[2048,1728]{0,1:T(8,128)} %get-tuple-element.192, bf16[2048,1152]{1,0:T(8,128)(2,1)S(1)} %bitcast.156, bf16[1728,1152]{1,0:T(8,128)(2,1)} %param.38), kind=kOutput, calls=%fused_computation.10 | convolution fusion | flops 8252817408 | bytes 51167232 | tf_op jit(solution)/shard_map/dot_general | solution.py:405
  246.1 8.5 %fusion.20 = f32[1024,1152]{1,0:T(8,128)S(1)} fusion(bf16[1152,1728]{0,1:T(8,128)(2,1)} %param.36, bf16[2048,1728]{0,1:T(8,128)(2,1)} %get-tuple-element.157), kind=kOutput, calls=%fused_computation.51 | convolution fusion | flops 4076863488 | bytes 12238848 | tf_op jit(solution)/shard_map/dot_general | solution.py:405
  254.6 6.8 convolution_add_fusion.2.refs_1_
  261.5 108.0 %sums_3.1 = (f32[2,864,1152]{2,1,0:T(8,128)}, f32[1024,1152]{1,0:T(8,128)}) custom-call(f32[864,1152]{1,0:T(8,128)S(1)} %fusion.24.refs_0_, f32[1024,1152]{1,0:T(8,128)} %convolution_add_fusion.2.refs_1_), custom_call_target="tpu_custom_call" | custom-call | tf_op jit(solution)/shard_map/sums_3/pallas_call | solution.py:321
  375.8 5.7 fusion.13
  381.5 15.9 %fusion.6.refs_0_ = f32[1152,1728]{1,0:T(8,128)} fusion(bf16[2048,1152]{1,0:T(8,128)(2,1)} %bitcast.154, bf16[2048,1728]{0,1:T(8,128)(2,1)} %get-tuple-element.157, bf16[2048,1728]{0,1:T(8,128)(2,1)} %get-tuple-element.156, pred[]{:T(512)S(6)} %eq.63), kind=kOutput, calls=%fused_computation.20 | convolution fusion | flops 8157265920 | bytes 26836992 | tf_op jit(solution)/shard_map/dot_general | solution.py:401
  403.5 2.4 fusion.80
  413.8 3.1 fusion.136.refs_4_
  416.9 241.3 %sums_4.1 = (f32[2,1152,1728]{2,1,0:T(8,128)}, f32[2,576,256]{2,1,0:T(8,128)}, f32[2,128,1152]{2,1,0:T(8,128)}, f32[1056,512]{1,0:T(8,128)}, f32[1024,1152]{1,0:T(8,128)}) custom-call(f32[1152,1728]{1,0:T(8,128)} %fusion.6.refs_0_, f32[1152,256]{1,0:T(8,128)} %fusion.121.refs_1_, f32[256,1152]{1,0:T(8,128)} %fusion.90.refs_2_, ...), custom_call_target="tpu_custom_call" | custom-call | tf_op jit(solution)/shard_map/sums_4/pallas_call | solution.py:321
  658.2 4.0 fusion.74
  664.0 3.4 fusion.12
  667.5 2.5 fusion.16
  676.0 55.9 %sums_5.1 = f32[2,608,512]{2,1,0:T(8,128)S(1)} custom-call(f32[1216,512]{1,0:T(8,128)S(1)} %pad_maximum_fusion.refs_0_), custom_call_target="tpu_custom_call" | custom-call | tf_op jit(solution)/shard_map/sums_5/pallas_call | solution.py:321
  733.5 11.4 %slice_bitcast_fusion = (f32[1152,1728]{1,0:T(8,128)}, f32[1152,1728]{1,0:T(8,128)}) fusion(f32[2,1152,1728]{2,1,0:T(8,128)} %get-tuple-element.111), kind=kLoop, calls=%fused_computation.18 | loop fusion | bytes 31850496 | tf_op jit(solution)/shard_map/squeeze | solution.py:582
  744.9 8.8 %copy.49 = f32[1152,1728]{0,1:T(8,128)} copy(f32[1152,1728]{1,0:T(8,128)} %get-tuple-element.159) | data formatting | bytes 15925248
  753.7 8.8 %copy.50 = f32[1152,1728]{0,1:T(8,128)} copy(f32[1152,1728]{1,0:T(8,128)} %get-tuple-element.158) | data formatting | bytes 15925248
  763.7 2.4 copy.66
  766.1 2.4 copy.67
  768.4 7.0 copy.68
  (251 shorter events, 46.6 us)
Async XLA Ops:
  3.5 8.2 %copy-start.49 = (f32[1024]{0:T(1024)}, f32[1024]{0:T(1024)S(1)}, u32[]{:S(2)}) copy-start(f32[1024]{0:T(1024)S(1)} %fusion.104) | copy-start | bytes 12292
  7.1 4.6 copy-start.35
  8.2 5.6 copy-start.12
  8.2 5.6 copy-start.44
  8.5 9.3 %copy-start.62 = (f32[128]{0:T(128)}, f32[128]{0:T(128)S(1)}, u32[]{:S(2)}) copy-start(f32[128]{0:T(128)S(1)} %negate_power_fusion) | copy-start | bytes 1540
  9.4 8.4 %copy-start.39 = (f32[1024]{0:T(1024)}, f32[1024]{0:T(1024)S(1)}, u32[]{:S(2)}) copy-start(f32[1024]{0:T(1024)S(1)} %subtract_convert_fusion) | copy-start | bytes 12292
  9.4 7.0 copy-start.60
  11.7 11.0 %copy-start.17 = (bf16[1024,1,128]{0,2,1:T(8,128)(2,1)}, bf16[1024,1,128]{0,2,1:T(8,128)(2,1)S(1)}, u32[]{:S(2)}) copy-start(bf16[1024,1,128]{0,2,1:T(8,128)(2,1)S(1)} %get-tuple-element.171) | copy-start | bytes 786436
  11.7 11.0 %copy-start.19 = (bf16[1024,1,128]{0,2,1:T(8,128)(2,1)}, bf16[1024,1,128]{0,2,1:T(8,128)(2,1)S(1)}, u32[]{:S(2)}) copy-start(bf16[1024,1,128]{0,2,1:T(8,128)(2,1)S(1)} %get-tuple-element.172) | copy-start | bytes 786436
  13.8 7.1 copy-start.54
  91.9 4.8 copy-start.72
  96.2 12.5 %copy-start.14 = (bf16[2,1024,1152]{2,1,0:T(8,128)(2,1)}, bf16[2,1024,1152]{2,1,0:T(8,128)(2,1)S(1)}, u32[]{:S(2)}) copy-start(bf16[2,1024,1152]{2,1,0:T(8,128)(2,1)S(1)} %convert_element_type.107) | copy-start | bytes 14155780
  129.8 8.3 %copy-start.51 = (f32[1152]{0:T(1024)S(1)}, f32[1152]{0:T(1024)}, u32[]{:S(2)}) copy-start(f32[1152]{0:T(1024)} %param.42) | copy-start | bytes 13828
  129.8 8.4 %copy-start.4 = (bf16[1024,1152]{1,0:T(8,128)(2,1)S(1)}, bf16[1024,1152]{1,0:T(8,128)(2,1)}, u32[]{:S(2)}) copy-start(bf16[1024,1152]{1,0:T(8,128)(2,1)} %refs_0_.3) | copy-start | bytes 7077892
  209.4 8.3 %copy-start.15 = (bf16[2,1024,1152]{2,1,0:T(8,128)(2,1)S(1)}, bf16[2,1024,1152]{2,1,0:T(8,128)(2,1)}, u32[]{:S(2)}) copy-start(bf16[2,1024,1152]{2,1,0:T(8,128)(2,1)} %convert_element_type.112) | copy-start | bytes 14155780
  246.0 8.6 %copy-start.73 = (bf16[1152,1728]{0,1:T(8,128)(2,1)S(1)}, bf16[1152,1728]{0,1:T(8,128)(2,1)}, u32[]{:S(2)}) copy-start(bf16[1152,1728]{0,1:T(8,128)(2,1)} %param.37) | copy-start | bytes 11943940
  246.0 8.6 %copy-start.74 = (bf16[2048,1728]{0,1:T(8,128)(2,1)S(1)}, bf16[2048,1728]{0,1:T(8,128)(2,1)}, u32[]{:S(2)}) copy-start(bf16[2048,1728]{0,1:T(8,128)(2,1)} %get-tuple-element.156) | copy-start | bytes 21233668
  246.0 123.4 %slice-start = ((s8[4718592]{0:T(1024)(128)(4,1)}), s8[4194304]{0:T(1024)(128)(4,1)S(1)}, s32[]{:S(2)}) async-start(s8[4718592]{0:T(1024)(128)(4,1)} %bitcast.139), calls=%async_computation | async-start | bytes 8388608
  254.6 114.8 %slice-start.1 = ((s8[4718592]{0:T(1024)(128)(4,1)}), s8[524288]{0:T(1024)(128)(4,1)S(1)}, s32[]{:S(2)}) async-start(s8[4718592]{0:T(1024)(128)(4,1)} %bitcast.139), calls=%async_computation.1 | async-start | bytes 1048576
  369.5 4.7 slice-start.4
  375.8 21.7 %slice-start.2 = ((s8[4718592]{0:T(1024)(128)(4,1)}), s8[524288]{0:T(1024)(128)(4,1)S(1)}, s32[]{:S(2)}) async-start(s8[4718592]{0:T(1024)(128)(4,1)} %bitcast.141), calls=%async_computation.2 | async-start | bytes 1048576
  381.5 15.9 %copy-start.69 = (f32[512]{0:T(512)S(1)}, f32[512]{0:T(512)}, u32[]{:S(2)}) copy-start(f32[512]{0:T(512)} %copy-done.68) | copy-start | bytes 6148
  381.5 15.9 %copy-start.71 = (f32[512]{0:T(512)S(1)}, f32[512]{0:T(512)}, u32[]{:S(2)}) copy-start(f32[512]{0:T(512)} %copy-done.70) | copy-start | bytes 6148
  381.5 16.0 %slice-start.3 = ((s8[4718592]{0:T(1024)(128)(4,1)}), s8[4194304]{0:T(1024)(128)(4,1)S(1)}, s32[]{:S(2)}) async-start(s8[4718592]{0:T(1024)(128)(4,1)} %bitcast.141), calls=%async_computation.3 | async-start | bytes 8388608
  381.5 16.0 %copy-start.6 = (f32[1024,1152]{1,0:T(8,128)S(1)}, f32[1024,1152]{1,0:T(8,128)}, u32[]{:S(2)}) copy-start(f32[1024,1152]{1,0:T(8,128)} %get-tuple-element.164) | copy-start | bytes 14155780
  416.9 245.3 %copy-start.9 = (f32[1024,256]{1,0:T(8,128)S(1)}, f32[1024,256]{1,0:T(8,128)}, u32[]{:S(2)}) copy-start(f32[1024,256]{1,0:T(8,128)} %copy.41) | copy-start | bytes 3145732
  416.9 245.3 %copy-start.43 = (f32[1024]{0:T(1024)S(1)}, f32[1024]{0:T(1024)}, u32[]{:S(2)}) copy-start(f32[1024]{0:T(1024)} %copy-done.42) | copy-start | bytes 12292
  416.9 245.3 %copy-start.61 = (f32[256]{0:T(256)S(1)}, f32[256]{0:T(256)}, u32[]{:S(2)}) copy-start(f32[256]{0:T(256)} %param.44) | copy-start | bytes 3076
  416.9 245.7 %copy-start.55 = (f32[1024]{0:T(1024)S(1)}, f32[1024]{0:T(1024)}, u32[]{:S(2)}) copy-start(f32[1024]{0:T(1024)} %copy-done.54) | copy-start | bytes 12292
  658.2 4.8 copy-start.16
  658.2 4.8 copy-start.36
  663.0 4.4 slice-start.6
  (53 other events, 117.9 us)

commit v2 on v1

--- a/solution.py
+++ b/solution.py
@@ -77,8 +77,8 @@
         pre = [pltpu.VMEM((h, c), jnp.float32), DMA((n,)), DMA] if presum else []
         return [pltpu.VMEM((h, c), jnp.float32)] * 2 + sems + pre
 
-    def __init__(self, at, own, out, r, presum, refs):
-        self.at, self.own, self.out, self.r, self.presum = at, own, out, r, presum
+    def __init__(self, at, own, out, r, presum, refs, make=None):
+        self.at, self.own, self.out, self.r, self.presum, self.make = at, own, out, r, presum, make
         self.r1, self.r2, self.r1s, self.r2s, self.s1, self.s2, self.ys, self.yr, self.ls = refs[:9]
         if presum:
             self.r0, self.r0s, self.s0 = refs[9:]
@@ -113,6 +113,8 @@
                 lax.fori_loop(0, self.n, give, 0)
 
     def local(self, k):
+        if self.make is not None:
+            return self.make(self.rows(k))
         if not self.presum:
             return self.own[self.rows(k), :]
         q = self.rows(k)
@@ -140,8 +142,9 @@
 
     def outer(self, k):
         at, q = self.at, self.rows(k)
-        self.r0[q, :] = self.local(k)
-        send_to(self.r0.at[q], self.r1.at[q], self.s1, self.r1s.at[k], at.chain, at.mp).start()
+        stage = self.r0 if self.presum else self.r1
+        stage[q, :] = self.local(k)
+        send_to(stage.at[q], self.r1.at[q], self.s1, self.r1s.at[k], at.chain, at.mp).start()
 
     def last(self, k):
         at, q = self.at, self.rows(k)
@@ -156,7 +159,7 @@
 
         @pl.when(self.at.end)
         def _():
-            if self.presum:
+            if self.presum or self.make is not None:
                 within(k, self.n, self.outer)
             within(k - self.lag_end, self.n, self.last)
 
@@ -366,6 +369,483 @@
     )(p, *aux)
 
 
+def dot(left, right):
+    return jnp.dot(left, right, preferred_element_type=jnp.float32)
+
+
+def right_dot(left, right):
+    return lax.dot_general(left, right, (((1,), (1,)), ((), ())), preferred_element_type=jnp.float32)
+
+
+class Channel:
+    def __init__(self, at, a, b, stage, sems):
+        self.at, self.a, self.b, self.stage = at, a, b, stage
+        self.given, self.taken, self.crossed, self.arrived = sems
+        self.r = stage.shape[1]
+        self.slots = stage.shape[0]
+        self.n = a.shape[0] // self.r
+
+    def rows(self, k):
+        return span(0, k, self.r)
+
+    def gift(self, k):
+        slot = lax.rem(k, self.slots)
+        return send_to(
+            self.stage.at[slot],
+            self.a.at[self.rows(k)],
+            self.given.at[slot],
+            self.taken.at[k],
+            self.at.dp,
+            self.at.sibling,
+        )
+
+    def give(self, k, value):
+        pl.when(k >= self.slots)(lambda: self.gift(k).wait_send())
+        self.stage[lax.rem(k, self.slots)] = value
+        self.gift(k).start()
+
+    def drain(self):
+        for k in range(self.slots):
+            self.gift(k).wait_send()
+
+    def cross(self, k):
+        q = self.rows(k)
+        return send_to(self.a.at[q], self.b.at[q], self.crossed.at[k], self.arrived.at[k], self.at.dp, self.at.far)
+
+    def first(self, k, mine):
+        q = self.rows(k)
+        self.gift(k).wait_recv()
+        self.a[q, :] = self.a[q, :] + mine
+        self.cross(k).start()
+
+    def total(self, k):
+        q = self.rows(k)
+        self.cross(k).wait_recv()
+        self.cross(k).wait_send()
+        return self.a[q, :] + self.b[q, :]
+
+
+def rms_scale(values):
+    return lax.rsqrt(jnp.mean(values * values, axis=-1, keepdims=True) + epsilon)
+
+
+def ffn_kernel(
+    n,
+    context,
+    w_out,
+    hidden_all,
+    cotangent_all,
+    gain_post_attn,
+    gain_pre_ffn,
+    gain_post_ffn,
+    w_gate_all,
+    w_up_all,
+    w_down_all,
+    attn_out,
+    mid_out,
+    mlp_out,
+    chosen_out,
+    down_out,
+    d_mid_out,
+    d_mlp_pair,
+    a1,
+    b1,
+    a2,
+    b2,
+    l1,
+    l2,
+    stage,
+    mine_stage,
+    load,
+    hidden,
+    cotangent,
+    w_gate,
+    w_up,
+    w_down,
+    d_mlp,
+    slope,
+    gelu,
+    chosen,
+    act_t,
+    r1,
+    r2,
+    given1,
+    taken1,
+    crossed1,
+    arrived1,
+    given2,
+    taken2,
+    crossed2,
+    arrived2,
+    given3,
+    taken3,
+    crossed3,
+    arrived3,
+    in_sems,
+    land1,
+    land2,
+    pair1,
+    pair2,
+    fwd1,
+    fwd2,
+    keep1,
+    keep2,
+    keep3,
+    load_sems,
+    attn_in,
+    mlp_in,
+    d_mid_in,
+    row_sems,
+    chosen_sem,
+    line_r1,
+    line_r2,
+    line_s1,
+    line_s2,
+    line_ys,
+    line_yr,
+    line_ls,
+):
+    at = Place()
+    r = stage.shape[1]
+    half = n * r
+    rows_all = 2 * half
+    mine, theirs = at.core * half, (1 - at.core) * half
+    bf16, f32 = jnp.bfloat16, jnp.float32
+    sel_gate = at.y == 0
+
+    def q(k):
+        return span(0, k, r)
+
+    def pairq(k, base=0):
+        return span(base, k, 2 * r)
+
+    fetch = [
+        (hidden_all.at[span(0, at.core, half)], hidden),
+        (w_gate_all, w_gate),
+        (w_up_all, w_up),
+        (w_down_all, w_down),
+        (cotangent_all.at[span(0, at.core, half)], cotangent),
+    ]
+    fetch = [pltpu.make_async_copy(src, dst, in_sems.at[i]) for i, (src, dst) in enumerate(fetch)]
+    for copy in fetch:
+        copy.start()
+    greet(
+        [
+            (None, at.dp, at.sibling),
+            (None, at.dp, at.far),
+            (None, at.pair, at.mp),
+            (None, at.chain, at.mp),
+            (at.mid, at.across, at.mp),
+        ]
+    )
+    one = Channel(at, a1, b1, stage, (given1, taken1, crossed1, arrived1))
+    two = Channel(at, a2, b2, stage, (given2, taken2, crossed2, arrived2))
+    three = Channel(at, a1, b1, stage, (given3, taken3, crossed3, arrived3))
+
+    def give1(k, _):
+        one.give(k, dot(context[span(theirs, k, r), :], w_out[...]))
+        return 0
+
+    def first1(k, _):
+        one.first(k, dot(context[span(mine, k, r), :], w_out[...]))
+        return 0
+
+    lax.fori_loop(0, n, give1, 0)
+    lax.fori_loop(0, n, first1, 0)
+    one.drain()
+    for copy in fetch:
+        copy.wait()
+
+    def attn_copies(k):
+        o = span(mine, k, r)
+        return (
+            send_to(b1.at[q(k)], attn_out.at[o], keep1.at[0, k], attn_in, at.dp, at.sibling),
+            pltpu.make_async_copy(b1.at[q(k)], attn_out.at[o], keep1.at[1, k]),
+        )
+
+    def mid_copies(k):
+        o = span(mine, k, r)
+        return (
+            send_to(a1.at[q(k)], l1.at[q(k)], keep1.at[2, k], land1.at[k], at.dp, at.sibling),
+            send_to(a1.at[q(k)], mid_out.at[1, o], keep1.at[3, k], pair1.at[k], at.pair, at.mp),
+            pltpu.make_async_copy(a1.at[q(k)], mid_out.at[0, o], keep1.at[4, k]),
+        )
+
+    def mlp_copies(k):
+        o = span(mine, k, r)
+        return (
+            send_to(b2.at[q(k)], mlp_out.at[o], keep2.at[0, k], mlp_in, at.dp, at.sibling),
+            pltpu.make_async_copy(b2.at[q(k)], mlp_out.at[o], keep2.at[1, k]),
+        )
+
+    def d_mlp_copies(k):
+        o = span(mine, k, r)
+        return (
+            send_to(a2.at[q(k)], l2.at[q(k)], keep2.at[2, k], land2.at[k], at.dp, at.sibling),
+            send_to(a2.at[q(k)], d_mlp_pair.at[o], keep2.at[3, k], pair2.at[k], at.pair, at.mp),
+        )
+
+    def d_mid_copies(k):
+        o = span(mine, k, r)
+        return (
+            send_to(b1.at[q(k)], d_mid_out.at[o], keep3.at[0, k], d_mid_in, at.dp, at.sibling),
+            pltpu.make_async_copy(b1.at[q(k)], d_mid_out.at[o], keep3.at[1, k]),
+        )
+
+    def begin(copies):
+        for copy in copies:
+            copy.start()
+
+    def sent(copies):
+        for copy in copies:
+            if copy.is_remote:
+                copy.wait_send()
+            else:
+                copy.wait()
+
+    def second1(k):
+        total = one.total(k)
+        b1[q(k), :] = total
+        begin(attn_copies(k))
+        resid = hidden[q(k), :].astype(f32) + total * rms_scale(total) * gain_post_attn[...]
+        a1[q(k), :] = resid * rms_scale(resid) * gain_pre_ffn[...]
+        begin(mid_copies(k))
+
+    def forward1(k):
+        o = span(mine, k, r)
+        mid_copies(k)[1].wait_recv()
+        send_to(mid_out.at[1, o], mid_out.at[1, o], fwd1.at[0, k], fwd1.at[1, k], at.dp, at.sibling).start()
+
+    def forward2(k):
+        o = span(mine, k, r)
+        d_mlp_copies(k)[1].wait_recv()
+        send_to(d_mlp_pair.at[o], d_mlp_pair.at[o], fwd2.at[0, k], fwd2.at[1, k], at.dp, at.sibling).start()
+
+    def gated(x):
+        gate = dot(x, w_gate[...])
+        up = dot(x, w_up[...])
+        th = jnp.tanh(gelu_coeff * (gate + 0.044715 * gate * gate * gate))
+        cdf = 0.5 * (1.0 + th)
+        ge = gate * cdf
+        sl = cdf + 0.5 * gate * (1.0 - th * th) * (gelu_coeff * (1.0 + 3.0 * 0.044715 * gate * gate))
+        act = (ge * up).astype(bf16)
+        return act, sl * up, ge
+
+    def keep_act(act, columns):
+        turned = act.T
+        units = turned.shape[0] // 2
+        act_t[:, columns] = jnp.where(sel_gate, turned[:units], turned[units:])
+
+    def row_copy(k):
+        return pltpu.make_async_copy(l1.at[q(k)], mid_out.at[0, span(theirs, k, r)], row_sems)
+
+    def forward_block(k):
+        mid_copies(k)[0].wait_recv()
+        row_copy(k).start()
+        x = jnp.concatenate([a1[q(k), :], l1[q(k), :]], axis=0).astype(bf16)
+        act, sl, ge = gated(x)
+        slope[pairq(k), :] = sl.astype(bf16)
+        gelu[pairq(k), :] = ge.astype(bf16)
+        keep_act(act, pairq(k))
+        part = dot(act, w_down[...])
+        two.give(k, part[r:])
+        mine_stage[lax.rem(k, 2)] = part[:r]
+
+    def first2(k):
+        sent(attn_copies(k))
+        two.first(k, mine_stage[lax.rem(k, 2)])
+
+    def load_copies(src, k):
+        slot = lax.rem(k, 2)
+        return (
+            pltpu.make_async_copy(src.at[span(mine, k, r)], load.at[slot, pl.ds(0, r)], load_sems.at[slot, 0]),
+            pltpu.make_async_copy(src.at[span(theirs, k, r)], load.at[slot, pl.ds(r, r)], load_sems.at[slot, 1]),
+        )
+
+    def load1(k):
+        o = span(theirs, k, r)
+        send_to(mid_out.at[1, o], mid_out.at[1, o], fwd1.at[0, k], fwd1.at[1, k], at.dp, at.sibling).wait_recv()
+        begin(load_copies(mid_out.at[1], k))
+
+    def load2(k):
+        o = span(theirs, k, r)
+        send_to(d_mlp_pair.at[o], d_mlp_pair.at[o], fwd2.at[0, k], fwd2.at[1, k], at.dp, at.sibling).wait_recv()
+        begin(load_copies(d_mlp_pair, k))
+
+    def pair_block(k):
+        sent(load_copies(mid_out.at[1], k))
+        act, sl, ge = gated(load[lax.rem(k, 2)].astype(bf16))
+        chosen[pairq(k), :] = jnp.where(sel_gate, sl, ge).astype(bf16)
+        keep_act(act, pairq(k, rows_all))
+
+    def second2(k):
+        total = two.total(k)
+        b2[q(k), :] = total
+        begin(mlp_copies(k))
+        sent(mid_copies(k))
+        scale = rms_scale(total)
+        ge = cotangent[q(k), :].astype(f32) * gain_post_ffn[...]
+        a2[q(k), :] = scale * ge - total * (scale * scale * scale) * jnp.mean(ge * total, axis=-1, keepdims=True)
+        begin(d_mlp_copies(k))
+
+    def chosen_copies(src, k, base):
+        return (
+            pltpu.make_async_copy(
+                src.at[span(0, 2 * k, r)], chosen_out.at[span(base + mine, k, r)], chosen_sem.at[0]
+            ),
+            pltpu.make_async_copy(
+                src.at[span(0, 2 * k + 1, r)], chosen_out.at[span(base + theirs, k, r)], chosen_sem.at[0]
+            ),
+        )
+
+    def backward_block(k):
+        d_mlp_copies(k)[0].wait_recv()
+        x = jnp.concatenate([a2[q(k), :], l2[q(k), :]], axis=0).astype(bf16)
+        d_mlp[pairq(k), :] = x
+        d_act = right_dot(x, w_down[...])
+        d_gate = (d_act * slope[pairq(k), :].astype(f32)).astype(bf16)
+        d_up = (d_act * gelu[pairq(k), :].astype(f32)).astype(bf16)
+        slope[pairq(k), :] = d_gate
+        gelu[pairq(k), :] = d_up
+
+        @pl.when(sel_gate)
+        def _():
+            begin(chosen_copies(slope, k, 0))
+
+        @pl.when(jnp.logical_not(sel_gate))
+        def _():
+            begin(chosen_copies(gelu, k, 0))
+
+        part = right_dot(d_gate, w_gate[...]) + right_dot(d_up, w_up[...])
+        three.give(k, part[r:])
+        mine_stage[lax.rem(k, 2)] = part[:r]
+
+    def first3(k):
+        three.first(k, mine_stage[lax.rem(k, 2)])
+
+    def second3(k):
+        b1[q(k), :] = three.total(k)
+        begin(d_mid_copies(k))
+
+    def take_pair(k):
+        sent(load_copies(d_mlp_pair, k))
+        d_mlp[pairq(k, rows_all), :] = load[lax.rem(k, 2)].astype(bf16)
+
+    def pair_backward(k):
+        d_act = right_dot(d_mlp[pairq(k, rows_all), :], w_down[...])
+        chosen[pairq(k), :] = (d_act * chosen[pairq(k), :].astype(f32)).astype(bf16)
+        begin(chosen_copies(chosen, k, rows_all))
+
+    far_lag = n + 1
+
+    def tick(t, _):
+        within(t, n, second1)
+        within(t - 1, n, forward1)
+        within(t - 1, n, forward_block)
+        within(t - 2, n, first2)
+        within(t - 4, n, load1)
+        within(t - 5, n, pair_block)
+
+        @pl.when(t == far_lag)
+        def _():
+            two.drain()
+
+        within(t - far_lag, n, second2)
+        within(t - far_lag - 1, n, forward2)
+        within(t - far_lag - 1, n, backward_block)
+        within(t - far_lag - 2, n, first3)
+        within(t - far_lag - 3, n, load2)
+        within(t - far_lag - 4, n, take_pair)
+        return 0
+
+    lax.fori_loop(0, far_lag + 4 + n, tick, 0)
+
+    line = LineSum(
+        at,
+        None,
+        down_out,
+        r1.shape[0] // line_r1.shape[0],
+        False,
+        (r1, r2, line_r1, line_r2, line_s1, line_s2, line_ys, line_yr, line_ls),
+        lambda rows: dot(act_t[rows, :], d_mlp[...]),
+    )
+
+    def line_step(t, _):
+        line.step(t)
+
+        @pl.when(lax.rem(t, 2) == 0)
+        def _():
+            within(t // 2 - 1, n, second3)
+
+        @pl.when(lax.rem(t, 2) == 1)
+        def _():
+            within(t // 2, n, pair_backward)
+
+        return 0
+
+    lax.fori_loop(0, max(line.steps, 2 * n + 2), line_step, 0)
+    line.finish()
+    three.drain()
+
+    def settle(k, _):
+        sent(mlp_copies(k))
+        sent(d_mlp_copies(k))
+        sent(d_mid_copies(k))
+        o = span(mine, k, r)
+        send_to(mid_out.at[1, o], mid_out.at[1, o], fwd1.at[0, k], fwd1.at[1, k], at.dp, at.sibling).wait_send()
+        send_to(d_mlp_pair.at[o], d_mlp_pair.at[o], fwd2.at[0, k], fwd2.at[1, k], at.dp, at.sibling).wait_send()
+        return 0
+
+    lax.fori_loop(0, n, settle, 0)
+    for sem in (attn_in, mlp_in, d_mid_in, row_sems):
+        wait_bytes(a1, sem)
+    wait_bytes(slope, chosen_sem.at[0])
+    wait_bytes(chosen, chosen_sem.at[0])
+
+
+def ffn_call(collective_id, context, w_out, hidden, cotangent, gains, w_gate, w_up, w_down, r, line_rows):
+    rows, width = hidden.shape
+    units = w_down.shape[0]
+    half = rows // 2
+    n = half // r
+    lines = units // 2 // line_rows
+    f32, bf16 = jnp.float32, jnp.bfloat16
+
+    def vm(*shape, dtype=f32):
+        return pltpu.VMEM(shape, dtype)
+
+    scratch = [vm(half, width)] * 6
+    scratch += [vm(4, r, width), vm(2, r, width), vm(2, 2 * r, width)]
+    scratch += [vm(half, width, dtype=bf16)] * 2
+    scratch += [vm(width, units, dtype=bf16)] * 2 + [vm(units, width, dtype=bf16)]
+    scratch += [vm(2 * rows, width, dtype=bf16)] + [vm(rows, units, dtype=bf16)] * 3
+    scratch += [vm(units // 2, 2 * rows, dtype=bf16)]
+    scratch += [vm(units // 2, width)] * 2
+    for _ in range(3):
+        scratch += [DMA((4,)), DMA((n,)), DMA((n,)), DMA((n,))]
+    scratch += [DMA((5,)), DMA((n,)), DMA((n,)), DMA((n,)), DMA((n,)), DMA((2, n)), DMA((2, n))]
+    scratch += [DMA((5, n)), DMA((4, n)), DMA((2, n)), DMA((2, 2)), DMA, DMA, DMA, DMA, DMA((1,))]
+    scratch += [DMA((lines,)), DMA((lines,)), DMA, DMA, DMA, DMA, DMA]
+    shape = jax.ShapeDtypeStruct
+    return pl.pallas_call(
+        functools.partial(ffn_kernel, n),
+        out_shape=[
+            shape((rows, width), f32),
+            shape((2, rows, width), f32),
+            shape((rows, width), f32),
+            shape((2 * rows, units), bf16),
+            shape((2, units // 2, width), f32),
+            shape((rows, width), f32),
+            shape((rows, width), f32),
+        ],
+        in_specs=[vmem_spec()] * 2 + [any_spec()] * 2 + [vmem_spec()] * 3 + [any_spec()] * 3,
+        out_specs=[any_spec()] * 7,
+        scratch_shapes=scratch,
+        compiler_params=comm_params(collective_id, 62),
+        name="ffn",
+    )(context, w_out, hidden, cotangent, *gains, w_gate, w_up, w_down)
+
+
 def rms_norm(values, gain_vec):
     return values * lax.rsqrt(jnp.mean(values * values, axis=-1, keepdims=True) + epsilon) * gain_vec
 
@@ -399,11 +879,6 @@
 
 def left_dot(left, right):
     return lax.dot_general(left, right, (((0,), (0,)), ((), ())), preferred_element_type=jnp.float32)
-
-
-def right_dot(left, right):
-    return lax.dot_general(left, right, (((1,), (1,)), ((), ())), preferred_element_type=jnp.float32)
-
 
 def per_device(
     rest_groups,
@@ -478,39 +953,28 @@
             )
         )
     context = jnp.concatenate(context_blocks, axis=0).reshape(row_total, head_local * HD).astype(jnp.bfloat16)
-    attn, mid_all = derive_call(
-        1, attn_derive, matmul(context, w_out), 32, (hidden, gain_post_attn[None], gain_pre_ffn[None])
+    units = w_down.shape[0]
+    attn, mid_all, mlp_out, chosen, grad_down, d_mid, _ = ffn_call(
+        1,
+        context,
+        w_out,
+        hidden,
+        cotangent,
+        (gain_post_attn[None], gain_pre_ffn[None], gain_post_ffn[None]),
+        w_gate,
+        w_up,
+        w_down,
+        64,
+        32,
     )
     post_attn, post_attn_back = jax.vjp(rms_norm, attn, gain_post_attn)
     resid = hidden_full + post_attn
-    mid_full, mid_back = jax.vjp(rms_norm, resid, gain_pre_ffn)
+    _, mid_back = jax.vjp(rms_norm, resid, gain_pre_ffn)
     mid_all = mid_all.reshape(2 * row_total, width).astype(jnp.bfloat16)
-    gate = matmul(mid_all, w_gate)
-    up_proj = matmul(mid_all, w_up)
-
-    def gated(gate_vals, up_vals):
-        return gelu_tanh(gate_vals) * up_vals
-
-    act_full, gated_back = jax.vjp(gated, gate, up_proj)
-    activated = act_full.astype(jnp.bfloat16)
-    mlp_out, d_mlp_all = derive_call(
-        2, mlp_derive, matmul(activated[:row_total], w_down), 32, (cotangent, gain_post_ffn[None])
-    )
     grad_out = cotangent.astype(jnp.float32)
     post_ffn, post_ffn_back = jax.vjp(rms_norm, mlp_out, gain_post_ffn)
     output = (resid + post_ffn).astype(jnp.bfloat16)
     _, grad_gain_post_ffn = post_ffn_back(grad_out)
-    d_mlp_all = d_mlp_all.reshape(2 * row_total, width).astype(jnp.bfloat16)
-    units = w_down.shape[0]
-    act_half = lax.dynamic_slice(activated, (0, y * (units // 2)), (2 * row_total, units // 2))
-    part_down = left_dot(act_half, d_mlp_all)
-    d_act = right_dot(d_mlp_all, w_down)
-    d_gate, d_up = gated_back(d_act)
-    d_gate_low = d_gate.astype(jnp.bfloat16)
-    d_up_low = d_up.astype(jnp.bfloat16)
-    d_mid_part = right_dot(d_gate_low[:row_total], w_gate) + right_dot(d_up_low[:row_total], w_up)
-    grad_down, d_mid = sums_call(3, 48, [(part_down, 32, False)], [(d_mid_part, 32)])
-    chosen = jnp.where(y == 0, d_gate_low, d_up_low)
     part_chosen = left_dot(mid_all, chosen)
 
     d_resid_norm, grad_gain_pre_ffn = mid_back(d_mid)

time: 785 us -> 699 us (0.89)
  matrix products: 136 us -> 39.8 us
    pallas_call x2 -> x1, Pallas kernels: 127 us -> 240 us  [ffn_call(): pl.pallas_call(functools.partial(ffn_kernel, n), out_shape=[shape((rows,...]
    pallas_call x3 -> x2, Pallas kernels: 405 us -> 298 us  [sums_call(): pl.pallas_call(functools.partial(sums_kernel, lines, sums), out_shape=out...]
    dot_general x7 -> x4, matrix products: 52 us -> 8.02 us  [right_dot(): lax.dot_general(left, right, (((1,), (1,)), ((), ())), preferred_element_...]
    dot_general x7 -> x3, matrix products: 48.9 us -> 5.99 us  [matmul(): return jnp.dot(left, right, preferred_element_type=jnp.float32)]
    dot_general x5 -> x4, matrix products: 29.7 us -> 19.5 us  [left_dot(): lax.dot_general(left, right, (((0,), (0,)), ((), ())), preferred_element_...]
    unnamed x182 -> x98, local copies, waits for them, and re-layouts: 41.2 us -> 44.8 us
where the time goes in v2:
time: 699 us; the launch traced here: 691 us
  Pallas kernels  538 us (77%)
  local copies, waits for them, and re-layouts  66.7 us (10%)
  other arithmetic  44.3 us (6%)
  matrix products  39.8 us (6%)
    pallas_call x2, Pallas kernels, sums_call(): pl.pallas_call(functools.partial(sums_kernel, lines, sums), out_shape=out...  298 us
    pallas_call x1, Pallas kernels, ffn_call(): pl.pallas_call(functools.partial(ffn_kernel, n), out_shape=[shape((rows,...  240 us
    unnamed x98, local copies, waits for them, and re-layouts  44.8 us
    dot_general x4, matrix products, left_dot(): lax.dot_general(left, right, (((0,), (0,)), ((), ())), preferred_element_...  19.5 us

profile of v2, /device:TPU:0, one launch (start us, length us, event | category | flops | bytes accessed | tf_op | source)
XLA Modules:
  0.0 690.7 jit_solution(608550515480804089)
XLA Ops:
  0.7 2.3 fusion.8
  3.0 2.7 convolution_convert_fusion.1
  7.8 2.3 fusion.61
  10.1 2.1 multiply_reduce_fusion.11
  14.0 2.4 fusion.55
  23.2 6.3 copy.48.w_gate_all
  29.6 6.3 copy.49.w_up_all
  35.9 239.8 %ffn.1 = (f32[1024,1152]{1,0:T(8,128)}, f32[2,1024,1152]{2,1,0:T(8,128)}, f32[1024,1152]{1,0:T(8,128)}, bf16[2048,1728]{1,0:T(8,128)(2,1)}, f32[2,864,1152]{2,1,...) custom-call(bf16[1024,256]{1,0:T(8,128)(2,1)} %maximum_bitcast_fusion.context, bf16[256,1152]{1,0:T(8,128)(2,1)} %w_out.1, ...), custom_call_target="tpu_custom_call" | custom-call | tf_op jit(solution)/shard_map/ffn/pallas_call | solution.py:830
  275.8 2.9 multiply_reduce_fusion.6
  279.5 3.1 multiply_reduce_fusion.4
  283.2 1.9 multiply_reduce_fusion
  285.1 7.1 %fusion.4 = (f32[1152]{0:T(1024)S(1)}, bf16[1024,1152]{1,0:T(8,128)(2,1)}, f32[1024]{0:T(1024)S(1)}, f32[1152]{0:T(1024)S(1)}, f32[1024,1152]{1,0:T(8,128)S(1)}) fusion(bf16[1024,1152]{1,0:T(8,128)(2,1)S(1)} %copy-done.11, f32[1024,1152]{1,0:T(8,128)S(1)} %bitcast.130, f32[1024]{0:T(1024)S(1)} %add_rsqrt_fusion, f32[1024,1152]{1,0:T(8,128)S(1)} %get-tuple-element.155, ...), kind=kLoop, calls=%fused_computation.18 | loop fusion | flops 22409984 | bytes 28355072 | tf_op jit(solution)/shard_map/transpose(jvp())/reduce_sum | solution.py:850
  292.2 4.2 convert_element_type.93
  296.4 14.0 %fusion.115.refs_0_ = f32[1152,1728]{1,0:T(8,128)} fusion(bf16[2048,1152]{1,0:T(8,128)(2,1)S(1)} %bitcast.132, bf16[2048,1728]{1,0:T(8,128)(2,1)} %get-tuple-element.106), kind=kOutput, calls=%fused_computation.201 | convolution fusion | flops 8153726976 | bytes 19759104 | tf_op jit(solution)/shard_map/dot_general | solution.py:881
  315.9 2.6 fusion.64
  319.1 2.1 fusion.101.refs_1_
  321.2 1.9 fusion.99.refs_2_
  324.7 1.7 select_maximum_fusion.refs_3_
  326.4 3.1 fusion.116.refs_4_
  329.5 241.9 %sums_4.1 = (f32[2,1152,1728]{2,1,0:T(8,128)}, f32[2,576,256]{2,1,0:T(8,128)}, f32[2,128,1152]{2,1,0:T(8,128)}, f32[1056,512]{1,0:T(8,128)}, f32[1024,1152]{1,0:T(8,128)}) custom-call(f32[1152,1728]{1,0:T(8,128)} %fusion.115.refs_0_, f32[1152,256]{1,0:T(8,128)} %fusion.101.refs_1_, f32[256,1152]{1,0:T(8,128)} %fusion.99.refs_2_, ...), custom_call_target="tpu_custom_call" | custom-call | tf_op jit(solution)/shard_map/sums_4/pallas_call | solution.py:324
  571.4 4.2 fusion.58
  575.7 1.7 multiply_reduce_fusion.7
  578.7 3.1 fusion.3
  581.8 2.5 fusion.7
  590.4 56.2 %sums_5.1 = f32[2,608,512]{2,1,0:T(8,128)S(1)} custom-call(f32[1216,512]{1,0:T(8,128)S(1)} %pad_maximum_fusion.refs_0_), custom_call_target="tpu_custom_call" | custom-call | tf_op jit(solution)/shard_map/sums_5/pallas_call | solution.py:324
  646.6 1.6 fusion.108
  648.2 11.5 %slice_bitcast_fusion = (f32[1152,1728]{1,0:T(8,128)}, f32[1152,1728]{1,0:T(8,128)}) fusion(f32[2,1152,1728]{2,1,0:T(8,128)} %get-tuple-element.111), kind=kLoop, calls=%fused_computation.5 | loop fusion | bytes 31850496 | tf_op jit(solution)/shard_map/squeeze | solution.py:1046
  659.7 8.8 %copy.57 = f32[1152,1728]{0,1:T(8,128)} copy(f32[1152,1728]{1,0:T(8,128)} %get-tuple-element.157) | data formatting | bytes 15925248
  668.5 8.8 %copy.58 = f32[1152,1728]{0,1:T(8,128)} copy(f32[1152,1728]{1,0:T(8,128)} %get-tuple-element.156) | data formatting | bytes 15925248
  678.5 2.4 copy.76
  680.9 2.4 copy.77
  683.2 7.0 %copy.78 = f32[1728,1152]{1,0:T(8,128)} copy(f32[1728,1152]{1,0:T(8,128)} %bitcast.131) | data formatting | bytes 15925248
  (153 shorter events, 28.1 us)
Async XLA Ops:
  0.6 2.3 copy-start
  2.9 2.8 copy-start.2
  3.0 2.8 copy-start.28
  3.0 2.7 copy-start.37
  5.7 11.7 %copy-start.17 = (bf16[1024,256]{1,0:T(8,128)(2,1)}, bf16[1024,256]{1,0:T(8,128)(2,1)S(1)}, u32[]{:S(2)}) copy-start(bf16[1024,256]{1,0:T(8,128)(2,1)S(1)} %convolution_convert_fusion.1) | copy-start | bytes 1572868
  5.8 4.3 copy-start.30
  6.9 5.3 copy-start.12
  7.8 6.0 copy-start.39
  10.1 8.3 %copy-start.15 = (bf16[1024,1,128]{0,2,1:T(8,128)(2,1)}, bf16[1024,1,128]{0,2,1:T(8,128)(2,1)S(1)}, u32[]{:S(2)}) copy-start(bf16[1024,1,128]{0,2,1:T(8,128)(2,1)S(1)} %get-tuple-element.170) | copy-start | bytes 786436
  13.8 3.7 copy-start.7
  16.4 2.0 copy-start.23
  16.4 2.0 copy-start.25
  18.4 3.1 copy-start.19
  18.4 3.0 copy-start.33
  18.4 3.6 copy-start.34
  18.4 4.2 copy-start.36
  18.8 296.4 %copy-start.9 = (f32[1,512,512]{1,2,0:T(8,128)}, f32[1,512,512]{1,2,0:T(8,128)S(1)}, u32[]{:S(2)}) copy-start(f32[1,512,512]{1,2,0:T(8,128)S(1)} %get-tuple-element.188) | copy-start | bytes 3145732
  275.7 3.8 copy-start.1
  275.8 6.9 slice-start
  279.5 3.1 slice-start.1
  279.5 3.7 copy-start.6
  283.2 1.9 copy-start.11
  314.8 3.6 copy-start.13
  315.5 3.5 copy-start.3
  319.1 2.1 copy-start.20
  319.1 2.1 copy-start.22
  319.1 4.0 copy-start.10
  321.2 2.7 copy-start.16
  323.9 2.5 copy-start.29
  571.4 6.0 copy-start.8
  571.4 6.3 copy-start.14
  571.4 6.3 copy-start.31
  (10 other events, 13.7 us)

commit v3 on v2

--- a/solution.py
+++ b/solution.py
@@ -83,7 +83,8 @@
         if presum:
             self.r0, self.r0s, self.s0 = refs[9:]
         self.h = out.shape[1]
-        self.n = self.h // r
+        self.n = self.r1s.shape[0]
+        self.r = self.h // self.n
         self.steps = self.n + self.lag_end
         self.base = at.y * self.h if presum else 0
 
@@ -441,22 +442,28 @@
     w_gate_all,
     w_up_all,
     w_down_all,
-    attn_out,
-    mid_out,
-    mlp_out,
+    out_out,
+    mid_low,
     chosen_out,
     down_out,
-    d_mid_out,
+    d_attn_out,
+    d_resid_out,
+    gains_out,
+    mid_pair,
     d_mlp_pair,
     a1,
     b1,
     a2,
     b2,
+    b3,
     l1,
     l2,
     stage,
     mine_stage,
     load,
+    mid_stage,
+    turned_stage,
+    gains,
     hidden,
     cotangent,
     w_gate,
@@ -492,11 +499,11 @@
     keep2,
     keep3,
     load_sems,
-    attn_in,
-    mlp_in,
-    d_mid_in,
-    row_sems,
-    chosen_sem,
+    mid_sems,
+    turned_sem,
+    out_in,
+    d_attn_in,
+    gains_sem,
     line_r1,
     line_r2,
     line_s1,
@@ -540,7 +547,7 @@
     )
     one = Channel(at, a1, b1, stage, (given1, taken1, crossed1, arrived1))
     two = Channel(at, a2, b2, stage, (given2, taken2, crossed2, arrived2))
-    three = Channel(at, a1, b1, stage, (given3, taken3, crossed3, arrived3))
+    three = Channel(at, a1, b3, stage, (given3, taken3, crossed3, arrived3))
 
     def give1(k, _):
         one.give(k, dot(context[span(theirs, k, r), :], w_out[...]))
@@ -556,40 +563,33 @@
     for copy in fetch:
         copy.wait()
 
-    def attn_copies(k):
+    gains[...] = jnp.zeros_like(gains)
+
+    def mid_copies(k):
+        return (
+            send_to(a1.at[q(k)], l1.at[q(k)], keep1.at[0, k], land1.at[k], at.dp, at.sibling),
+            send_to(a1.at[q(k)], mid_pair.at[span(mine, k, r)], keep1.at[1, k], pair1.at[k], at.pair, at.mp),
+        )
+
+    def out_copies(k):
         o = span(mine, k, r)
         return (
-            send_to(b1.at[q(k)], attn_out.at[o], keep1.at[0, k], attn_in, at.dp, at.sibling),
-            pltpu.make_async_copy(b1.at[q(k)], attn_out.at[o], keep1.at[1, k]),
+            send_to(b2.at[q(k)], out_out.at[o], keep2.at[0, k], out_in, at.dp, at.sibling),
+            pltpu.make_async_copy(b2.at[q(k)], out_out.at[o], keep2.at[1, k]),
         )
 
-    def mid_copies(k):
+    def d_mlp_copies(k):
+        return (
+            send_to(a2.at[q(k)], l2.at[q(k)], keep2.at[2, k], land2.at[k], at.dp, at.sibling),
+            send_to(a2.at[q(k)], d_mlp_pair.at[span(mine, k, r)], keep2.at[3, k], pair2.at[k], at.pair, at.mp),
+        )
+
+    def d_attn_copies(k):
         o = span(mine, k, r)
         return (
-            send_to(a1.at[q(k)], l1.at[q(k)], keep1.at[2, k], land1.at[k], at.dp, at.sibling),
-            send_to(a1.at[q(k)], mid_out.at[1, o], keep1.at[3, k], pair1.at[k], at.pair, at.mp),
-            pltpu.make_async_copy(a1.at[q(k)], mid_out.at[0, o], keep1.at[4, k]),
-        )
-
-    def mlp_copies(k):
-        o = span(mine, k, r)
-        return (
-            send_to(b2.at[q(k)], mlp_out.at[o], keep2.at[0, k], mlp_in, at.dp, at.sibling),
-            pltpu.make_async_copy(b2.at[q(k)], mlp_out.at[o], keep2.at[1, k]),
-        )
-
-    def d_mlp_copies(k):
-        o = span(mine, k, r)
-        return (
-            send_to(a2.at[q(k)], l2.at[q(k)], keep2.at[2, k], land2.at[k], at.dp, at.sibling),
-            send_to(a2.at[q(k)], d_mlp_pair.at[o], keep2.at[3, k], pair2.at[k], at.pair, at.mp),
-        )
-
-    def d_mid_copies(k):
-        o = span(mine, k, r)
-        return (
-            send_to(b1.at[q(k)], d_mid_out.at[o], keep3.at[0, k], d_mid_in, at.dp, at.sibling),
-            pltpu.make_async_copy(b1.at[q(k)], d_mid_out.at[o], keep3.at[1, k]),
+            send_to(b3.at[q(k)], d_attn_out.at[o], keep3.at[0, k], d_attn_in, at.dp, at.sibling),
+            pltpu.make_async_copy(b3.at[q(k)], d_attn_out.at[o], keep3.at[1, k]),
+            pltpu.make_async_copy(a1.at[q(k)], d_resid_out.at[q(k)], keep3.at[2, k]),
         )
 
     def begin(copies):
@@ -603,18 +603,21 @@
             else:
                 copy.wait()
 
+    def resid_rows(k):
+        attn = b1[q(k), :]
+        scale = rms_scale(attn)
+        return attn, scale, hidden[q(k), :].astype(f32) + attn * scale * gain_post_attn[...]
+
     def second1(k):
-        total = one.total(k)
-        b1[q(k), :] = total
-        begin(attn_copies(k))
-        resid = hidden[q(k), :].astype(f32) + total * rms_scale(total) * gain_post_attn[...]
+        b1[q(k), :] = one.total(k)
+        _, _, resid = resid_rows(k)
         a1[q(k), :] = resid * rms_scale(resid) * gain_pre_ffn[...]
         begin(mid_copies(k))
 
     def forward1(k):
         o = span(mine, k, r)
         mid_copies(k)[1].wait_recv()
-        send_to(mid_out.at[1, o], mid_out.at[1, o], fwd1.at[0, k], fwd1.at[1, k], at.dp, at.sibling).start()
+        send_to(mid_pair.at[o], mid_pair.at[o], fwd1.at[0, k], fwd1.at[1, k], at.dp, at.sibling).start()
 
     def forward2(k):
         o = span(mine, k, r)
@@ -622,8 +625,8 @@
         send_to(d_mlp_pair.at[o], d_mlp_pair.at[o], fwd2.at[0, k], fwd2.at[1, k], at.dp, at.sibling).start()
 
     def gated(x):
-        gate = dot(x, w_gate[...])
-        up = dot(x, w_up[...])
+        gate = right_dot(x, w_gate[...])
+        up = right_dot(x, w_up[...])
         th = jnp.tanh(gelu_coeff * (gate + 0.044715 * gate * gate * gate))
         cdf = 0.5 * (1.0 + th)
         ge = gate * cdf
@@ -636,13 +639,27 @@
         units = turned.shape[0] // 2
         act_t[:, columns] = jnp.where(sel_gate, turned[:units], turned[units:])
 
-    def row_copy(k):
-        return pltpu.make_async_copy(l1.at[q(k)], mid_out.at[0, span(theirs, k, r)], row_sems)
+    def mid_copy(k, base):
+        slot = 1 if base else 0
+        return pltpu.make_async_copy(mid_stage.at[slot], mid_low.at[pairq(k, base)], mid_sems.at[slot])
+
+    def keep_mid(x, k, base):
+        pl.when(k >= 1)(lambda: mid_copy(k, base).wait())
+        mid_stage[1 if base else 0] = x
+        mid_copy(k, base).start()
+
+    def turned_copy(k, base):
+        return pltpu.make_async_copy(turned_stage, chosen_out.at[:, pairq(k, base)], turned_sem)
+
+    def keep_chosen(x, k, base):
+        pl.when((k >= 1) | (base > 0))(lambda: turned_copy(k, base).wait())
+        turned_stage[...] = x.T
+        turned_copy(k, base).start()
 
     def forward_block(k):
         mid_copies(k)[0].wait_recv()
-        row_copy(k).start()
         x = jnp.concatenate([a1[q(k), :], l1[q(k), :]], axis=0).astype(bf16)
+        keep_mid(x, k, 0)
         act, sl, ge = gated(x)
         slope[pairq(k), :] = sl.astype(bf16)
         gelu[pairq(k), :] = ge.astype(bf16)
@@ -652,7 +669,6 @@
         mine_stage[lax.rem(k, 2)] = part[:r]
 
     def first2(k):
-        sent(attn_copies(k))
         two.first(k, mine_stage[lax.rem(k, 2)])
 
     def load_copies(src, k):
@@ -664,8 +680,8 @@
 
     def load1(k):
         o = span(theirs, k, r)
-        send_to(mid_out.at[1, o], mid_out.at[1, o], fwd1.at[0, k], fwd1.at[1, k], at.dp, at.sibling).wait_recv()
-        begin(load_copies(mid_out.at[1], k))
+        send_to(mid_pair.at[o], mid_pair.at[o], fwd1.at[0, k], fwd1.at[1, k], at.dp, at.sibling).wait_recv()
+        begin(load_copies(mid_pair, k))
 
     def load2(k):
         o = span(theirs, k, r)
@@ -673,30 +689,26 @@
         begin(load_copies(d_mlp_pair, k))
 
     def pair_block(k):
-        sent(load_copies(mid_out.at[1], k))
-        act, sl, ge = gated(load[lax.rem(k, 2)].astype(bf16))
+        sent(load_copies(mid_pair, k))
+        x = load[lax.rem(k, 2)].astype(bf16)
+        keep_mid(x, k, rows_all)
+        act, sl, ge = gated(x)
         chosen[pairq(k), :] = jnp.where(sel_gate, sl, ge).astype(bf16)
         keep_act(act, pairq(k, rows_all))
 
     def second2(k):
         total = two.total(k)
-        b2[q(k), :] = total
-        begin(mlp_copies(k))
         sent(mid_copies(k))
         scale = rms_scale(total)
-        ge = cotangent[q(k), :].astype(f32) * gain_post_ffn[...]
+        cot = cotangent[q(k), :].astype(f32)
+        unit = total * scale
+        gains[2:3, :] = gains[2:3, :] + jnp.sum(cot * unit, axis=0, keepdims=True)
+        ge = cot * gain_post_ffn[...]
         a2[q(k), :] = scale * ge - total * (scale * scale * scale) * jnp.mean(ge * total, axis=-1, keepdims=True)
         begin(d_mlp_copies(k))
-
-    def chosen_copies(src, k, base):
-        return (
-            pltpu.make_async_copy(
-                src.at[span(0, 2 * k, r)], chosen_out.at[span(base + mine, k, r)], chosen_sem.at[0]
-            ),
-            pltpu.make_async_copy(
-                src.at[span(0, 2 * k + 1, r)], chosen_out.at[span(base + theirs, k, r)], chosen_sem.at[0]
-            ),
-        )
+        _, _, resid = resid_rows(k)
+        b2[q(k), :] = resid + unit * gain_post_ffn[...]
+        begin(out_copies(k))
 
     def backward_block(k):
         d_mlp_copies(k)[0].wait_recv()
@@ -705,18 +717,8 @@
         d_act = right_dot(x, w_down[...])
         d_gate = (d_act * slope[pairq(k), :].astype(f32)).astype(bf16)
         d_up = (d_act * gelu[pairq(k), :].astype(f32)).astype(bf16)
-        slope[pairq(k), :] = d_gate
-        gelu[pairq(k), :] = d_up
-
-        @pl.when(sel_gate)
-        def _():
-            begin(chosen_copies(slope, k, 0))
-
-        @pl.when(jnp.logical_not(sel_gate))
-        def _():
-            begin(chosen_copies(gelu, k, 0))
-
-        part = right_dot(d_gate, w_gate[...]) + right_dot(d_up, w_up[...])
+        keep_chosen(jnp.where(sel_gate, d_gate, d_up), k, 0)
+        part = dot(d_gate, w_gate[...]) + dot(d_up, w_up[...])
         three.give(k, part[r:])
         mine_stage[lax.rem(k, 2)] = part[:r]
 
@@ -724,8 +726,18 @@
         three.first(k, mine_stage[lax.rem(k, 2)])
 
     def second3(k):
-        b1[q(k), :] = three.total(k)
-        begin(d_mid_copies(k))
+        d_mid = three.total(k)
+        attn, scale, resid = resid_rows(k)
+        rescale = rms_scale(resid)
+        gains[1:2, :] = gains[1:2, :] + jnp.sum(d_mid * (resid * rescale), axis=0, keepdims=True)
+        ge = d_mid * gain_pre_ffn[...]
+        back = rescale * ge - resid * (rescale * rescale * rescale) * jnp.mean(ge * resid, axis=-1, keepdims=True)
+        d_resid = cotangent[q(k), :].astype(f32) + back
+        a1[q(k), :] = d_resid
+        gains[0:1, :] = gains[0:1, :] + jnp.sum(d_resid * (attn * scale), axis=0, keepdims=True)
+        ge = d_resid * gain_post_attn[...]
+        b3[q(k), :] = scale * ge - attn * (scale * scale * scale) * jnp.mean(ge * attn, axis=-1, keepdims=True)
+        begin(d_attn_copies(k))
 
     def take_pair(k):
         sent(load_copies(d_mlp_pair, k))
@@ -733,8 +745,7 @@
 
     def pair_backward(k):
         d_act = right_dot(d_mlp[pairq(k, rows_all), :], w_down[...])
-        chosen[pairq(k), :] = (d_act * chosen[pairq(k), :].astype(f32)).astype(bf16)
-        begin(chosen_copies(chosen, k, rows_all))
+        keep_chosen((d_act * chosen[pairq(k), :].astype(f32)).astype(bf16), k, rows_all)
 
     far_lag = n + 1
 
@@ -788,19 +799,23 @@
     three.drain()
 
     def settle(k, _):
-        sent(mlp_copies(k))
+        sent(out_copies(k))
         sent(d_mlp_copies(k))
-        sent(d_mid_copies(k))
+        sent(d_attn_copies(k))
         o = span(mine, k, r)
-        send_to(mid_out.at[1, o], mid_out.at[1, o], fwd1.at[0, k], fwd1.at[1, k], at.dp, at.sibling).wait_send()
+        send_to(mid_pair.at[o], mid_pair.at[o], fwd1.at[0, k], fwd1.at[1, k], at.dp, at.sibling).wait_send()
         send_to(d_mlp_pair.at[o], d_mlp_pair.at[o], fwd2.at[0, k], fwd2.at[1, k], at.dp, at.sibling).wait_send()
         return 0
 
+    keep_gains = pltpu.make_async_copy(gains, gains_out, gains_sem)
+    keep_gains.start()
     lax.fori_loop(0, n, settle, 0)
-    for sem in (attn_in, mlp_in, d_mid_in, row_sems):
+    for sem in (out_in, d_attn_in):
         wait_bytes(a1, sem)
-    wait_bytes(slope, chosen_sem.at[0])
-    wait_bytes(chosen, chosen_sem.at[0])
+    mid_copy(n - 1, 0).wait()
+    mid_copy(n - 1, rows_all).wait()
+    turned_copy(n - 1, rows_all).wait()
+    keep_gains.wait()
 
 
 def ffn_call(collective_id, context, w_out, hidden, cotangent, gains, w_gate, w_up, w_down, r, line_rows):
@@ -814,36 +829,545 @@
     def vm(*shape, dtype=f32):
         return pltpu.VMEM(shape, dtype)
 
-    scratch = [vm(half, width)] * 6
+    scratch = [vm(half, width)] * 7
     scratch += [vm(4, r, width), vm(2, r, width), vm(2, 2 * r, width)]
+    scratch += [vm(2, 2 * r, width, dtype=bf16), vm(units, 2 * r, dtype=bf16), vm(8, width)]
     scratch += [vm(half, width, dtype=bf16)] * 2
-    scratch += [vm(width, units, dtype=bf16)] * 2 + [vm(units, width, dtype=bf16)]
+    scratch += [vm(units, width, dtype=bf16)] * 3
     scratch += [vm(2 * rows, width, dtype=bf16)] + [vm(rows, units, dtype=bf16)] * 3
     scratch += [vm(units // 2, 2 * rows, dtype=bf16)]
     scratch += [vm(units // 2, width)] * 2
     for _ in range(3):
         scratch += [DMA((4,)), DMA((n,)), DMA((n,)), DMA((n,))]
     scratch += [DMA((5,)), DMA((n,)), DMA((n,)), DMA((n,)), DMA((n,)), DMA((2, n)), DMA((2, n))]
-    scratch += [DMA((5, n)), DMA((4, n)), DMA((2, n)), DMA((2, 2)), DMA, DMA, DMA, DMA, DMA((1,))]
+    scratch += [DMA((2, n)), DMA((4, n)), DMA((3, n)), DMA((2, 2)), DMA((2,)), DMA, DMA, DMA, DMA]
     scratch += [DMA((lines,)), DMA((lines,)), DMA, DMA, DMA, DMA, DMA]
     shape = jax.ShapeDtypeStruct
     return pl.pallas_call(
         functools.partial(ffn_kernel, n),
         out_shape=[
             shape((rows, width), f32),
-            shape((2, rows, width), f32),
+            shape((2 * rows, width), bf16),
+            shape((units, 2 * rows), bf16),
+            shape((2, units // 2, width), f32),
             shape((rows, width), f32),
-            shape((2 * rows, units), bf16),
-            shape((2, units // 2, width), f32),
+            shape((half, width), f32),
+            shape((8, width), f32),
             shape((rows, width), f32),
             shape((rows, width), f32),
         ],
         in_specs=[vmem_spec()] * 2 + [any_spec()] * 2 + [vmem_spec()] * 3 + [any_spec()] * 3,
+        out_specs=[any_spec()] * 9,
+        scratch_shapes=scratch,
+        compiler_params=comm_params(collective_id, 63),
+        name="ffn",
+    )(context, w_out, hidden, cotangent, *gains, w_gate, w_up, w_down)
+
+
+def turn_dot(left, right):
+    return lax.dot_general(left, right, (((0,), (0,)), ((), ())), preferred_element_type=jnp.float32)
+
+
+def grads_kernel(
+    n,
+    columns_in,
+    seg_row,
+    gain_in,
+    gain_query,
+    gain_key,
+    gain_parts,
+    chosen_all,
+    mid_all,
+    d_attn_all,
+    d_resid_all,
+    hidden_all,
+    normed_all,
+    queries_all,
+    keys_all,
+    values_all,
+    context_all,
+    query_raw_all,
+    key_raw_all,
+    cosine_all,
+    sine_all,
+    w_out_all,
+    w_query_all,
+    w_key_all,
+    w_value_all,
+    hidden_out,
+    chosen_out,
+    w_out_out,
+    w_query_out,
+    key_value_part,
+    key_value_out,
+    gains_out,
+    chosen,
+    mid,
+    hidden,
+    normed,
+    queries,
+    keys,
+    values,
+    context,
+    query_raw,
+    key_raw,
+    cosine,
+    sine,
+    w_out,
+    w_query,
+    w_key,
+    w_value,
+    d_attn,
+    d_context,
+    load,
+    d_keys,
+    d_values,
+    d_raw,
+    a,
+    b,
+    stage,
+    mine_stage,
+    own_out,
+    own_query,
+    own_kv,
+    kv_core,
+    kv_far,
+    kv_quarter,
+    gain_hops,
+    given,
+    taken,
+    crossed,
+    arrived,
+    in_sems,
+    load_sems,
+    keep,
+    hidden_in,
+    kv_sems,
+    gain_send,
+    gain_arrive,
+    gains_sem,
+    *line_refs,
+):
+    at = Place()
+    f32, bf16 = jnp.float32, jnp.bfloat16
+    r = stage.shape[1]
+    half = n * r
+    rows_all, width = normed.shape
+    mine, theirs = at.core * half, (1 - at.core) * half
+    x = at.mp // 2
+    blocks = rows_all // (2 * r)
+    wide = 2 * r
+
+    def q(k):
+        return span(0, k, r)
+
+    pairs = [
+        (chosen_all, chosen),
+        (mid_all, mid),
+        (w_out_all, w_out),
+        (context_all, context),
+        (queries_all, queries),
+        (keys_all, keys),
+        (values_all, values),
+        (cosine_all, cosine),
+        (sine_all, sine),
+        (query_raw_all, query_raw),
+        (key_raw_all, key_raw),
+        (w_query_all, w_query),
+        (w_key_all, w_key),
+        (w_value_all, w_value),
+        (normed_all, normed),
+    ]
+    fetch = [pltpu.make_async_copy(src, dst, in_sems.at[i]) for i, (src, dst) in enumerate(pairs)]
+
+    def load_copy(k):
+        slot = lax.rem(k, 2)
+        return pltpu.make_async_copy(d_attn_all.at[span(0, k, wide)], load.at[slot], load_sems.at[slot])
+
+    def late_copies(k):
+        slot = lax.rem(k, 2)
+        return (
+            pltpu.make_async_copy(d_resid_all.at[q(k)], load.at[slot, pl.ds(0, r)], load_sems.at[slot]),
+            pltpu.make_async_copy(hidden_all.at[span(mine, k, r)], hidden.at[slot], in_sems.at[15 + slot]),
+        )
+
+    for copy in fetch[:4]:
+        copy.start()
+    load_copy(0).start()
+    for copy in fetch[4:]:
+        copy.start()
+    greet(
+        [
+            (None, at.dp, at.sibling),
+            (None, at.dp, at.far),
+            (None, at.pair, at.mp),
+            (None, at.chain, at.mp),
+            (at.mid, at.across, at.mp),
+        ]
+    )
+    channel = Channel(at, a, b, stage, (given, taken, crossed, arrived))
+    line_refs = list(line_refs)
+
+    def take(count):
+        got = line_refs[:count]
+        del line_refs[:count]
+        return got
+
+    line_chosen = LineSum(
+        at, None, chosen_out, None, False, take(9), lambda rows: dot(chosen[rows, :], mid[...])
+    )
+    line_out = LineSum(at, own_out, w_out_out, None, True, take(12))
+    line_query = LineSum(at, own_query, w_query_out, None, True, take(12))
+    line_kv = LineSum(at, kv_quarter, key_value_part, None, True, take(12))
+
+    d_keys[...] = jnp.zeros_like(d_keys)
+    d_values[...] = jnp.zeros_like(d_values)
+    gain_hops[0] = gain_parts[...]
+    gain_hops[0, 4:5, : 2 * HD] = jnp.zeros((1, 2 * HD), f32)
+
+    def context_block(k):
+        @pl.when(k == 0)
+        def _():
+            fetch[2].wait()
+
+        load_copy(k).wait()
+        pl.when(k + 1 < blocks)(lambda: load_copy(k + 1).start())
+        rows = span(0, k, wide)
+        low = load[lax.rem(k, 2)].astype(bf16)
+        d_attn[rows, :] = low
+        d_context[rows, :] = right_dot(low, w_out[...]).astype(bf16)
+
+    def out_block(j):
+        @pl.when(j == 0)
+        def _():
+            fetch[3].wait()
+
+        columns = span(0, j, 128)
+        own_out[columns, :] = dot(context[:, columns].T, d_attn[...])
+
+    def attention_block(i, size):
+        stop = (i + 1) * size
+        rows = slice(i * size, stop)
+        qi, ki, vi, dc = queries[rows, :], keys[:stop, :], values[:stop, :], d_context[rows, :]
+        scores = right_dot(qi, ki) * score_scale
+        row_at = i * size + lax.broadcasted_iota(jnp.int32, (size, stop), 0)
+        key_at = lax.broadcasted_iota(jnp.int32, (size, stop), 1)
+        allowed = (columns_in[rows, 1:2] == seg_row[:, :stop]) & (key_at <= row_at)
+        probs = jnp.exp(jnp.where(allowed, scores, masked_value) - columns_in[rows, 0:1])
+        d_probs = right_dot(dc, vi)
+        inner = jnp.sum(probs * d_probs, axis=-1, keepdims=True)
+        d_scores = (probs * (d_probs - inner)).astype(bf16)
+        d_query = dot(d_scores, ki) * score_scale
+        d_query, part_query = head_back(d_query, query_raw[rows, :], gain_query, rows)
+        d_raw[rows, :HD] = d_query.astype(bf16)
+        gain_hops[0, 4:5, :HD] = gain_hops[0, 4:5, :HD] + part_query
+        d_keys[:stop, :] = d_keys[:stop, :] + turn_dot(d_scores, qi) * score_scale
+        d_values[:stop, :] = d_values[:stop, :] + turn_dot(probs.astype(bf16), dc)
+
+    def rope_back(grad, cos_rows, sin_rows):
+        first, second = grad[:, : HD // 2], grad[:, HD // 2 :]
+        return jnp.concatenate(
+            [first * cos_rows + second * sin_rows, second * cos_rows - first * sin_rows], axis=-1
+        )
+
+    def head_back(grad, raw, gain, rows):
+        back = rope_back(grad, cosine[rows, :], sine[rows, :])
+        scale = rms_scale(raw)
+        part = jnp.sum(back * (raw * scale), axis=0, keepdims=True)
+        ge = gain[...] * back
+        return scale * ge - raw * (scale * scale * scale) * jnp.mean(ge * raw, axis=-1, keepdims=True), part
+
+    def raw_block(k):
+        rows = span(0, k, 2 * wide)
+        d_key, part_key = head_back(d_keys[rows, :], key_raw[rows, :], gain_key, rows)
+        d_raw[rows, HD : 2 * HD] = d_key.astype(bf16)
+        d_raw[rows, 2 * HD :] = d_values[rows, :].astype(bf16)
+        gain_hops[0, 4:5, HD : 2 * HD] = gain_hops[0, 4:5, HD : 2 * HD] + part_key
+
+    def in_block(k):
+        @pl.when(k == 0)
+        def _():
+            for copy in fetch[11:14]:
+                copy.wait()
+
+        low = jnp.concatenate([d_raw[span(mine, k, r), :], d_raw[span(theirs, k, r), :]], axis=0)
+        part = (
+            right_dot(low[:, :HD], w_query[...])
+            + right_dot(low[:, HD : 2 * HD], w_key[...])
+            + right_dot(low[:, 2 * HD :], w_value[...])
+        )
+        channel.give(k, part[r:])
+        mine_stage[lax.rem(k, 2)] = part[:r]
+
+    def in_first(k):
+        channel.first(k, mine_stage[lax.rem(k, 2)])
+
+    def weight_block(j):
+        @pl.when(j == 0)
+        def _():
+            fetch[14].wait()
+
+        columns = span(0, j, 128)
+        grad = dot(normed[:, columns].T, d_raw[...])
+        own_query[columns, :] = grad[:, :HD]
+        own_kv[columns, :] = grad[:, HD:]
+
+    def hidden_copies(k):
+        o = span(mine, k, r)
+        return (
+            send_to(b.at[q(k)], hidden_out.at[o], keep.at[0, k], hidden_in, at.dp, at.sibling),
+            pltpu.make_async_copy(b.at[q(k)], hidden_out.at[o], keep.at[1, k]),
+        )
+
+    def in_second(k):
+        @pl.when(k == 0)
+        def _():
+            for copy in late_copies(0):
+                copy.start()
+
+        for copy in late_copies(k):
+            copy.wait()
+
+        @pl.when(k + 1 < n)
+        def _():
+            for copy in late_copies(k + 1):
+                copy.start()
+
+        d_in = channel.total(k)
+        rows = hidden[lax.rem(k, 2)].astype(f32)
+        scale = rms_scale(rows)
+        gain_hops[0, 3:4, :] = gain_hops[0, 3:4, :] + jnp.sum(d_in * (rows * scale), axis=0, keepdims=True)
+        ge = d_in * gain_in[...]
+        back = scale * ge - rows * (scale * scale * scale) * jnp.mean(ge * rows, axis=-1, keepdims=True)
+        b[q(k), :] = load[lax.rem(k, 2), :r] + back
+        for copy in hidden_copies(k):
+            copy.start()
+
+    kv_rows = width // 2
+    kv_part = width // 4
+    kv_mine = at.core * kv_rows
+    kv_give = send_to(
+        own_kv.at[span(0, 1 - at.core, kv_rows)], kv_core, kv_sems.at[0], kv_sems.at[1], at.dp, at.sibling
+    )
+    kv_cross = send_to(kv_core.at[span(0, 1 - x, kv_part)], kv_far, kv_sems.at[2], kv_sems.at[3], at.dp, at.far)
+    quarter = span(kv_mine, x, kv_part)
+    far_quarter = span(kv_mine, 1 - x, kv_part)
+    kv_whole = key_value_out.at[span(0, at.core, kv_rows)]
+    kv_back = send_to(
+        key_value_out.at[quarter], key_value_out.at[quarter], kv_sems.at[4], kv_sems.at[5], at.dp, at.far
+    )
+    kv_return = send_to(kv_whole, kv_whole, kv_sems.at[6], kv_sems.at[7], at.dp, at.sibling)
+
+    def kv_add_core():
+        kv_give.wait_recv()
+        kv_core[...] = kv_core[...] + own_kv[span(0, at.core, kv_rows), :]
+        kv_cross.start()
+
+    def kv_add_far():
+        kv_cross.wait_recv()
+        kv_quarter[...] = kv_far[...] + kv_core[span(0, x, kv_part), :]
+        line_kv.start()
+
+    hops = [(at.dp, at.sibling), (at.dp, at.far), (at.pair, at.mp)]
+
+    def gain_copy(i, dp, mp, src=None):
+        src = i if src is None else src
+        return send_to(gain_hops.at[src], gain_hops.at[i + 1], gain_send.at[i], gain_arrive.at[i], dp, mp)
+
+    def hop_copy(i):
+        src = 0 if i == 0 else 6 + i
+        return gain_copy(i, *hops[i], src=src)
+
+    def gain_start():
+        keep_x = jnp.where(lax.broadcasted_iota(jnp.int32, (8, width), 0) < 4, 0.5, 1.0)
+        gain_hops[0] = gain_hops[0] * keep_x
+        hop_copy(0).start()
+
+    def gain_hop(i):
+        hop_copy(i).wait_recv()
+        before = 0 if i == 0 else 6 + i
+        gain_hops[7 + i] = gain_hops[before] + gain_hops[i + 1]
+        if i < 2:
+            hop_copy(i + 1).start()
+        else:
+
+            @pl.when(at.end)
+            def _():
+                gain_copy(3, at.chain, at.mp, 9).start()
+
+    to_mid = gain_copy(3, at.chain, at.mp, 9)
+    over = send_to(gain_hops.at[10], gain_hops.at[5], gain_send.at[4], gain_arrive.at[4], at.across, at.mp)
+    to_end = send_to(gain_hops.at[11], gain_hops.at[11], gain_send.at[5], gain_arrive.at[5], at.chain, at.mp)
+
+    def gain_mid():
+        @pl.when(at.mid)
+        def _():
+            to_mid.wait_recv()
+            gain_hops[10] = gain_hops[9] + gain_hops[4]
+            over.start()
+
+    def gain_total():
+        @pl.when(at.mid)
+        def _():
+            over.wait_recv()
+            gain_hops[11] = gain_hops[10] + gain_hops[5]
+            to_end.start()
+
+    def gain_end():
+        pl.when(at.end)(lambda: to_end.wait_recv())
+        pltpu.make_async_copy(gain_hops.at[11], gains_out, gains_sem).start()
+
+    def at_step(t, when, body):
+        pl.when(t == when)(body)
+
+    fetch[0].wait()
+    fetch[1].wait()
+    size = wide
+    queue = line_chosen.n
+    starts = [0, queue, queue + line_out.n, queue + line_out.n + line_query.n]
+    lines = [line_chosen, line_out, line_query, line_kv]
+    steps = starts[-1] + line_kv.steps
+
+    def step(t, _):
+        for line, begin in zip(lines, starts):
+            line.step(t - begin)
+        within(t, blocks, context_block)
+        within(t - blocks, 2, out_block)
+
+        @pl.when(t == blocks + 2)
+        def _():
+            line_out.start()
+            for copy in fetch[4:11]:
+                copy.wait()
+
+        after = blocks + 2
+        for i in range(rows_all // size):
+            at_step(t, after + i, functools.partial(attention_block, i, size))
+        after += rows_all // size
+        within(t - after, rows_all // (2 * wide), raw_block)
+        after += rows_all // (2 * wide)
+        within(t - after, n, in_block)
+        within(t - after - 1, n, in_first)
+        within(t - after, width // 128, weight_block)
+        done = after + width // 128
+
+        @pl.when(t == done)
+        def _():
+            line_query.start()
+            kv_give.start()
+
+        at_step(t, done + 1, kv_add_core)
+        at_step(t, done + 2, kv_add_far)
+
+        late = after + 4
+        within2 = t - late
+
+        @pl.when((within2 >= 0) & (within2 < 2 * n) & (lax.rem(within2, 2) == 0))
+        def _():
+            in_second(within2 // 2)
+
+        final = late + 2 * n
+        at_step(t, final, gain_start)
+        for i in range(3):
+            at_step(t, final + 1 + i, functools.partial(gain_hop, i))
+        at_step(t, final + 4, gain_mid)
+        at_step(t, final + 5, gain_total)
+        at_step(t, final + 6, gain_end)
+        return 0
+
+    final_step = blocks + 2 + rows_all // size + rows_all // (2 * wide) + 4 + 2 * n + 7
+    lax.fori_loop(0, max(steps, final_step), step, 0)
+    line_kv.finish()
+    own_copies = [
+        pltpu.make_async_copy(
+            key_value_part.at[i], key_value_out.at[span(kv_mine + x * kv_part, i, kv_part // 2)], kv_sems.at[8 + i]
+        )
+        for i in range(2)
+    ]
+    for copy in own_copies:
+        copy.start()
+    for copy in own_copies:
+        copy.wait()
+    kv_back.start()
+    line_chosen.finish()
+    line_out.finish()
+    line_query.finish()
+    send_to(key_value_out.at[far_quarter], key_value_out.at[far_quarter], kv_sems.at[4], kv_sems.at[5], at.dp, at.far).wait_recv()
+    kv_return.start()
+    channel.drain()
+
+    def settle(k, _):
+        for copy in hidden_copies(k):
+            if copy.is_remote:
+                copy.wait_send()
+            else:
+                copy.wait()
+        return 0
+
+    lax.fori_loop(0, n, settle, 0)
+    wait_bytes(b, hidden_in)
+    kv_give.wait_send()
+    kv_cross.wait_send()
+    kv_back.wait_send()
+    for i in range(3):
+        hop_copy(i).wait_send()
+    pl.when(at.end)(lambda: to_mid.wait_send())
+
+    @pl.when(at.mid)
+    def _():
+        over.wait_send()
+        to_end.wait_send()
+
+    pltpu.make_async_copy(gain_hops.at[11], gains_out, gains_sem).wait()
+    kv_return.wait_send()
+    other = key_value_out.at[span(0, 1 - at.core, kv_rows)]
+    send_to(other, other, kv_sems.at[6], kv_sems.at[7], at.dp, at.sibling).wait_recv()
+
+
+def grads_call(collective_id, small, large, r, line_rows):
+    chosen, mid, d_attn, d_resid, hidden, normed = large[:6]
+    f32, bf16 = jnp.float32, jnp.bfloat16
+    rows, width = normed.shape
+    units = chosen.shape[0]
+    half = rows // 2
+    n = half // r
+    heads = large[12].shape[1] * 2
+
+    def vm(*shape, dtype=f32):
+        return pltpu.VMEM(shape, dtype)
+
+    scratch = [vm(*chosen.shape, dtype=bf16), vm(*mid.shape, dtype=bf16)]
+    scratch += [vm(2, r, width, dtype=bf16)]
+    scratch += [vm(*x.shape, dtype=x.dtype) for x in large[5:]]
+    scratch += [vm(rows, width, dtype=bf16), vm(rows, heads, dtype=bf16), vm(2, 2 * r, width)]
+    scratch += [vm(rows, heads)] * 2 + [vm(rows, 3 * heads, dtype=bf16)]
+    scratch += [vm(half, width)] * 2 + [vm(2, r, width), vm(2, r, width)]
+    scratch += [vm(heads, width), vm(width, heads), vm(width, 2 * heads)]
+    scratch += [vm(width // 2, 2 * heads), vm(width // 4, 2 * heads), vm(width // 4, 2 * heads), vm(12, 8, width)]
+    scratch += [DMA((2,)), DMA((n,)), DMA((n,)), DMA((n,))]
+    scratch += [DMA((17,)), DMA((2,)), DMA((2, n)), DMA, DMA((10,)), DMA((6,)), DMA((6,)), DMA]
+    scratch += LineSum.scratch(units, width, line_rows[0], False)
+    scratch += LineSum.scratch(heads // 2, width, line_rows[1], True)
+    scratch += LineSum.scratch(width // 2, heads, line_rows[2], True)
+    scratch += LineSum.scratch(width // 8, 2 * heads, line_rows[3], True)
+    shape = jax.ShapeDtypeStruct
+    return pl.pallas_call(
+        functools.partial(grads_kernel, n),
+        out_shape=[
+            shape((rows, width), f32),
+            shape((2, units, width), f32),
+            shape((2, heads // 2, width), f32),
+            shape((2, width // 2, heads), f32),
+            shape((2, width // 8, 2 * heads), f32),
+            shape((width, 2 * heads), f32),
+            shape((8, width), f32),
+        ],
+        in_specs=[vmem_spec()] * len(small) + [any_spec()] * len(large),
         out_specs=[any_spec()] * 7,
         scratch_shapes=scratch,
-        compiler_params=comm_params(collective_id, 62),
-        name="ffn",
-    )(context, w_out, hidden, cotangent, *gains, w_gate, w_up, w_down)
+        compiler_params=comm_params(collective_id, 63),
+        name="grads",
+    )(*small, *large)
 
 
 def rms_norm(values, gain_vec):
@@ -954,96 +1478,62 @@
         )
     context = jnp.concatenate(context_blocks, axis=0).reshape(row_total, head_local * HD).astype(jnp.bfloat16)
     units = w_down.shape[0]
-    attn, mid_all, mlp_out, chosen, grad_down, d_mid, _ = ffn_call(
+    output, mid_low, chosen, grad_down, d_attn, d_resid, gain_parts, _, _ = ffn_call(
         1,
         context,
         w_out,
         hidden,
         cotangent,
         (gain_post_attn[None], gain_pre_ffn[None], gain_post_ffn[None]),
-        w_gate,
-        w_up,
+        w_gate.T,
+        w_up.T,
         w_down,
         64,
         32,
     )
-    post_attn, post_attn_back = jax.vjp(rms_norm, attn, gain_post_attn)
-    resid = hidden_full + post_attn
-    _, mid_back = jax.vjp(rms_norm, resid, gain_pre_ffn)
-    mid_all = mid_all.reshape(2 * row_total, width).astype(jnp.bfloat16)
-    grad_out = cotangent.astype(jnp.float32)
-    post_ffn, post_ffn_back = jax.vjp(rms_norm, mlp_out, gain_post_ffn)
-    output = (resid + post_ffn).astype(jnp.bfloat16)
-    _, grad_gain_post_ffn = post_ffn_back(grad_out)
-    part_chosen = left_dot(mid_all, chosen)
-
-    d_resid_norm, grad_gain_pre_ffn = mid_back(d_mid)
-    d_resid = grad_out + d_resid_norm
-    d_attn, grad_gain_post_attn = post_attn_back(d_resid)
-    d_attn_low = d_attn.astype(jnp.bfloat16)
-    part_out = left_dot(context, d_attn_low)
-    d_context = right_dot(d_attn_low, w_out).astype(jnp.bfloat16).reshape(row_total, head_local, HD)
-    d_query_blocks = []
-    d_keys = jnp.zeros((row_total, HD), jnp.float32)
-    d_values = jnp.zeros((row_total, HD), jnp.float32)
-    for block_index in range(block_count):
-        scores, start, stop = block_scores(block_index)
-        probs = jnp.exp(scores - log_totals[block_index])
-        probs_low = probs.astype(jnp.bfloat16)
-        grad_block = d_context[start:stop]
-        d_probs = jnp.einsum("rhd,kd->hrk", grad_block, value_rows[:stop], preferred_element_type=jnp.float32)
-        row_inner = jnp.sum(probs * d_probs, axis=-1, keepdims=True)
-        d_scores = (probs * (d_probs - row_inner)).astype(jnp.bfloat16)
-        d_query_blocks.append(
-            jnp.einsum("hrk,kd->rhd", d_scores, key_rows[:stop], preferred_element_type=jnp.float32) * score_scale
-        )
-        d_keys = d_keys.at[:stop].add(
-            jnp.einsum("hrk,rhd->kd", d_scores, queries[start:stop], preferred_element_type=jnp.float32)
-            * score_scale
-        )
-        d_values = d_values.at[:stop].add(
-            jnp.einsum("hrk,rhd->kd", probs_low, grad_block, preferred_element_type=jnp.float32)
-        )
-    d_queries = jnp.concatenate(d_query_blocks, axis=0)
-    d_query_raw, grad_query_part = query_back(d_queries)
-    d_query_low = d_query_raw.astype(jnp.bfloat16)
-    part_query = left_dot(normed_in, d_query_low)
-    d_in_part = right_dot(d_query_low, w_query)
-    extra = jnp.zeros((32, 2 * HD), jnp.float32).at[0, :HD].set(grad_query_part)
-    key_value_part = jnp.concatenate([jnp.concatenate([d_keys, d_values], axis=1), extra], axis=0)
-    grad_chosen, grad_query, grad_out_w, key_value_sum, d_in_sum = sums_call(
-        4,
-        56,
-        [(part_chosen, 16, False), (part_query, 64, True), (part_out, 16, True)],
-        [(key_value_part, 16), (d_in_part, 16)],
+    output = output.astype(jnp.bfloat16)
+    grad_hidden, grad_chosen, grad_out_w, grad_query, _, grad_kv, gains = grads_call(
+        2,
+        (
+            jnp.concatenate([jnp.concatenate(log_totals, axis=1)[0], segment_row[:, None].astype(jnp.float32)], axis=1),
+            segment_row[None, :].astype(jnp.float32),
+            gain_in[None],
+            gain_query[None],
+            gain_key[None],
+            gain_parts,
+        ),
+        (
+            chosen,
+            mid_low,
+            d_attn,
+            d_resid,
+            hidden,
+            normed_in,
+            queries.reshape(row_total, HD),
+            key_rows,
+            value_rows,
+            context,
+            query_raw,
+            key_raw,
+            cosine,
+            sine_table,
+            w_out,
+            w_query,
+            w_key,
+            w_value,
+        ),
+        64,
+        (32, 32, 144, 72),
     )
-    grad_gain_query = key_value_sum[row_total, :HD]
-    d_keys_sum = key_value_sum[:row_total, :HD]
-    d_values_sum = key_value_sum[:row_total, HD:]
-    d_key_raw, grad_gain_key = key_back(d_keys_sum)
-    d_key_low = d_key_raw.astype(jnp.bfloat16)
-    d_value_low = d_values_sum.astype(jnp.bfloat16)
-    part_key_value = left_dot(normed_in, jnp.concatenate([d_key_low, d_value_low], axis=1))
-    d_in = d_in_sum + right_dot(d_key_low, w_key) + right_dot(d_value_low, w_value)
-    d_hidden_norm, grad_gain_in = norm_in_back(d_in)
-    grad_hidden = (d_resid + d_hidden_norm).astype(jnp.bfloat16)
-    gains = (grad_gain_in, grad_gain_post_attn, grad_gain_pre_ffn, grad_gain_post_ffn, grad_gain_query, grad_gain_key)
-    flat = jnp.concatenate(gains)
-    flat = jnp.pad(flat, (0, 64 * 2 * HD - flat.shape[0])).reshape(64, 2 * HD)
-    (last,) = sums_call(5, 32, [(jnp.concatenate([part_key_value, flat], axis=0), 32, True)], [])
-    last = last.reshape(-1, 2 * HD)
-    flat = last[width:].reshape(-1)
-    cuts = [0]
-    for gain in gains:
-        cuts.append(cuts[-1] + gain.shape[0])
-    gains = [flat[a:b] for a, b in zip(cuts, cuts[1:])]
+    grad_hidden = grad_hidden.astype(jnp.bfloat16)
+    grad_kv = (grad_kv[:, :HD], grad_kv[:, HD:])
+    gains = [gains[3], gains[0], gains[1], gains[2], gains[4, :HD], gains[4, HD : 2 * HD]]
     grads = [
         grad_query.reshape(width, head_local * HD),
-        last[:width, :HD],
-        last[:width, HD:],
+        *grad_kv,
         grad_out_w.reshape(head_local * HD, width),
-        grad_chosen[0],
-        grad_chosen[1],
+        grad_chosen[0].T,
+        grad_chosen[1].T,
         grad_down.reshape(units, width),
     ] + gains
     if rest_groups is not None:

time: 699 us -> 603 us (0.86); the launches traced: 691 us -> 602 us
  local copies, waits for them, and re-layouts: 66.7 us -> 27.2 us
  matrix products: 39.8 us -> 6.46 us
  other arithmetic: 44.3 us -> 21.4 us
  Pallas kernels: 538 us -> 546 us
    unnamed x98 -> x51, local copies, waits for them, and re-layouts: 44.8 us -> 6.87 us
    dot_general x16 -> x0, matrix products: 30.7 us -> none  [the longest x4 19.5 us: left_dot(): lax.dot_general(left, right, (((0,), (0,)), ((), ())), preferred_element_...]
    transpose x0 -> x1, local copies, waits for them, and re-layouts: none -> 12.2 us  [per_device(): grad_chosen[1]]
    squeeze x1 -> x0, local copies, waits for them, and re-layouts: 11.5 us -> none  [per_device(): grad_chosen[1]]
    reduce_sum x4 -> x0, other arithmetic: 11 us -> none  [rms_norm(): values * lax.rsqrt(jnp.mean(values * values, axis=-1, keepdims=True) + ep...]
    pallas_call x2 -> x1, Pallas kernels: 298 us -> 301 us  [grads_call(): pl.pallas_call(functools.partial(grads_kernel, n), out_shape=[shape((rows...]
where the time goes in v3:
time: 603 us; the launch traced here: 602 us
  Pallas kernels  546 us (91%)
  local copies, waits for them, and re-layouts  27.2 us (5%)
  other arithmetic  21.4 us (4%)
  matrix products  6.46 us (1%)
    pallas_call x1, Pallas kernels, grads_call(): pl.pallas_call(functools.partial(grads_kernel, n), out_shape=[shape((rows...  301 us
    pallas_call x1, Pallas kernels, ffn_call(): pl.pallas_call(functools.partial(ffn_kernel, n), out_shape=[shape((rows,...  245 us
    transpose x1, local copies, waits for them, and re-layouts, per_device(): grad_chosen[1]  12.2 us

profile of v3, /device:TPU:0, one launch (start us, length us, event | category | flops | bytes accessed | tf_op | source)
XLA Modules:
  0.0 602.1 jit_solution(12215916886434481274)
XLA Ops:
  0.7 1.4 convert_reduce_fusion
  2.2 2.2 fusion
  4.4 0.6 broadcast_in_dim.21.gain_post_attn
  5.0 0.6 broadcast_in_dim.22.gain_pre_ffn
  5.6 0.6 broadcast_in_dim.23.gain_post_ffn
  6.2 0.6 broadcast_in_dim.25.gain_in
  6.8 0.6 fusion.33
  7.4 0.6 fusion.2.normed_all
  8.1 0.4 copy-done.11
  8.5 1.6 convolution_convert_fusion.values_all
  10.1 1.9 multiply_reduce_fusion.1
  12.0 1.6 copy.59.key_raw_all
  13.8 3.2 subtract_convert_fusion
  17.0 0.9 multiply_reduce_fusion
  18.6 2.4 fusion.16
  22.4 1.1 pad_maximum_fusion
  23.5 0.6 fusion.35
  24.5 0.6 fusion.8
  25.1 0.8 maximum_bitcast_fusion.context.context_all
  25.9 1.0 copy.63.columns_in
  27.0 245.0 %ffn.1 = (f32[1024,1152]{1,0:T(8,128)}, bf16[2048,1152]{1,0:T(8,128)(2,1)}, bf16[1728,2048]{1,0:T(8,128)(2,1)}, f32[2,864,1152]{2,1,0:T(8,128)}, f32[1024,1152]{...) custom-call(bf16[1024,256]{1,0:T(8,128)(2,1)} %maximum_bitcast_fusion.conte, ...), custom_call_target="tpu_custom_call" | custom-call | tf_op jit(solution)/shard_map/ffn/pallas_call | solution.py:846
  272.0 4.0 convert_element_type.68
  275.9 301.0 %grads.1 = (f32[1024,1152]{1,0:T(8,128)}, f32[2,1728,1152]{2,1,0:T(8,128)}, f32[2,128,1152]{2,1,0:T(8,128)}, f32[2,576,256]{2,1,0:T(8,128)}, f32[2,144,512]{2,1,...) custom-call(f32[1024,2]{1,0:T(8,128)} %copy.63.columns_in, f32[1,1024]{1,0:T(1,128)} %get-tuple-element.57.seg_row, ...), custom_call_target="tpu_custom_call" | custom-call | tf_op jit(solution)/shard_map/grads/pallas_call | solution.py:1354
  577.0 4.1 convert_element_type.71
  581.1 0.6 fusion.32
  581.7 0.6 slice_reduce_fusion
  582.3 1.6 fusion.31
  583.9 12.2 %slice_bitcast_fusion = (f32[1152,1728]{0,1:T(8,128)}, f32[1152,1728]{0,1:T(8,128)}) fusion(f32[2,1728,1152]{2,1,0:T(8,128)} %get-tuple-element.38), kind=kLoop, calls=%fused_computation | loop fusion | bytes 31850496 | tf_op jit(solution)/shard_map/transpose | solution.py:1536
  596.1 1.0 copy.71
  597.1 0.7 copy-done.7
  597.8 1.0 copy.72
  598.8 3.3 copy.73
  (69 shorter events, 2.7 us)
Async XLA Ops:
  0.6 6.8 %copy-start = (bf16[1024,1152]{1,0:T(8,128)(2,1)S(1)}, bf16[1024,1152]{1,0:T(8,128)(2,1)}, u32[]{:S(2)}) copy-start(bf16[1024,1152]{1,0:T(8,128)(2,1)} %hidden_all.3) | copy-start | bytes 7077892
  0.7 3.7 copy-start.13
  0.7 5.6 copy-start.14
  0.7 5.0 copy-start.19
  0.7 4.3 copy-start.18
  0.7 3.7 copy-start.17
  4.4 3.7 copy-start.16
  7.4 1.1 copy-start.11
  8.5 8.5 %copy-start.1 = (bf16[1024,1152]{1,0:T(8,128)(2,1)}, bf16[1024,1152]{1,0:T(8,128)(2,1)S(1)}, u32[]{:S(2)}) copy-start(bf16[1024,1152]{1,0:T(8,128)(2,1)S(1)} %fusion.2.normed_all) | copy-start | bytes 7077892
  8.5 1.6 copy-start.6
  10.1 3.5 copy-start.21
  13.6 3.4 copy-start.2
  13.6 3.4 copy-start.5
  17.0 1.3 copy-start.20
  18.3 3.1 copy-start.3
  18.3 2.6 copy-start.9
  18.3 2.6 copy-start.10
  18.3 2.6 slice-start.2
  20.9 1.0 copy-start.12
  576.9 4.2 copy-start.15
  577.0 5.4 copy-start.4
  582.3 16.5 %slice-start = ((s8[7962624]{0:T(1024)(128)(4,1)}), s8[4194304]{0:T(1024)(128)(4,1)S(1)}, s32[]{:S(2)}) async-start(s8[7962624]{0:T(1024)(128)(4,1)} %bitcast.73), calls=%async_computation | async-start | bytes 8388608
  583.9 12.2 %copy-start.8 = (f32[2,576,256]{2,1,0:T(8,128)S(1)}, f32[2,576,256]{2,1,0:T(8,128)}, u32[]{:S(2)}) copy-start(f32[2,576,256]{2,1,0:T(8,128)} %get-tuple-element.35) | copy-start | bytes 3538948
  583.9 14.9 %slice-start.1 = ((s8[7962624]{0:T(1024)(128)(4,1)}), s8[3768320]{0:T(1024)(128)(4,1)S(1)}, s32[]{:S(2)}) async-start(s8[7962624]{0:T(1024)(128)(4,1)} %bitcast.73), calls=%async_computation.1 | async-start | bytes 7536640
  596.1 1.7 copy-start.7

commit v4 on v2

v4 whole, which is shorter than its diff:
```python
import functools

import jax
import jax.numpy as jnp
from jax import lax
from jax.experimental import pallas as pl
from jax.experimental.pallas import tpu as pltpu
from jax.sharding import PartitionSpec as P

HD = 256
BLOCK = 512
LINE = 4
PAIR = 2

epsilon = 1e-06
rope_base = 1000000.0
gelu_coeff = 0.7978845608028654
score_scale = 0.0625
masked_value = -1e30

MESH = pl.DeviceIdType.MESH
DMA = pltpu.SemaphoreType.DMA


def send_to(src, dst, sent, arrived, dp, mp):
    return pltpu.make_async_remote_copy(
        src_ref=src, dst_ref=dst, send_sem=sent, recv_sem=arrived, device_id=(dp, mp), device_id_type=MESH
    )


def wait_bytes(ref, sem):
    pltpu.make_async_copy(ref, ref, sem).wait()


def span(start, k, r):
    return pl.ds(pl.multiple_of(start + k * r, r), r)


class Place:
    def __init__(self):
        dp, mp = lax.axis_index("dp"), lax.axis_index("mp")
        self.dp, self.mp = dp, mp
        self.y = lax.rem(dp, 2)
        z = lax.rem(dp // 2, LINE)
        self.core = lax.rem(mp, 2)
        self.pair = dp + 1 - 2 * self.y
        self.mid = (z == 1) | (z == 2)
        self.end = (z == 0) | (z == LINE - 1)
        self.chain = jnp.where((z == 0) | (z == 2), dp + 2, dp - 2)
        self.across = jnp.where(z == 1, dp + 2, dp - 2)
        self.sibling = mp + 1 - 2 * self.core
        self.far = lax.rem(mp + 2, 4)


def greet(peers):
    barrier = pltpu.get_barrier_semaphore()
    for cond, dp, mp in peers:

        def signal(dp=dp, mp=mp):
            pl.semaphore_signal(barrier, inc=1, device_id=(dp, mp), device_id_type=MESH)

        signal() if cond is None else pl.when(cond)(signal)
    pl.semaphore_wait(barrier, sum(1 if cond is None else cond.astype(jnp.int32) for cond, _, _ in peers))


def within(k, n, body):
    pl.when((k >= 0) & (k < n))(lambda: body(k))


def dot(left, right):
    return jnp.dot(left, right, preferred_element_type=jnp.float32)


def right_dot(left, right):
    return lax.dot_general(left, right, (((1,), (1,)), ((), ())), preferred_element_type=jnp.float32)


def turn_dot(left, right):
    return lax.dot_general(left, right, (((0,), (0,)), ((), ())), preferred_element_type=jnp.float32)


def vmem_spec():
    return pl.BlockSpec(memory_space=pltpu.VMEM)


def any_spec():
    return pl.BlockSpec(memory_space=pl.ANY)


def comm_params(collective_id, mib):
    return pltpu.CompilerParams(collective_id=collective_id, has_side_effects=True, vmem_limit_bytes=mib * 2**20)


class Section:
    def __init__(self, count, out, base, arrived, group=1, make=None, own=None, r0=None, r0s=None, sent=None):
        self.count, self.out, self.base, self.arrived = count, out, base, arrived
        self.group, self.make = group, make
        self.own, self.r0, self.r0s, self.sent = own, r0, r0s, sent
        self.begin = 0


class Stream:
    lag_mid, lag_end, keep = 2, 5, 12

    def __init__(self, at, r, r1, r2, group, sems, credits, sections):
        self.at, self.r, self.r1, self.r2, self.group = at, r, r1, r2, group
        self.r1s, self.r2s, self.s1, self.s2, self.ys, self.ls = sems
        self.end_free, self.over_free, self.back_free = credits
        self.sections = sections
        self.slots = r1.shape[0] // r
        self.n = 0
        for section in sections:
            section.begin = self.n
            self.n += section.count
        self.steps = self.n + self.keep

    def slot(self, t):
        return lax.rem(t, self.slots)

    def rows(self, t):
        return span(0, self.slot(t), self.r)

    def each(self, t, body):
        for section in self.sections:
            k = t - section.begin
            pl.when((k >= 0) & (k < section.count))(functools.partial(body, section, k))

    def start(self, section):
        at = self.at
        theirs = (1 - at.y) * section.count * self.r

        def give(k, _):
            self.gift(section, k, theirs).start()
            return 0

        lax.fori_loop(0, section.count, give, 0)

    def gift(self, section, k, theirs):
        return send_to(
            section.own.at[span(theirs, k, self.r)],
            section.r0.at[span(0, k, self.r)],
            section.sent.at[k],
            section.r0s.at[k],
            self.at.pair,
            self.at.mp,
        )

    def prepare(self, t):
        def body(section, k):
            if section.make is not None:

                @pl.when(lax.rem(k, section.group) == 0)
                def _():
                    self.group[...] = section.make(k // section.group)

            else:
                mine = self.at.y * section.count * self.r
                self.gift(section, k, 0).wait_recv()
                self.group[: self.r, :] = section.own[span(mine, k, self.r), :] + section.r0[span(0, k, self.r), :]

        self.each(t, body)

    def local(self, t):
        at_group = 0
        for section in self.sections:
            if section.group > 1:
                k = t - section.begin
                at_group = jnp.where((k >= 0) & (k < section.count), lax.rem(k, section.group), at_group)
        return self.group[span(0, at_group, self.r), :]

    def to_mid(self, t):
        q, slot = self.rows(t), self.slot(t)
        return send_to(
            self.r1.at[q], self.r1.at[q], self.s1.at[slot], self.r1s.at[slot], self.at.chain, self.at.mp
        )

    def over(self, t):
        q, slot = self.rows(t), self.slot(t)
        return send_to(
            self.r1.at[q], self.r2.at[q], self.s1.at[slot], self.r2s.at[slot], self.at.across, self.at.mp
        )

    def back(self, t):
        q, slot = self.rows(t), self.slot(t)
        return send_to(
            self.r2.at[q], self.r2.at[q], self.s2.at[slot], self.r2s.at[slot], self.at.chain, self.at.mp
        )

    def total_copies(self, section, k, t):
        q, slot = self.rows(t), self.slot(t)
        o = section.out.at[self.at.y, span(section.base, k, self.r)]
        return (
            send_to(self.r2.at[q], o, self.ys.at[slot], section.arrived, self.at.pair, self.at.mp),
            pltpu.make_async_copy(self.r2.at[q], o, self.ls.at[slot]),
        )

    def give_total(self, t):
        def body(section, k):
            for copy in self.total_copies(section, k, t):
                copy.start()

        self.each(t, body)

    def credit(self, t, sem):
        pl.when(t >= self.slots)(lambda: pl.semaphore_wait(sem, 1))

    def outer(self, t):
        self.r1[self.rows(t), :] = self.local(t)
        self.credit(t, self.end_free)
        self.to_mid(t).start()

    def last(self, t):
        self.back(t).wait_recv()
        self.give_total(t)

    def first(self, t):
        q = self.rows(t)
        self.to_mid(t).wait_recv()
        self.r1[q, :] = self.r1[q, :] + self.local(t)
        self.credit(t, self.over_free)
        self.over(t).start()

    def second(self, t):
        q = self.rows(t)
        self.over(t).wait_recv()
        self.r2[q, :] = self.r2[q, :] + self.r1[q, :]
        self.credit(t, self.back_free)
        self.back(t).start()
        self.give_total(t)

    def signal(self, sem, dp):
        pl.semaphore_signal(sem, inc=1, device_id=(dp, self.at.mp), device_id_type=MESH)

    def release(self, t):
        at = self.at
        again = t < self.n - self.slots
        to_pair, kept = self.total_copies(self.sections[0], 0, t)
        self.to_mid(t).wait_send()
        to_pair.wait_send()
        kept.wait()

        @pl.when(at.mid)
        def _():
            self.back(t).wait_send()

            @pl.when(again)
            def _():
                self.signal(self.end_free, at.chain)
                self.signal(self.over_free, at.across)

        @pl.when(at.end & again)
        def _():
            self.signal(self.back_free, at.chain)

    def step(self, t):
        within(t - self.keep, self.n, self.release)
        within(t, self.n, self.prepare)

        @pl.when(self.at.mid)
        def _():
            within(t, self.n, self.first)
            within(t - self.lag_mid, self.n, self.second)

        @pl.when(self.at.end)
        def _():
            within(t, self.n, self.outer)
            within(t - self.lag_end, self.n, self.last)

    def collect(self, section):
        other = section.out.at[1 - self.at.y, pl.ds(section.base, section.count * self.r)]
        send_to(other, other, self.ys.at[0], section.arrived, self.at.pair, self.at.mp).wait_recv()

    def finish_start(self, section):
        for k in range(section.count):
            self.gift(section, k, 0).wait_send()


class Channel:
    def __init__(self, at, a, b, stage, sems):
        self.at, self.a, self.b, self.stage = at, a, b, stage
        self.given, self.taken, self.crossed, self.arrived = sems
        self.r = stage.shape[1]
        self.slots = stage.shape[0]
        self.n = a.shape[0] // self.r

    def rows(self, k):
        return span(0, k, self.r)

    def gift(self, k):
        slot = lax.rem(k, self.slots)
        return send_to(
            self.stage.at[slot],
            self.a.at[self.rows(k)],
            self.given.at[slot],
            self.taken.at[k],
            self.at.dp,
            self.at.sibling,
        )

    def give(self, k, value):
        pl.when(k >= self.slots)(lambda: self.gift(k).wait_send())
        self.stage[lax.rem(k, self.slots)] = value
        self.gift(k).start()

    def drain(self):
        for k in range(self.slots):
            self.gift(k).wait_send()

    def cross(self, k):
        q = self.rows(k)
        return send_to(self.a.at[q], self.b.at[q], self.crossed.at[k], self.arrived.at[k], self.at.dp, self.at.far)

    def first(self, k, mine):
        q = self.rows(k)
        self.gift(k).wait_recv()
        self.a[q, :] = self.a[q, :] + mine
        self.cross(k).start()

    def total(self, k):
        q = self.rows(k)
        self.cross(k).wait_recv()
        self.cross(k).wait_send()
        return self.a[q, :] + self.b[q, :]


def rms_scale(values):
    return lax.rsqrt(jnp.mean(values * values, axis=-1, keepdims=True) + epsilon)


def layer_kernel(
    n,
    r,
    chunk,
    held,
    context,
    w_out,
    columns_in,
    seg_row,
    gain_in,
    gain_post_attn,
    gain_pre_ffn,
    gain_post_ffn,
    gain_query,
    gain_key,
    hidden_all,
    cotangent_all,
    w_gate_all,
    w_up_all,
    w_down_all,
    normed_all,
    queries_all,
    keys_all,
    values_all,
    query_raw_all,
    key_raw_all,
    cosine_all,
    sine_all,
    w_query_all,
    w_key_all,
    w_value_all,
    out_out,
    hidden_out,
    down_out,
    chosen_grad,
    w_out_out,
    w_query_out,
    key_value_part,
    key_value_out,
    gains_out,
    mid_low,
    chosen_out,
    mid_pair,
    d_mlp_pair,
    a1,
    b1,
    a2,
    b2,
    b3,
    l1,
    stage,
    mine_stage,
    load,
    mid_stage,
    turned_stage,
    gain_hops,
    hidden,
    cotangent,
    w_gate,
    w_up,
    w_down,
    d_mlp,
    slope,
    gelu,
    chosen,
    act_t,
    r1,
    r2,
    group,
    chosen_load,
    r0_out,
    r0_query,
    r0_kv,
    kv_far,
    given1,
    taken1,
    crossed1,
    arrived1,
    given2,
    taken2,
    crossed2,
    arrived2,
    given3,
    taken3,
    crossed3,
    arrived3,
    in_sems,
    land1,
    land2,
    land3,
    pair1,
    pair2,
    fwd1,
    fwd2,
    keep1,
    keep2,
    keep3,
    keep4,
    load_sems,
    mid_sems,
    turned_sem,
    out_in,
    hidden_in,
    late_sems,
    chosen_sems,
    kv_sems,
    gain_send,
    gain_arrive,
    gains_sem,
    ring_sems,
    credit_end,
    credit_over,
    credit_back,
    arrived_sems,
    out_sems,
    query_sems,
    kv_pair_sems,
):
    at = Place()
    half = n * r
    rows_all = 2 * half
    width = a1.shape[1]
    units = w_down.shape[0]
    mine, theirs = at.core * half, (1 - at.core) * half
    bf16, f32 = jnp.bfloat16, jnp.float32
    sel_gate = at.y == 0
    x_at = at.mp // 2
    wide = 2 * r

    def q(k):
        return span(0, k, r)

    def pairq(k, base=0):
        return span(base, k, 2 * r)

    fetch = [
        (hidden_all.at[span(0, at.core, half)], hidden),
        (w_gate_all, w_gate),
        (w_up_all, w_up),
        (w_down_all, w_down),
        (cotangent_all.at[span(0, at.core, half)], cotangent),
    ]
    fetch = [pltpu.make_async_copy(src, dst, in_sems.at[i]) for i, (src, dst) in enumerate(fetch)]
    for copy in fetch:
        copy.start()
    greet(
        [
            (None, at.dp, at.sibling),
            (None, at.dp, at.far),
            (None, at.pair, at.mp),
            (None, at.chain, at.mp),
            (at.mid, at.across, at.mp),
        ]
    )
    one = Channel(at, a1, b1, stage, (given1, taken1, crossed1, arrived1))
    two = Channel(at, a2, b2, stage, (given2, taken2, crossed2, arrived2))
    three = Channel(at, a1, b3, stage, (given3, taken3, crossed3, arrived3))

    def give1(k, _):
        one.give(k, dot(context[span(theirs, k, r), :], w_out[...]))
        return 0

    def first1(k, _):
        one.first(k, dot(context[span(mine, k, r), :], w_out[...]))
        return 0

    lax.fori_loop(0, n, give1, 0)
    lax.fori_loop(0, n, first1, 0)
    one.drain()
    for copy in fetch:
        copy.wait()

    gain_hops[0] = jnp.zeros(gain_hops.shape[1:], f32)

    def add_gain(row, part):
        gain_hops[0, row : row + 1, : part.shape[1]] = gain_hops[0, row : row + 1, : part.shape[1]] + part

    def mid_copies(k):
        return (
            send_to(a1.at[q(k)], l1.at[q(k)], keep1.at[0, k], land1.at[k], at.dp, at.sibling),
            send_to(a1.at[q(k)], mid_pair.at[span(mine, k, r)], keep1.at[1, k], pair1.at[k], at.pair, at.mp),
        )

    def out_copies(k):
        o = span(mine, k, r)
        return (
            send_to(b2.at[q(k)], out_out.at[o], keep2.at[0, k], out_in, at.dp, at.sibling),
            pltpu.make_async_copy(b2.at[q(k)], out_out.at[o], keep2.at[1, k]),
        )

    def d_mlp_copies(k):
        return (
            send_to(a2.at[q(k)], l1.at[q(k)], keep2.at[2, k], land2.at[k], at.dp, at.sibling),
            send_to(a2.at[q(k)], d_mlp_pair.at[span(mine, k, r)], keep2.at[3, k], pair2.at[k], at.pair, at.mp),
        )

    def d_attn_copy(k):
        return send_to(b3.at[q(k)], l1.at[q(k)], keep3.at[k], land3.at[k], at.dp, at.sibling)

    def hidden_copies(k):
        o = span(mine, k, r)
        return (
            send_to(b2.at[q(k)], hidden_out.at[o], keep4.at[0, k], hidden_in, at.dp, at.sibling),
            pltpu.make_async_copy(b2.at[q(k)], hidden_out.at[o], keep4.at[1, k]),
        )

    def begin(copies):
        for copy in copies:
            copy.start()

    def sent(copies):
        for copy in copies:
            if copy.is_remote:
                copy.wait_send()
            else:
                copy.wait()

    def resid_rows(k):
        attn = b1[q(k), :]
        scale = rms_scale(attn)
        return attn, scale, hidden[q(k), :].astype(f32) + attn * scale * gain_post_attn[...]

    def second1(k):
        b1[q(k), :] = one.total(k)
        _, _, resid = resid_rows(k)
        a1[q(k), :] = resid * rms_scale(resid) * gain_pre_ffn[...]
        begin(mid_copies(k))

    def forward1(k):
        o = span(mine, k, r)
        mid_copies(k)[1].wait_recv()
        send_to(mid_pair.at[o], mid_pair.at[o], fwd1.at[0, k], fwd1.at[1, k], at.dp, at.sibling).start()

    def forward2(k):
        o = span(mine, k, r)
        d_mlp_copies(k)[1].wait_recv()
        send_to(d_mlp_pair.at[o], d_mlp_pair.at[o], fwd2.at[0, k], fwd2.at[1, k], at.dp, at.sibling).start()

    def gated(x):
        gate = right_dot(x, w_gate[...])
        up = right_dot(x, w_up[...])
        th = jnp.tanh(gelu_coeff * (gate + 0.044715 * gate * gate * gate))
        cdf = 0.5 * (1.0 + th)
        ge = gate * cdf
        sl = cdf + 0.5 * gate * (1.0 - th * th) * (gelu_coeff * (1.0 + 3.0 * 0.044715 * gate * gate))
        act = (ge * up).astype(bf16)
        return act, sl * up, ge

    def keep_act(act, columns):
        turned = act.T
        units = turned.shape[0] // 2
        act_t[:, columns] = jnp.where(sel_gate, turned[:units], turned[units:])

    def mid_copy(k, base):
        slot = 1 if base else 0
        return pltpu.make_async_copy(mid_stage.at[slot], mid_low.at[pairq(k, base)], mid_sems.at[slot])

    def keep_mid(x, k, base):
        pl.when(k >= 1)(lambda: mid_copy(k, base).wait())
        mid_stage[1 if base else 0] = x
        mid_copy(k, base).start()

    def turned_copy(k, base):
        return pltpu.make_async_copy(turned_stage, chosen_out.at[:, pairq(k, base)], turned_sem)

    def keep_chosen(x, k, base):
        pl.when((k >= 1) | (base > 0))(lambda: turned_copy(k, base).wait())
        turned_stage[...] = x.T
        turned_copy(k, base).start()

    def forward_block(k):
        mid_copies(k)[0].wait_recv()
        x = jnp.concatenate([a1[q(k), :], l1[q(k), :]], axis=0).astype(bf16)
        keep_mid(x, k, 0)
        act, sl, ge = gated(x)
        slope[pairq(k), :] = sl.astype(bf16)
        gelu[pairq(k), :] = ge.astype(bf16)
        keep_act(act, pairq(k))
        part = dot(act, w_down[...])
        two.give(k, part[r:])
        mine_stage[lax.rem(k, 2)] = part[:r]

    def first2(k):
        two.first(k, mine_stage[lax.rem(k, 2)])

    def load_copies(src, k):
        slot = lax.rem(k, 2)
        return (
            pltpu.make_async_copy(src.at[span(mine, k, r)], load.at[slot, pl.ds(0, r)], load_sems.at[slot, 0]),
            pltpu.make_async_copy(src.at[span(theirs, k, r)], load.at[slot, pl.ds(r, r)], load_sems.at[slot, 1]),
        )

    def load1(k):
        o = span(theirs, k, r)
        send_to(mid_pair.at[o], mid_pair.at[o], fwd1.at[0, k], fwd1.at[1, k], at.dp, at.sibling).wait_recv()
        begin(load_copies(mid_pair, k))

    def load2(k):
        o = span(theirs, k, r)
        send_to(d_mlp_pair.at[o], d_mlp_pair.at[o], fwd2.at[0, k], fwd2.at[1, k], at.dp, at.sibling).wait_recv()
        begin(load_copies(d_mlp_pair, k))

    def pair_block(k):
        sent(load_copies(mid_pair, k))
        x = load[lax.rem(k, 2)].astype(bf16)
        keep_mid(x, k, rows_all)
        act, sl, ge = gated(x)
        chosen[pairq(k), :] = jnp.where(sel_gate, sl, ge).astype(bf16)
        keep_act(act, pairq(k, rows_all))

    def second2(k):
        total = two.total(k)
        sent(mid_copies(k))
        scale = rms_scale(total)
        cot = cotangent[q(k), :].astype(f32)
        unit = total * scale
        add_gain(2, jnp.sum(cot * unit, axis=0, keepdims=True))
        ge = cot * gain_post_ffn[...]
        a2[q(k), :] = scale * ge - total * (scale * scale * scale) * jnp.mean(ge * total, axis=-1, keepdims=True)
        begin(d_mlp_copies(k))
        _, _, resid = resid_rows(k)
        b2[q(k), :] = resid + unit * gain_post_ffn[...]
        begin(out_copies(k))

    def backward_block(k):
        d_mlp_copies(k)[0].wait_recv()
        x = jnp.concatenate([a2[q(k), :], l1[q(k), :]], axis=0).astype(bf16)
        d_mlp[pairq(k), :] = x
        d_act = right_dot(x, w_down[...])
        d_gate = (d_act * slope[pairq(k), :].astype(f32)).astype(bf16)
        d_up = (d_act * gelu[pairq(k), :].astype(f32)).astype(bf16)
        keep_chosen(jnp.where(sel_gate, d_gate, d_up), k, 0)
        part = dot(d_gate, w_gate[...]) + dot(d_up, w_up[...])
        three.give(k, part[r:])
        mine_stage[lax.rem(k, 2)] = part[:r]

    def first3(k):
        sent(out_copies(k))
        three.first(k, mine_stage[lax.rem(k, 2)])

    def second3(k):
        d_mid = three.total(k)
        sent(d_mlp_copies(k))
        attn, scale, resid = resid_rows(k)
        rescale = rms_scale(resid)
        add_gain(1, jnp.sum(d_mid * (resid * rescale), axis=0, keepdims=True))
        ge = d_mid * gain_pre_ffn[...]
        back = rescale * ge - resid * (rescale * rescale * rescale) * jnp.mean(ge * resid, axis=-1, keepdims=True)
        d_resid = cotangent[q(k), :].astype(f32) + back
        a1[q(k), :] = d_resid
        add_gain(0, jnp.sum(d_resid * (attn * scale), axis=0, keepdims=True))
        ge = d_resid * gain_post_attn[...]
        b3[q(k), :] = scale * ge - attn * (scale * scale * scale) * jnp.mean(ge * attn, axis=-1, keepdims=True)
        d_attn_copy(k).start()

    def take_pair(k):
        sent(load_copies(d_mlp_pair, k))
        d_mlp[pairq(k, rows_all), :] = load[lax.rem(k, 2)].astype(bf16)

    def pair_backward(k):
        d_act = right_dot(d_mlp[pairq(k, rows_all), :], w_down[...])
        keep_chosen((d_act * chosen[pairq(k), :].astype(f32)).astype(bf16), k, rows_all)

    far_lag = n + 1

    def tick(t, _):
        within(t, n, second1)
        within(t - 1, n, forward1)
        within(t - 1, n, forward_block)
        within(t - 2, n, first2)
        within(t - 4, n, load1)
        within(t - 5, n, pair_block)

        @pl.when(t == far_lag)
        def _():
            two.drain()

        within(t - far_lag, n, second2)
        within(t - far_lag - 1, n, forward2)
        within(t - far_lag - 1, n, backward_block)
        within(t - far_lag - 2, n, first3)
        within(t - far_lag - 3, n, load2)
        within(t - far_lag - 4, n, take_pair)
        return 0

    lax.fori_loop(0, far_lag + 4 + n, tick, 0)
    three.drain()
    mid_copy(n - 1, 0).wait()
    mid_copy(n - 1, rows_all).wait()

    normed = w_gate.at[pl.ds(0, rows_all)]
    w_query = w_gate.at[pl.ds(rows_all, HD)]
    w_key = w_gate.at[pl.ds(rows_all + HD, HD)]
    d_attn = w_up.at[pl.ds(0, rows_all)]
    w_value = w_up.at[pl.ds(rows_all, HD)]
    queries = slope.at[:, pl.ds(0, HD)]
    keys = slope.at[:, pl.ds(HD, HD)]
    values = slope.at[:, pl.ds(2 * HD, HD)]
    d_context = slope.at[:, pl.ds(3 * HD, HD)]
    d_raw = gelu.at[:, pl.ds(0, 3 * HD)]

    def halves(ref, base, cols):
        return [ref.at[:, pl.ds(base + i * cols, cols)] for i in range(2)]

    cosine, sine = halves(l1, 0, HD // 2), halves(l1, HD, HD // 2)
    raws = halves(l1, 2 * HD, HD)
    d_keys, d_values = halves(b1, 0, HD), halves(b1, 2 * HD, HD)
    own_out = b3.at[pl.ds(0, HD)]
    kv_core = b3.at[pl.ds(HD, HD)]
    own_query = l1.at[pl.ds(0, HD)]
    own_kv = b1

    def half_copies(src, dst, first):
        return [
            pltpu.make_async_copy(src.at[pl.ds(i * half, half)], dst[i], late_sems.at[first + i]) for i in range(2)
        ]

    early = [
        (normed_all, normed),
        (w_query_all, w_query),
        (w_key_all, w_key),
        (w_value_all, w_value),
        (queries_all, queries),
        (keys_all, keys),
        (values_all, values),
    ]
    early = [pltpu.make_async_copy(src, dst, late_sems.at[i]) for i, (src, dst) in enumerate(early)]
    rope_copies = half_copies(cosine_all, cosine, 7) + half_copies(sine_all, sine, 9)
    rope_copies += half_copies(query_raw_all, raws, 11)
    key_copies = half_copies(key_raw_all, raws, 13)
    mid_load = pltpu.make_async_copy(mid_low, d_mlp, late_sems.at[15])

    def chosen_copy(g):
        slot = lax.rem(g, 2)
        rows = chosen_load.shape[1]
        return pltpu.make_async_copy(chosen_out.at[span(0, g, rows)], chosen_load.at[slot], chosen_sems.at[slot])

    groups = units // chosen_load.shape[1]

    def make_chosen(first, g):
        @pl.when(first + g == 0)
        def _():
            mid_load.wait()

        chosen_copy(first + g).wait()
        pl.when(first + g + 1 < groups)(lambda: chosen_copy(first + g + 1).start())
        return dot(chosen_load[lax.rem(first + g, 2)], d_mlp[...])

    def make_down(g):
        return dot(act_t[span(0, g, group.shape[0]), :], d_mlp[...])

    per = group.shape[0] // chunk
    down_count = units // 2 // chunk
    chosen_count = units // chunk
    head = held * per
    down = Section(down_count, down_out, 0, arrived_sems.at[0], per, make_down)
    chosen_one = Section(head, chosen_grad, 0, arrived_sems.at[1], per, functools.partial(make_chosen, 0))
    chosen_two = Section(
        chosen_count - head,
        chosen_grad,
        head * chunk,
        arrived_sems.at[2],
        per,
        functools.partial(make_chosen, held),
    )

    def presum(out, i, own, r0, sems):
        return Section(
            r0.shape[0] // chunk, out, 0, arrived_sems.at[i], own=own, r0=r0, r0s=sems.at[0], sent=sems.at[1]
        )

    part_kv = presum(key_value_part, 3, kv_far, r0_kv, kv_pair_sems)
    part_out = presum(w_out_out, 4, own_out, r0_out, out_sems)
    part_query = presum(w_query_out, 5, own_query, r0_query, query_sems)
    stream = Stream(
        at,
        chunk,
        r1,
        r2,
        group,
        tuple(ring_sems.at[i] for i in range(6)),
        (credit_end, credit_over, credit_back),
        [down, chosen_one, part_kv, part_out, part_query, chosen_two],
    )

    def take_attn(k):
        d_attn_copy(k).wait_recv()
        low = jnp.concatenate([b3[q(k), :], l1[q(k), :]], axis=0).astype(bf16)
        d_attn[span(mine, k, r), :] = low[:r]
        d_attn[span(theirs, k, r), :] = low[r:]
        grad = right_dot(low, w_out[...]).astype(bf16)
        d_context[span(mine, k, r), :] = grad[:r]
        d_context[span(theirs, k, r), :] = grad[r:]
        d_attn_copy(k).wait_send()

    def out_block(j):
        own_out[span(0, j, 128), :] = dot(context[:, span(0, j, 128)].T, d_attn[...])

    def rope_back(grad, cos_rows, sin_rows):
        first, second = grad[:, : HD // 2], grad[:, HD // 2 :]
        return jnp.concatenate([first * cos_rows + second * sin_rows, second * cos_rows - first * sin_rows], axis=-1)

    def head_back(grad, gain, row, column, part, rows):
        raw = raws[part][rows, :]
        back = rope_back(grad, cosine[part][rows, :], sine[part][rows, :])
        scale = rms_scale(raw)
        share = jnp.sum(back * (raw * scale), axis=0, keepdims=True)
        gain_hops[0, row : row + 1, column : column + HD] = gain_hops[0, row : row + 1, column : column + HD] + share
        ge = gain[...] * back
        return (scale * ge - raw * (scale * scale * scale) * jnp.mean(ge * raw, axis=-1, keepdims=True)).astype(bf16)

    def add_rows(target, stop, value):
        low = min(stop, half)
        target[0][:low, :] = target[0][:low, :] + value[:low]
        if stop > half:
            target[1][: stop - half, :] = target[1][: stop - half, :] + value[half:]

    def attention_block(i, size):
        start, stop = i * size, (i + 1) * size
        part, inside = start // half, slice(start % half, start % half + size)
        rows = slice(start, stop)
        qi, ki, vi, dc = queries[rows, :], keys[:stop, :], values[:stop, :], d_context[rows, :]
        scores = right_dot(qi, ki) * score_scale
        row_at = start + lax.broadcasted_iota(jnp.int32, (size, stop), 0)
        key_at = lax.broadcasted_iota(jnp.int32, (size, stop), 1)
        allowed = (columns_in[rows, 1:2] == seg_row[:, :stop]) & (key_at <= row_at)
        probs = jnp.exp(jnp.where(allowed, scores, masked_value) - columns_in[rows, 0:1])
        d_probs = right_dot(dc, vi)
        inner = jnp.sum(probs * d_probs, axis=-1, keepdims=True)
        d_scores = (probs * (d_probs - inner)).astype(bf16)
        d_query = dot(d_scores, ki) * score_scale
        d_raw[rows, :HD] = head_back(d_query, gain_query, 4, 0, part, inside)
        add_rows(d_keys, stop, turn_dot(d_scores, qi) * score_scale)
        add_rows(d_values, stop, turn_dot(probs.astype(bf16), dc))

    def raw_block(i, size):
        start = i * size
        part, inside = start // half, slice(start % half, start % half + size)
        rows = slice(start, start + size)
        d_raw[rows, HD : 2 * HD] = head_back(d_keys[part][inside, :], gain_key, 4, HD, part, inside)
        d_raw[rows, 2 * HD :] = d_values[part][inside, :].astype(bf16)

    def in_block(k):
        low = jnp.concatenate([d_raw[span(mine, k, r), :], d_raw[span(theirs, k, r), :]], axis=0)
        part = (
            dot(low[:, :HD], w_query[...]) + dot(low[:, HD : 2 * HD], w_key[...]) + dot(low[:, 2 * HD :], w_value[...])
        )
        two.give(k, part[r:])
        mine_stage[lax.rem(k, 2)] = part[:r]

    def weight_block(j):
        grad = dot(d_raw[:, span(0, j, 128)].T, normed[...])

        @pl.when(j < HD // 128)
        def _():
            own_query[span(0, j, 128), :] = grad

        @pl.when(j >= HD // 128)
        def _():
            own_kv[span(0, j - HD // 128, 128), :] = grad

    def in_second(k):
        d_in = two.total(k)
        rows = hidden[q(k), :].astype(f32)
        scale = rms_scale(rows)
        add_gain(3, jnp.sum(d_in * (rows * scale), axis=0, keepdims=True))
        ge = d_in * gain_in[...]
        back = scale * ge - rows * (scale * scale * scale) * jnp.mean(ge * rows, axis=-1, keepdims=True)
        b2[q(k), :] = a1[q(k), :] + back
        begin(hidden_copies(k))

    kv_mine = at.core * HD
    kv_part = HD // 2
    kv_give = send_to(own_kv.at[span(0, 1 - at.core, HD)], kv_core, kv_sems.at[0], kv_sems.at[1], at.dp, at.sibling)
    kv_cross = send_to(
        kv_core.at[span(0, 1 - x_at, kv_part)], kv_far, kv_sems.at[2], kv_sems.at[3], at.dp, at.far
    )
    quarter = key_value_out.at[span(kv_mine, x_at, kv_part)]
    far_quarter = key_value_out.at[span(kv_mine, 1 - x_at, kv_part)]
    kv_whole = key_value_out.at[span(0, at.core, HD)]
    kv_other = key_value_out.at[span(0, 1 - at.core, HD)]
    kv_back = send_to(quarter, quarter, kv_sems.at[4], kv_sems.at[5], at.dp, at.far)
    kv_return = send_to(kv_whole, kv_whole, kv_sems.at[6], kv_sems.at[7], at.dp, at.sibling)

    def kv_add_core():
        kv_give.wait_recv()
        kv_core[...] = kv_core[...] + own_kv[span(0, at.core, HD), :]
        kv_cross.start()

    def kv_add_far():
        kv_cross.wait_recv()
        kv_far[...] = kv_far[...] + kv_core[span(0, x_at, kv_part), :]
        stream.start(part_kv)

    def kv_collect():
        stream.collect(part_kv)
        copies = [
            pltpu.make_async_copy(
                key_value_part.at[i],
                key_value_out.at[span(kv_mine + x_at * kv_part, i, kv_part // 2)],
                kv_sems.at[8 + i],
            )
            for i in range(2)
        ]
        begin(copies)
        sent(copies)
        kv_back.start()

    def kv_send_back():
        send_to(far_quarter, far_quarter, kv_sems.at[4], kv_sems.at[5], at.dp, at.far).wait_recv()
        kv_return.start()

    hops = [(at.dp, at.sibling), (at.dp, at.far), (at.pair, at.mp)]

    def slot_copy(src, dst, i, dp, mp):
        return send_to(gain_hops.at[src], gain_hops.at[dst], gain_send.at[i], gain_arrive.at[i], dp, mp)

    def hop_copy(i):
        return slot_copy(0 if i == 0 else 6 + i, i + 1, i, *hops[i])

    gain_to_mid = slot_copy(9, 4, 3, at.chain, at.mp)
    gain_over = slot_copy(10, 5, 4, at.across, at.mp)
    gain_to_end = slot_copy(11, 11, 5, at.chain, at.mp)
    gain_keep = pltpu.make_async_copy(gain_hops.at[11], gains_out, gains_sem)

    def gain_start():
        keep_x = jnp.where(lax.broadcasted_iota(jnp.int32, (8, width), 0) < 4, 0.5, 1.0)
        gain_hops[0] = gain_hops[0] * keep_x
        hop_copy(0).start()

    def gain_hop(i):
        hop_copy(i).wait_recv()
        gain_hops[7 + i] = gain_hops[0 if i == 0 else 6 + i] + gain_hops[i + 1]
        if i < 2:
            hop_copy(i + 1).start()
        else:
            pl.when(at.end)(lambda: gain_to_mid.start())

    def gain_mid():
        @pl.when(at.mid)
        def _():
            gain_to_mid.wait_recv()
            gain_hops[10] = gain_hops[9] + gain_hops[4]
            gain_over.start()

    def gain_total():
        @pl.when(at.mid)
        def _():
            gain_over.wait_recv()
            gain_hops[11] = gain_hops[10] + gain_hops[5]
            gain_to_end.start()

    def gain_end():
        pl.when(at.end)(lambda: gain_to_end.wait_recv())
        gain_keep.start()

    def at_step(t, when, *bodies):
        @pl.when(t == when)
        def _():
            for body in bodies:
                body()

    def start_all(copies):
        return lambda: begin(copies)

    def wait_all(copies):
        return lambda: sent(copies)

    def clear():
        for ref in d_keys + d_values:
            ref[...] = jnp.zeros(ref.shape, f32)

    def alternate(t, first, body):
        k = t - first

        @pl.when((k >= 0) & (k < 2 * n) & (lax.rem(k, 2) == 0))
        def _():
            body(k // 2)

    size = wide
    blocks = rows_all // size
    t_attn = 2 * n + 2
    t_raw = t_attn + 2 + blocks
    t_in = t_raw + 4
    t_done = t_in + 3 * HD // 128
    t_gain = t_in + 4 + 2 * n
    t_kv = part_kv.begin + part_kv.count + Stream.keep + 1

    def step(t, _):
        stream.step(t)
        at_step(t, 0, start_all(early))
        alternate(t, 1, pair_backward)
        alternate(t, 2, second3)
        alternate(t, 3, take_attn)
        at_step(t, t_attn, start_all(rope_copies), clear)
        within(t - t_attn, 2, out_block)
        at_step(t, t_attn + 2, lambda: stream.start(part_out), wait_all(rope_copies), wait_all(early))
        for i in range(blocks):
            at_step(t, t_attn + 2 + i, functools.partial(attention_block, i, size))
        at_step(t, t_raw, start_all(key_copies), wait_all(key_copies))
        for i in range(4):
            at_step(t, t_raw + i, functools.partial(raw_block, i, rows_all // 4))
        within(t - t_in, n, in_block)
        within(t - t_in - 1, n, first2)
        within(t - t_in, 3 * HD // 128, weight_block)
        at_step(t, t_done, lambda: stream.start(part_query), lambda: kv_give.start())
        at_step(t, t_done + 1, kv_add_core)
        at_step(t, t_done + 6, kv_add_far)
        alternate(t, t_in + 4, in_second)
        at_step(t, t_gain, gain_start)
        for i in range(3):
            at_step(t, t_gain + 2 + 2 * i, functools.partial(gain_hop, i))
        at_step(t, t_gain + 8, gain_mid)
        at_step(t, t_gain + 10, gain_total)
        at_step(t, t_gain + 12, gain_end)
        at_step(t, t_kv, kv_collect)
        at_step(t, t_kv + 6, kv_send_back)

        @pl.when(t == down_count - 2)
        def _():
            turned_copy(n - 1, rows_all).wait()
            mid_load.start()
            chosen_copy(0).start()

        return 0

    lax.fori_loop(0, stream.steps, step, 0)
    for section in (down, chosen_one, chosen_two, part_out, part_query):
        stream.collect(section)
    for section in (part_kv, part_out, part_query):
        stream.finish_start(section)
    two.drain()

    def settle(k, _):
        sent(hidden_copies(k))
        o = span(mine, k, r)
        send_to(mid_pair.at[o], mid_pair.at[o], fwd1.at[0, k], fwd1.at[1, k], at.dp, at.sibling).wait_send()
        send_to(d_mlp_pair.at[o], d_mlp_pair.at[o], fwd2.at[0, k], fwd2.at[1, k], at.dp, at.sibling).wait_send()
        return 0

    lax.fori_loop(0, n, settle, 0)
    wait_bytes(a1, out_in)
    wait_bytes(a1, hidden_in)
    kv_give.wait_send()
    kv_cross.wait_send()
    kv_back.wait_send()
    for i in range(3):
        hop_copy(i).wait_send()
    pl.when(at.end)(lambda: gain_to_mid.wait_send())

    @pl.when(at.mid)
    def _():
        gain_over.wait_send()
        gain_to_end.wait_send()

    gain_keep.wait()
    kv_return.wait_send()
    send_to(kv_other, kv_other, kv_sems.at[6], kv_sems.at[7], at.dp, at.sibling).wait_recv()


def layer_call(collective_id, small, large, r, chunk, per, slots, held):
    hidden = large[0]
    w_down = large[4]
    rows, width = hidden.shape
    units = w_down.shape[0]
    half = rows // 2
    n = half // r
    f32, bf16 = jnp.float32, jnp.bfloat16
    regular = pltpu.SemaphoreType.REGULAR

    def vm(*shape, dtype=f32):
        return pltpu.VMEM(shape, dtype)

    scratch = [vm(half, width)] * 6
    scratch += [vm(2, r, width), vm(2, r, width), vm(2, 2 * r, width)]
    scratch += [vm(2, 2 * r, width, dtype=bf16), vm(units, 2 * r, dtype=bf16), vm(12, 8, width)]
    scratch += [vm(half, width, dtype=bf16)] * 2
    scratch += [vm(units, width, dtype=bf16)] * 3
    scratch += [vm(2 * rows, width, dtype=bf16)] + [vm(rows, units, dtype=bf16)] * 3
    scratch += [vm(units // 2, 2 * rows, dtype=bf16)]
    scratch += [vm(slots * chunk, width)] * 2 + [vm(per * chunk, width), vm(2, per * chunk, 2 * rows, dtype=bf16)]
    scratch += [vm(HD // 2, width), vm(HD // 2, width), vm(HD // 4, width), vm(HD // 2, width)]
    for _ in range(3):
        scratch += [DMA((2,)), DMA((n,)), DMA((n,)), DMA((n,))]
    scratch += [DMA((5,))] + [DMA((n,))] * 5 + [DMA((2, n)), DMA((2, n))]
    scratch += [DMA((2, n)), DMA((4, n)), DMA((n,)), DMA((2, n)), DMA((2, 2)), DMA((2,)), DMA, DMA, DMA]
    scratch += [DMA((16,)), DMA((2,)), DMA((10,)), DMA((6,)), DMA((6,)), DMA]
    scratch += [DMA((6, slots)), regular, regular, regular, DMA((6,))]
    scratch += [DMA((2, HD // 2 // chunk)), DMA((2, HD // 2 // chunk)), DMA((2, HD // 4 // chunk))]
    shape = jax.ShapeDtypeStruct
    outs = [
        shape((rows, width), f32),
        shape((rows, width), f32),
        shape((2, units // 2, width), f32),
        shape((2, units, width), f32),
        shape((2, HD // 2, width), f32),
        shape((2, HD // 2, width), f32),
        shape((2, HD // 4, width), f32),
        shape((2 * HD, width), f32),
        shape((8, width), f32),
        shape((2 * rows, width), bf16),
        shape((units, 2 * rows), bf16),
        shape((rows, width), f32),
        shape((rows, width), f32),
    ]
    return pl.pallas_call(
        functools.partial(layer_kernel, n, r, chunk, held),
        out_shape=outs,
        in_specs=[vmem_spec()] * len(small) + [any_spec()] * len(large),
        out_specs=[any_spec()] * len(outs),
        scratch_shapes=scratch,
        compiler_params=comm_params(collective_id, 63),
        name="layer",
    )(*small, *large)


def rms_norm(values, gain_vec):
    return values * lax.rsqrt(jnp.mean(values * values, axis=-1, keepdims=True) + epsilon) * gain_vec


def gelu_tanh(values):
    return 0.5 * values * (1.0 + jnp.tanh(gelu_coeff * (values + 0.044715 * values * values * values)))


def rotate(values, cosine, sine_table):
    half_dim = values.shape[-1] // 2
    first_half = values[..., :half_dim]
    second_half = values[..., half_dim:]
    return jnp.concatenate(
        [first_half * cosine - second_half * sine_table, second_half * cosine + first_half * sine_table], axis=-1
    )


def rope_tables(segment_row):
    row_count = segment_row.shape[0]
    earlier = jnp.sum((segment_row[None, :] < segment_row[:, None]).astype(jnp.int32), axis=1)
    position = jnp.arange(row_count, dtype=jnp.int32) - earlier
    exponent = jnp.arange(HD // 2, dtype=jnp.float32) * (2.0 / HD)
    frequency = rope_base ** (-exponent)
    angles = position.astype(jnp.float32)[:, None] * frequency[None, :]
    return (jnp.cos(angles), jnp.sin(angles))


def matmul(left, right):
    return jnp.dot(left, right, preferred_element_type=jnp.float32)


def left_dot(left, right):
    return lax.dot_general(left, right, (((0,), (0,)), ((), ())), preferred_element_type=jnp.float32)

def per_device(
    rest_groups,
    hidden,
    segment_ids,
    w_query,
    w_key,
    w_value,
    w_out,
    w_gate,
    w_up,
    w_down,
    gain_in,
    gain_post_attn,
    gain_pre_ffn,
    gain_post_ffn,
    gain_query,
    gain_key,
    cotangent,
):
    row_total, width = hidden.shape
    head_local = w_query.shape[1] // HD
    y = lax.rem(lax.axis_index("dp"), 2)
    segment_row = segment_ids[0]
    cosine, sine_table = rope_tables(segment_row)
    hidden_full = hidden.astype(jnp.float32)
    normed_full, norm_in_back = jax.vjp(rms_norm, hidden_full, gain_in)
    normed_in = normed_full.astype(jnp.bfloat16)
    query_raw = matmul(normed_in, w_query)
    key_raw = matmul(normed_in, w_key)
    value_raw = matmul(normed_in, w_value)

    def query_path(raw_rows, gain_vec):
        shaped = raw_rows.reshape(row_total, head_local, HD)
        return rotate(rms_norm(shaped, gain_vec), cosine[:, None, :], sine_table[:, None, :])

    def key_path(raw_rows, gain_vec):
        return rotate(rms_norm(raw_rows, gain_vec), cosine, sine_table)

    query_rot, query_back = jax.vjp(query_path, query_raw, gain_query)
    key_rot, key_back = jax.vjp(key_path, key_raw, gain_key)
    queries = query_rot.astype(jnp.bfloat16)
    key_rows = key_rot.astype(jnp.bfloat16)
    value_rows = value_raw.astype(jnp.bfloat16)
    positions_all = jnp.arange(row_total, dtype=jnp.int32)
    block_count = row_total // BLOCK

    def block_scores(block_index):
        start = block_index * BLOCK
        stop = start + BLOCK
        raw_scores = (
            jnp.einsum("rhd,kd->hrk", queries[start:stop], key_rows[:stop], preferred_element_type=jnp.float32)
            * score_scale
        )
        allowed = (segment_row[start:stop, None] == segment_row[None, :stop]) & (
            positions_all[None, :stop] <= positions_all[start:stop, None]
        )
        return (jnp.where(allowed[None], raw_scores, masked_value), start, stop)

    context_blocks = []
    log_totals = []
    for block_index in range(block_count):
        scores, start, stop = block_scores(block_index)
        peak = jnp.max(scores, axis=-1, keepdims=True)
        expo_scores = jnp.exp(scores - peak)
        row_totals = jnp.sum(expo_scores, axis=-1, keepdims=True)
        probs = expo_scores / row_totals
        log_totals.append(peak + jnp.log(row_totals))
        context_blocks.append(
            jnp.einsum(
                "hrk,kd->rhd", probs.astype(jnp.bfloat16), value_rows[:stop], preferred_element_type=jnp.float32
            )
        )
    context = jnp.concatenate(context_blocks, axis=0).reshape(row_total, head_local * HD).astype(jnp.bfloat16)
    units = w_down.shape[0]
    (output, grad_hidden, grad_down, grad_chosen, grad_out_w, grad_query, _, grad_kv, gains, *_) = layer_call(
        1,
        (
            context,
            w_out,
            jnp.concatenate([jnp.concatenate(log_totals, axis=1)[0], segment_row[:, None].astype(jnp.float32)], axis=1),
            segment_row[None, :].astype(jnp.float32),
            gain_in[None],
            gain_post_attn[None],
            gain_pre_ffn[None],
            gain_post_ffn[None],
            gain_query[None],
            gain_key[None],
        ),
        (
            hidden,
            cotangent,
            w_gate.T,
            w_up.T,
            w_down,
            normed_in,
            queries.reshape(row_total, HD),
            key_rows,
            value_rows,
            query_raw,
            key_raw,
            cosine,
            sine_table,
            w_query.T,
            w_key.T,
            w_value.T,
        ),
        64,
        32,
        3,
        18,
        10,
    )
    output = output.astype(jnp.bfloat16)
    grad_hidden = grad_hidden.astype(jnp.bfloat16)
    gains = [gains[3], gains[0], gains[1], gains[2], gains[4, :HD], gains[4, HD : 2 * HD]]
    grads = [
        grad_query.reshape(head_local * HD, width).T,
        grad_kv[:HD].T,
        grad_kv[HD:].T,
        grad_out_w.reshape(head_local * HD, width),
        grad_chosen[0].T,
        grad_chosen[1].T,
        grad_down.reshape(units, width),
    ] + gains
    if rest_groups is not None:
        grads = [lax.psum(grad, "dp", axis_index_groups=rest_groups) for grad in grads]
    return (output, grad_hidden, *grads)


def solution(mesh):
    dp_size = mesh.shape["dp"]
    span_size = LINE * PAIR
    rest_groups = None
    if dp_size > span_size:
        rest_groups = [list(range(i, dp_size, span_size)) for i in range(span_size)]
    rows, columns, whole = P("dp", None), P(None, "mp"), P()
    in_specs = (rows, rows, columns, whole, whole, P("mp", None), columns, columns, P("mp", None)) + (whole,) * 6 + (rows,)
    out_specs = (rows, rows, columns, whole, whole, P("mp", None), columns, columns, P("mp", None)) + (whole,) * 6
    return jax.shard_map(
        functools.partial(per_device, rest_groups), mesh=mesh, in_specs=in_specs, out_specs=out_specs, check_vma=False
    )
```

time: 699 us -> 562 us (0.80); the launches traced: 691 us -> 562 us
  Pallas kernels: 538 us -> 495 us
  matrix products: 39.8 us -> 6.45 us
  local copies, waits for them, and re-layouts: 66.7 us -> 35 us
  other arithmetic: 44.3 us -> 24.3 us
    pallas_call x3 -> x1, Pallas kernels: 538 us -> 495 us  [layer_call(): pl.pallas_call(functools.partial(layer_kernel, n, r, chunk, held), out_sh...]
    dot_general x16 -> x0, matrix products: 30.7 us -> none  [the longest x4 19.5 us: left_dot(): lax.dot_general(left, right, (((0,), (0,)), ((), ())), preferred_element_...]
    unnamed x98 -> x61, local copies, waits for them, and re-layouts: 44.8 us -> 14.5 us
    squeeze x1 -> x0, local copies, waits for them, and re-layouts: 11.5 us -> none  [per_device(): grad_chosen[1]]
    transpose x0 -> x2, local copies, waits for them, and re-layouts: none -> 11.5 us  [the longest x1 11.3 us: per_device(): grad_chosen[1]]
    reduce_sum x4 -> x0, other arithmetic: 11 us -> none  [rms_norm(): values * lax.rsqrt(jnp.mean(values * values, axis=-1, keepdims=True) + ep...]
where the time goes in v4:
time: 562 us
  Pallas kernels  495 us (88%)
  local copies, waits for them, and re-layouts  35 us (6%)
  other arithmetic  24.3 us (4%)
  matrix products  6.45 us (1%)
    pallas_call x1, Pallas kernels, layer_call(): pl.pallas_call(functools.partial(layer_kernel, n, r, chunk, held), out_sh...  495 us
    unnamed x61, local copies, waits for them, and re-layouts  14.5 us
    transpose x1, local copies, waits for them, and re-layouts, per_device(): grad_chosen[1]  11.3 us

profile of v4, /device:TPU:0, one launch (start us, length us, event | category | flops | bytes accessed | tf_op | source)
XLA Modules:
  0.0 561.6 jit_solution(1481957291716119440)
XLA Ops:
  1.2 1.3 convert_reduce_fusion
  2.6 2.3 fusion
  4.8 0.6 add_rsqrt_fusion.2
  6.0 0.6 fusion.33
  6.6 0.6 broadcast_in_dim.22.gain_post_attn
  7.8 0.6 broadcast_in_dim.25.gain_post_ffn
  9.0 0.6 fusion.32
  9.6 1.1 copy.87
  10.7 1.1 copy.88
  11.8 1.1 copy.89
  12.8 2.3 fusion.2.normed_all
  15.1 1.6 convolution_convert_fusion.values_all
  16.8 1.9 multiply_reduce_fusion.1
  18.6 1.6 copy.83.key_raw_all
  20.5 3.1 subtract_convert_fusion
  23.6 0.9 multiply_reduce_fusion
  25.2 2.4 fusion.16
  29.0 1.2 pad_maximum_fusion
  30.1 0.6 fusion.34
  31.2 0.6 fusion.8
  31.9 0.8 maximum_bitcast_fusion.context
  32.7 1.0 copy.90.columns_in
  33.7 494.8 %layer.1 = (f32[1024,1152]{1,0:T(8,128)}, f32[1024,1152]{1,0:T(8,128)}, f32[2,864,1152]{2,1,0:T(8,128)}, f32[2,1728,1152]{2,1,0:T(8,128)}, f32[2,128,1152]{2,1,0...) custom-call(bf16[1024,256]{1,0:T(8,128)(2,1)} %maximum_bitcast_fusio, ...), custom_call_target="tpu_custom_call" | custom-call | tf_op jit(solution)/shard_map/layer/pallas_call | solution.py:1135
  528.5 4.1 convert_element_type.70
  533.2 0.6 slice_reduce_fusion
  533.8 1.4 copy.93
  535.2 4.1 convert_element_type.71
  539.5 1.4 copy.95
  540.9 1.4 copy.94
  542.3 11.3 %slice_bitcast_fusion = (f32[1152,1728]{0,1:T(8,128)}, f32[1152,1728]{0,1:T(8,128)}) fusion(f32[2,1728,1152]{2,1,0:T(8,128)} %get-tuple-element.28), kind=kLoop, calls=%fused_computation | loop fusion | bytes 31850496 | tf_op jit(solution)/shard_map/transpose | solution.py:1301
  553.6 1.0 copy.100
  554.6 7.0 %copy.101 = f32[1728,1152]{1,0:T(8,128)} copy(f32[1728,1152]{1,0:T(8,128)} %bitcast.81) | data formatting | bytes 15925248
  (78 shorter events, 5.7 us)
Async XLA Ops:
  0.6 5.4 copy-start.13
  0.7 7.8 %copy-start.14 = (f32[1152]{0:T(1024)S(1)}, f32[1152]{0:T(1024)}, u32[]{:S(2)}) copy-start(f32[1152]{0:T(1024)} %param.25) | copy-start | bytes 13828
  0.7 10.0 %copy-start.3 = (bf16[1152,256]{1,0:T(8,128)(2,1)S(1)}, bf16[1152,256]{1,0:T(8,128)(2,1)}, u32[]{:S(2)}) copy-start(bf16[1152,256]{1,0:T(8,128)(2,1)} %param.19) | copy-start | bytes 1769476
  0.7 9.0 %copy-start.4 = (bf16[1152,256]{1,0:T(8,128)(2,1)S(1)}, bf16[1152,256]{1,0:T(8,128)(2,1)}, u32[]{:S(2)}) copy-start(bf16[1152,256]{1,0:T(8,128)(2,1)} %param.18) | copy-start | bytes 1769476
  0.7 7.2 %copy-start.20 = (f32[1152]{0:T(1024)S(1)}, f32[1152]{0:T(1024)}, u32[]{:S(2)}) copy-start(f32[1152]{0:T(1024)} %param.28) | copy-start | bytes 13828
  0.7 6.5 %copy-start.19 = (f32[1152]{0:T(1024)S(1)}, f32[1152]{0:T(1024)}, u32[]{:S(2)}) copy-start(f32[1152]{0:T(1024)} %param.27) | copy-start | bytes 13828
  0.7 5.9 %copy-start.18 = (f32[1152]{0:T(1024)S(1)}, f32[1152]{0:T(1024)}, u32[]{:S(2)}) copy-start(f32[1152]{0:T(1024)} %param.26) | copy-start | bytes 13828
  2.6 9.2 %copy-start.11 = (bf16[1152,256]{1,0:T(8,128)(2,1)S(1)}, bf16[1152,256]{1,0:T(8,128)(2,1)}, u32[]{:S(2)}) copy-start(bf16[1152,256]{1,0:T(8,128)(2,1)} %param.20) | copy-start | bytes 1769476
  6.0 6.8 %copy-start.17 = (s32[1024]{0:T(1024)}, s32[1024]{0:T(1024)S(1)}, u32[]{:S(2)}) copy-start(s32[1024]{0:T(1024)S(1)} %iota.23) | copy-start | bytes 12292
  15.1 8.5 %copy-start = (bf16[1024,1152]{1,0:T(8,128)(2,1)}, bf16[1024,1152]{1,0:T(8,128)(2,1)S(1)}, u32[]{:S(2)}) copy-start(bf16[1024,1152]{1,0:T(8,128)(2,1)S(1)} %fusion.2.normed_all) | copy-start | bytes 7077892
  16.8 3.4 copy-start.22
  18.6 1.8 copy-start.26
  20.2 3.4 copy-start.1
  20.2 3.4 copy-start.5
  23.6 1.3 copy-start.21
  24.9 3.1 copy-start.2
  24.9 2.6 copy-start.9
  24.9 2.6 copy-start.10
  24.9 2.6 slice-start
  25.0 2.6 copy-start.25
  27.5 1.0 copy-start.12
  28.6 1.6 copy-start.23
  28.6 1.6 copy-start.24
  31.1 0.7 copy-start.15
  528.5 4.1 copy-start.16
  528.5 5.3 copy-start.8
  535.2 4.1 copy-start.6
  542.3 11.3 %copy-start.7 = (f32[2,128,1152]{2,1,0:T(8,128)S(1)}, f32[2,128,1152]{2,1,0:T(8,128)}, u32[]{:S(2)}) copy-start(f32[2,128,1152]{2,1,0:T(8,128)} %get-tuple-element.27) | copy-start | bytes 3538948

commit v5 on v4

--- a/solution.py
+++ b/solution.py
@@ -92,19 +92,20 @@
 
 
 class Section:
-    def __init__(self, count, out, base, arrived, group=1, make=None, own=None, r0=None, r0s=None, sent=None):
-        self.count, self.out, self.base, self.arrived = count, out, base, arrived
+    def __init__(self, count, out, base, arrived, left, group=1, make=None, own=None, r0=None, r0s=None, sent=None, both=None):
+        self.count, self.out, self.base, self.arrived, self.left = count, out, base, arrived, left
         self.group, self.make = group, make
         self.own, self.r0, self.r0s, self.sent = own, r0, r0s, sent
+        self.both = both
         self.begin = 0
 
 
 class Stream:
-    lag_mid, lag_end, keep = 2, 5, 12
+    lag_mid, lag_end, keep = 2, 5, 9
 
     def __init__(self, at, r, r1, r2, group, sems, credits, sections):
         self.at, self.r, self.r1, self.r2, self.group = at, r, r1, r2, group
-        self.r1s, self.r2s, self.s1, self.s2, self.ys, self.ls = sems
+        self.r1s, self.r2s, self.s1, self.s2, self.ls = sems
         self.end_free, self.over_free, self.back_free = credits
         self.sections = sections
         self.slots = r1.shape[0] // r
@@ -125,15 +126,8 @@
             k = t - section.begin
             pl.when((k >= 0) & (k < section.count))(functools.partial(body, section, k))
 
-    def start(self, section):
-        at = self.at
-        theirs = (1 - at.y) * section.count * self.r
-
-        def give(k, _):
-            self.gift(section, k, theirs).start()
-            return 0
-
-        lax.fori_loop(0, section.count, give, 0)
+    def give(self, section, k):
+        self.gift(section, k, (1 - self.at.y) * section.count * self.r).start()
 
     def gift(self, section, k, theirs):
         return send_to(
@@ -186,18 +180,22 @@
             self.r2.at[q], self.r2.at[q], self.s2.at[slot], self.r2s.at[slot], self.at.chain, self.at.mp
         )
 
-    def total_copies(self, section, k, t):
-        q, slot = self.rows(t), self.slot(t)
-        o = section.out.at[self.at.y, span(section.base, k, self.r)]
-        return (
-            send_to(self.r2.at[q], o, self.ys.at[slot], section.arrived, self.at.pair, self.at.mp),
-            pltpu.make_async_copy(self.r2.at[q], o, self.ls.at[slot]),
-        )
+    def place(self, section, k):
+        part = lax.rem(self.at.y + (section.both or 0), 2)
+        return section.out.at[part, span(section.base, k, self.r)]
+
+    def keep_copy(self, section, k, t):
+        return pltpu.make_async_copy(self.r2.at[self.rows(t)], self.place(section, k), self.ls.at[self.slot(t)])
 
     def give_total(self, t):
+        self.each(t, lambda section, k: self.keep_copy(section, k, t).start())
+
+    def forward(self, t):
         def body(section, k):
-            for copy in self.total_copies(section, k, t):
-                copy.start()
+            self.keep_copy(section, k, t).wait()
+            if section.both is None:
+                o = self.place(section, k)
+                send_to(o, o, section.left, section.arrived, self.at.pair, self.at.mp).start()
 
         self.each(t, body)
 
@@ -234,10 +232,7 @@
     def release(self, t):
         at = self.at
         again = t < self.n - self.slots
-        to_pair, kept = self.total_copies(self.sections[0], 0, t)
         self.to_mid(t).wait_send()
-        to_pair.wait_send()
-        kept.wait()
 
         @pl.when(at.mid)
         def _():
@@ -260,15 +255,19 @@
         def _():
             within(t, self.n, self.first)
             within(t - self.lag_mid, self.n, self.second)
+            within(t - self.lag_mid - 1, self.n, self.forward)
 
         @pl.when(self.at.end)
         def _():
             within(t, self.n, self.outer)
             within(t - self.lag_end, self.n, self.last)
+            within(t - self.lag_end - 1, self.n, self.forward)
 
     def collect(self, section):
         other = section.out.at[1 - self.at.y, pl.ds(section.base, section.count * self.r)]
-        send_to(other, other, self.ys.at[0], section.arrived, self.at.pair, self.at.mp).wait_recv()
+        whole = send_to(other, other, section.left, section.arrived, self.at.pair, self.at.mp)
+        whole.wait_recv()
+        whole.wait_send()
 
     def finish_start(self, section):
         for k in range(section.count):
@@ -332,6 +331,7 @@
     r,
     chunk,
     held,
+    shared,
     context,
     w_out,
     columns_in,
@@ -392,6 +392,7 @@
     slope,
     gelu,
     chosen,
+    other,
     act_t,
     r1,
     r2,
@@ -400,6 +401,7 @@
     r0_out,
     r0_query,
     r0_kv,
+    kv_core,
     kv_far,
     given1,
     taken1,
@@ -441,6 +443,7 @@
     credit_over,
     credit_back,
     arrived_sems,
+    left_sems,
     out_sems,
     query_sems,
     kv_pair_sems,
@@ -454,6 +457,7 @@
     bf16, f32 = jnp.bfloat16, jnp.float32
     sel_gate = at.y == 0
     x_at = at.mp // 2
+    lanes = other.shape[1]
     wide = 2 * r
 
     def q(k):
@@ -592,9 +596,10 @@
     def turned_copy(k, base):
         return pltpu.make_async_copy(turned_stage, chosen_out.at[:, pairq(k, base)], turned_sem)
 
-    def keep_chosen(x, k, base):
+    def keep_chosen(x, rest, k, base):
         pl.when((k >= 1) | (base > 0))(lambda: turned_copy(k, base).wait())
-        turned_stage[...] = x.T
+        turned_stage[:units, :] = x.T
+        turned_stage[units:, :] = rest.T[: shared * chunk]
         turned_copy(k, base).start()
 
     def forward_block(k):
@@ -635,6 +640,7 @@
         keep_mid(x, k, rows_all)
         act, sl, ge = gated(x)
         chosen[pairq(k), :] = jnp.where(sel_gate, sl, ge).astype(bf16)
+        other[pairq(k), :] = jnp.where(sel_gate, ge[:, :lanes], sl[:, :lanes]).astype(bf16)
         keep_act(act, pairq(k, rows_all))
 
     def second2(k):
@@ -658,7 +664,7 @@
         d_act = right_dot(x, w_down[...])
         d_gate = (d_act * slope[pairq(k), :].astype(f32)).astype(bf16)
         d_up = (d_act * gelu[pairq(k), :].astype(f32)).astype(bf16)
-        keep_chosen(jnp.where(sel_gate, d_gate, d_up), k, 0)
+        keep_chosen(jnp.where(sel_gate, d_gate, d_up), jnp.where(sel_gate, d_up[:, :lanes], d_gate[:, :lanes]), k, 0)
         part = dot(d_gate, w_gate[...]) + dot(d_up, w_up[...])
         three.give(k, part[r:])
         mine_stage[lax.rem(k, 2)] = part[:r]
@@ -688,7 +694,8 @@
 
     def pair_backward(k):
         d_act = right_dot(d_mlp[pairq(k, rows_all), :], w_down[...])
-        keep_chosen((d_act * chosen[pairq(k), :].astype(f32)).astype(bf16), k, rows_all)
+        rest = (d_act[:, :lanes] * other[pairq(k), :].astype(f32)).astype(bf16)
+        keep_chosen((d_act * chosen[pairq(k), :].astype(f32)).astype(bf16), rest, k, rows_all)
 
     far_lag = n + 1
 
@@ -705,14 +712,14 @@
             two.drain()
 
         within(t - far_lag, n, second2)
+        within(t - far_lag - 1, n, backward_block)
         within(t - far_lag - 1, n, forward2)
-        within(t - far_lag - 1, n, backward_block)
         within(t - far_lag - 2, n, first3)
-        within(t - far_lag - 3, n, load2)
-        within(t - far_lag - 4, n, take_pair)
+        within(t - far_lag - 2, n, load2)
+        within(t - far_lag - 3, n, take_pair)
         return 0
 
-    lax.fori_loop(0, far_lag + 4 + n, tick, 0)
+    lax.fori_loop(0, far_lag + 3 + n, tick, 0)
     three.drain()
     mid_copy(n - 1, 0).wait()
     mid_copy(n - 1, rows_all).wait()
@@ -735,7 +742,6 @@
     raws = halves(l1, 2 * HD, HD)
     d_keys, d_values = halves(b1, 0, HD), halves(b1, 2 * HD, HD)
     own_out = b3.at[pl.ds(0, HD)]
-    kv_core = b3.at[pl.ds(HD, HD)]
     own_query = l1.at[pl.ds(0, HD)]
     own_kv = b1
 
@@ -759,43 +765,59 @@
     key_copies = half_copies(key_raw_all, raws, 13)
     mid_load = pltpu.make_async_copy(mid_low, d_mlp, late_sems.at[15])
 
-    def chosen_copy(g):
-        slot = lax.rem(g, 2)
-        rows = chosen_load.shape[1]
-        return pltpu.make_async_copy(chosen_out.at[span(0, g, rows)], chosen_load.at[slot], chosen_sems.at[slot])
-
-    groups = units // chosen_load.shape[1]
-
-    def make_chosen(first, g):
-        @pl.when(first + g == 0)
+    per = group.shape[0] // chunk
+    ahead = shared // per
+    groups = units // group.shape[0] + ahead
+    first, middle = held
+
+    def group_of(p):
+        turn = ahead + first
+        return jnp.where(p < turn, p, jnp.where(p < turn + ahead, p - turn + groups - ahead, p - ahead))
+
+    def chosen_copy(p):
+        slot = lax.rem(p, 2)
+        rows = chosen_out.at[span(0, group_of(p), group.shape[0])]
+        return pltpu.make_async_copy(rows, chosen_load.at[slot], chosen_sems.at[slot])
+
+    def make_chosen(at_group, g):
+        @pl.when(at_group + g == 0)
         def _():
             mid_load.wait()
 
-        chosen_copy(first + g).wait()
-        pl.when(first + g + 1 < groups)(lambda: chosen_copy(first + g + 1).start())
-        return dot(chosen_load[lax.rem(first + g, 2)], d_mlp[...])
+        p = at_group + g
+        chosen_copy(p).wait()
+        pl.when(p + 1 < groups)(lambda: chosen_copy(p + 1).start())
+        return dot(chosen_load[lax.rem(p, 2)], d_mlp[...])
 
     def make_down(g):
         return dot(act_t[span(0, g, group.shape[0]), :], d_mlp[...])
 
-    per = group.shape[0] // chunk
     down_count = units // 2 // chunk
-    chosen_count = units // chunk
-    head = held * per
-    down = Section(down_count, down_out, 0, arrived_sems.at[0], per, make_down)
-    chosen_one = Section(head, chosen_grad, 0, arrived_sems.at[1], per, functools.partial(make_chosen, 0))
-    chosen_two = Section(
-        chosen_count - head,
-        chosen_grad,
-        head * chunk,
-        arrived_sems.at[2],
-        per,
-        functools.partial(make_chosen, held),
-    )
+    down = Section(down_count, down_out, 0, arrived_sems.at[0], left_sems.at[0], per, make_down)
+
+    def chosen_part(i, at_group, count, base, both=None):
+        sems = (None, None) if both is not None else (arrived_sems.at[i], left_sems.at[i])
+        make = functools.partial(make_chosen, at_group)
+        return Section(count * per, chosen_grad, base * chunk, *sems, per, make, both=both)
+
+    both_one = chosen_part(None, 0, ahead, 0, 0)
+    chosen_one = chosen_part(1, ahead, first, shared)
+    both_two = chosen_part(None, ahead + first, ahead, 0, 1)
+    chosen_mid = chosen_part(2, 2 * ahead + first, middle, shared + first * per)
+    done = first + middle
+    chosen_two = chosen_part(6, 2 * ahead + done, groups - 2 * ahead - done, shared + done * per)
 
     def presum(out, i, own, r0, sems):
         return Section(
-            r0.shape[0] // chunk, out, 0, arrived_sems.at[i], own=own, r0=r0, r0s=sems.at[0], sent=sems.at[1]
+            r0.shape[0] // chunk,
+            out,
+            0,
+            arrived_sems.at[i],
+            left_sems.at[i],
+            own=own,
+            r0=r0,
+            r0s=sems.at[0],
+            sent=sems.at[1],
         )
 
     part_kv = presum(key_value_part, 3, kv_far, r0_kv, kv_pair_sems)
@@ -807,9 +829,9 @@
         r1,
         r2,
         group,
-        tuple(ring_sems.at[i] for i in range(6)),
+        tuple(ring_sems.at[i] for i in range(5)),
         (credit_end, credit_over, credit_back),
-        [down, chosen_one, part_kv, part_out, part_query, chosen_two],
+        [down, both_one, chosen_one, both_two, chosen_mid, part_kv, part_out, part_query, chosen_two],
     )
 
     def take_attn(k):
@@ -877,7 +899,8 @@
         two.give(k, part[r:])
         mine_stage[lax.rem(k, 2)] = part[:r]
 
-    def weight_block(j):
+    def weight_block(i):
+        j = lax.rem(i + HD // 128, 3 * HD // 128)
         grad = dot(d_raw[:, span(0, j, 128)].T, normed[...])
 
         @pl.when(j < HD // 128)
@@ -919,7 +942,6 @@
     def kv_add_far():
         kv_cross.wait_recv()
         kv_far[...] = kv_far[...] + kv_core[span(0, x_at, kv_part), :]
-        stream.start(part_kv)
 
     def kv_collect():
         stream.collect(part_kv)
@@ -1010,9 +1032,10 @@
     blocks = rows_all // size
     t_attn = 2 * n + 2
     t_raw = t_attn + 2 + blocks
-    t_in = t_raw + 4
-    t_done = t_in + 3 * HD // 128
-    t_gain = t_in + 4 + 2 * n
+    t_weight = t_raw + 4
+    t_kv_give = t_weight + 2 * HD // 128
+    t_in = t_kv_give + 2
+    t_gain = t_in + 8 + 2 * n
     t_kv = part_kv.begin + part_kv.count + Stream.keep + 1
 
     def step(t, _):
@@ -1023,7 +1046,10 @@
         alternate(t, 3, take_attn)
         at_step(t, t_attn, start_all(rope_copies), clear)
         within(t - t_attn, 2, out_block)
-        at_step(t, t_attn + 2, lambda: stream.start(part_out), wait_all(rope_copies), wait_all(early))
+        at_step(t, t_attn + 2, wait_all(rope_copies), wait_all(early))
+        within(t - both_one.begin, part_out.count, functools.partial(stream.give, part_out))
+        within(t - both_two.begin, part_kv.count, functools.partial(stream.give, part_kv))
+        within(t - both_two.begin - part_kv.count, part_query.count, functools.partial(stream.give, part_query))
         for i in range(blocks):
             at_step(t, t_attn + 2 + i, functools.partial(attention_block, i, size))
         at_step(t, t_raw, start_all(key_copies), wait_all(key_copies))
@@ -1031,11 +1057,11 @@
             at_step(t, t_raw + i, functools.partial(raw_block, i, rows_all // 4))
         within(t - t_in, n, in_block)
         within(t - t_in - 1, n, first2)
-        within(t - t_in, 3 * HD // 128, weight_block)
-        at_step(t, t_done, lambda: stream.start(part_query), lambda: kv_give.start())
-        at_step(t, t_done + 1, kv_add_core)
-        at_step(t, t_done + 6, kv_add_far)
-        alternate(t, t_in + 4, in_second)
+        at_step(t, t_kv_give, lambda: kv_give.start())
+        at_step(t, t_kv_give + 1, kv_add_core)
+        within(t - t_weight, 3 * HD // 128, weight_block)
+        at_step(t, t_kv_give + 7, kv_add_far)
+        alternate(t, t_in + 8, in_second)
         at_step(t, t_gain, gain_start)
         for i in range(3):
             at_step(t, t_gain + 2 + 2 * i, functools.partial(gain_hop, i))
@@ -1054,7 +1080,7 @@
         return 0
 
     lax.fori_loop(0, stream.steps, step, 0)
-    for section in (down, chosen_one, chosen_two, part_out, part_query):
+    for section in (down, chosen_one, chosen_mid, chosen_two, part_out, part_query):
         stream.collect(section)
     for section in (part_kv, part_out, part_query):
         stream.finish_start(section)
@@ -1087,7 +1113,7 @@
     send_to(kv_other, kv_other, kv_sems.at[6], kv_sems.at[7], at.dp, at.sibling).wait_recv()
 
 
-def layer_call(collective_id, small, large, r, chunk, per, slots, held):
+def layer_call(collective_id, small, large, r, chunk, per, slots, held, shared):
     hidden = large[0]
     w_down = large[4]
     rows, width = hidden.shape
@@ -1102,19 +1128,20 @@
 
     scratch = [vm(half, width)] * 6
     scratch += [vm(2, r, width), vm(2, r, width), vm(2, 2 * r, width)]
-    scratch += [vm(2, 2 * r, width, dtype=bf16), vm(units, 2 * r, dtype=bf16), vm(12, 8, width)]
+    scratch += [vm(2, 2 * r, width, dtype=bf16), vm(units + shared * chunk, 2 * r, dtype=bf16), vm(12, 8, width)]
     scratch += [vm(half, width, dtype=bf16)] * 2
     scratch += [vm(units, width, dtype=bf16)] * 3
     scratch += [vm(2 * rows, width, dtype=bf16)] + [vm(rows, units, dtype=bf16)] * 3
+    scratch += [vm(rows, -(-shared * chunk // 128) * 128, dtype=bf16)]
     scratch += [vm(units // 2, 2 * rows, dtype=bf16)]
     scratch += [vm(slots * chunk, width)] * 2 + [vm(per * chunk, width), vm(2, per * chunk, 2 * rows, dtype=bf16)]
-    scratch += [vm(HD // 2, width), vm(HD // 2, width), vm(HD // 4, width), vm(HD // 2, width)]
+    scratch += [vm(HD // 2, width), vm(HD // 2, width), vm(HD // 4, width), vm(HD, width), vm(HD // 2, width)]
     for _ in range(3):
         scratch += [DMA((2,)), DMA((n,)), DMA((n,)), DMA((n,))]
     scratch += [DMA((5,))] + [DMA((n,))] * 5 + [DMA((2, n)), DMA((2, n))]
     scratch += [DMA((2, n)), DMA((4, n)), DMA((n,)), DMA((2, n)), DMA((2, 2)), DMA((2,)), DMA, DMA, DMA]
     scratch += [DMA((16,)), DMA((2,)), DMA((10,)), DMA((6,)), DMA((6,)), DMA]
-    scratch += [DMA((6, slots)), regular, regular, regular, DMA((6,))]
+    scratch += [DMA((5, slots)), regular, regular, regular, DMA((7,)), DMA((7,))]
     scratch += [DMA((2, HD // 2 // chunk)), DMA((2, HD // 2 // chunk)), DMA((2, HD // 4 // chunk))]
     shape = jax.ShapeDtypeStruct
     outs = [
@@ -1128,12 +1155,12 @@
         shape((2 * HD, width), f32),
         shape((8, width), f32),
         shape((2 * rows, width), bf16),
-        shape((units, 2 * rows), bf16),
+        shape((units + shared * chunk, 2 * rows), bf16),
         shape((rows, width), f32),
         shape((rows, width), f32),
     ]
     return pl.pallas_call(
-        functools.partial(layer_kernel, n, r, chunk, held),
+        functools.partial(layer_kernel, n, r, chunk, held, shared),
         out_shape=outs,
         in_specs=[vmem_spec()] * len(small) + [any_spec()] * len(large),
         out_specs=[any_spec()] * len(outs),
@@ -1286,8 +1313,9 @@
         64,
         32,
         3,
-        18,
-        10,
+        16,
+        (4, 3),
+        6,
     )
     output = output.astype(jnp.bfloat16)
     grad_hidden = grad_hidden.astype(jnp.bfloat16)

time: 562 us -> 551 us (0.980)
  Pallas kernels: 495 us -> 484 us
    pallas_call x1, Pallas kernels: 495 us -> 484 us  [layer_call(): pl.pallas_call(functools.partial(layer_kernel, n, r, chunk, held, shared)...]
where the time goes in v5:
time: 551 us
  Pallas kernels  484 us (88%)
  local copies, waits for them, and re-layouts  35 us (6%)
  other arithmetic  24.3 us (4%)
  matrix products  6.45 us (1%)
    pallas_call x1, Pallas kernels, layer_call(): pl.pallas_call(functools.partial(layer_kernel, n, r, chunk, held, shared)...  484 us
    unnamed x61, local copies, waits for them, and re-layouts  14.5 us
    transpose x1, local copies, waits for them, and re-layouts, per_device(): grad_chosen[1]  11.3 us

profile of v5, /device:TPU:0, one launch (start us, length us, event | category | flops | bytes accessed | tf_op | source)
XLA Modules:
  0.0 551.0 jit_solution(415123341886790626)
XLA Ops:
  1.2 1.3 convert_reduce_fusion
  2.6 2.3 fusion
  4.8 0.6 add_rsqrt_fusion.2
  6.0 0.6 fusion.33
  6.6 0.6 broadcast_in_dim.22.gain_post_attn
  7.2 0.6 broadcast_in_dim.23.gain_pre_ffn
  9.0 0.6 fusion.32
  9.7 1.1 copy.87
  10.7 1.1 copy.88
  11.8 1.1 copy.89
  12.8 2.3 fusion.2.normed_all
  15.1 1.6 convolution_convert_fusion.values_all
  16.8 1.9 multiply_reduce_fusion.1
  18.6 1.6 copy.83.key_raw_all
  20.5 3.2 subtract_convert_fusion
  23.6 0.9 multiply_reduce_fusion
  25.2 2.4 fusion.16
  29.0 1.1 pad_maximum_fusion
  30.1 0.6 fusion.34
  31.1 0.6 fusion.8
  31.8 0.8 maximum_bitcast_fusion.context
  32.6 1.0 copy.90.columns_in
  33.7 484.2 %layer.1 = (f32[1024,1152]{1,0:T(8,128)}, f32[1024,1152]{1,0:T(8,128)}, f32[2,864,1152]{2,1,0:T(8,128)}, f32[2,1728,1152]{2,1,0:T(8,128)}, f32[2,128,1152]{2,1,0...) custom-call(bf16[1024,256]{1,0:T(8,128)(2,1)} %maximum_bitcast_fusio, ...), custom_call_target="tpu_custom_call" | custom-call | tf_op jit(solution)/shard_map/layer/pallas_call | solution.py:1162
  517.9 4.1 convert_element_type.70
  522.5 0.6 slice_reduce_fusion
  523.2 1.4 copy.93
  524.6 4.1 convert_element_type.71
  528.9 1.4 copy.95
  530.3 1.4 copy.94
  531.6 11.3 %slice_bitcast_fusion = (f32[1152,1728]{0,1:T(8,128)}, f32[1152,1728]{0,1:T(8,128)}) fusion(f32[2,1728,1152]{2,1,0:T(8,128)} %get-tuple-element.28), kind=kLoop, calls=%fused_computation | loop fusion | bytes 31850496 | tf_op jit(solution)/shard_map/transpose | solution.py:1329
  542.9 1.0 copy.100
  544.0 7.0 %copy.101 = f32[1728,1152]{1,0:T(8,128)} copy(f32[1728,1152]{1,0:T(8,128)} %bitcast.81) | data formatting | bytes 15925248
  (78 shorter events, 5.7 us)
Async XLA Ops:
  0.6 5.4 copy-start.13
  0.7 7.8 %copy-start.14 = (f32[1152]{0:T(1024)S(1)}, f32[1152]{0:T(1024)}, u32[]{:S(2)}) copy-start(f32[1152]{0:T(1024)} %param.25) | copy-start | bytes 13828
  0.7 10.1 %copy-start.3 = (bf16[1152,256]{1,0:T(8,128)(2,1)S(1)}, bf16[1152,256]{1,0:T(8,128)(2,1)}, u32[]{:S(2)}) copy-start(bf16[1152,256]{1,0:T(8,128)(2,1)} %param.19) | copy-start | bytes 1769476
  0.7 9.0 %copy-start.4 = (bf16[1152,256]{1,0:T(8,128)(2,1)S(1)}, bf16[1152,256]{1,0:T(8,128)(2,1)}, u32[]{:S(2)}) copy-start(bf16[1152,256]{1,0:T(8,128)(2,1)} %param.18) | copy-start | bytes 1769476
  0.7 7.2 %copy-start.20 = (f32[1152]{0:T(1024)S(1)}, f32[1152]{0:T(1024)}, u32[]{:S(2)}) copy-start(f32[1152]{0:T(1024)} %param.28) | copy-start | bytes 13828
  0.7 6.5 %copy-start.19 = (f32[1152]{0:T(1024)S(1)}, f32[1152]{0:T(1024)}, u32[]{:S(2)}) copy-start(f32[1152]{0:T(1024)} %param.27) | copy-start | bytes 13828
  0.7 5.9 %copy-start.18 = (f32[1152]{0:T(1024)S(1)}, f32[1152]{0:T(1024)}, u32[]{:S(2)}) copy-start(f32[1152]{0:T(1024)} %param.26) | copy-start | bytes 13828
  2.6 9.2 %copy-start.11 = (bf16[1152,256]{1,0:T(8,128)(2,1)S(1)}, bf16[1152,256]{1,0:T(8,128)(2,1)}, u32[]{:S(2)}) copy-start(bf16[1152,256]{1,0:T(8,128)(2,1)} %param.20) | copy-start | bytes 1769476
  6.0 6.8 %copy-start.17 = (s32[1024]{0:T(1024)}, s32[1024]{0:T(1024)S(1)}, u32[]{:S(2)}) copy-start(s32[1024]{0:T(1024)S(1)} %iota.23) | copy-start | bytes 12292
  15.1 8.5 %copy-start = (bf16[1024,1152]{1,0:T(8,128)(2,1)}, bf16[1024,1152]{1,0:T(8,128)(2,1)S(1)}, u32[]{:S(2)}) copy-start(bf16[1024,1152]{1,0:T(8,128)(2,1)S(1)} %fusion.2.normed_all) | copy-start | bytes 7077892
  16.8 3.4 copy-start.22
  18.6 1.8 copy-start.26
  20.2 3.4 copy-start.1
  20.2 3.4 copy-start.5
  23.6 1.3 copy-start.21
  24.9 3.1 copy-start.2
  24.9 2.6 copy-start.9
  24.9 2.6 copy-start.10
  25.0 2.6 slice-start
  25.0 2.6 copy-start.25
  27.6 1.0 copy-start.12
  28.6 1.5 copy-start.23
  28.6 1.5 copy-start.24
  31.1 0.7 copy-start.15
  517.9 4.1 copy-start.16
  517.9 5.3 copy-start.8
  524.6 4.1 copy-start.6
  531.6 11.3 %copy-start.7 = (f32[2,128,1152]{2,1,0:T(8,128)S(1)}, f32[2,128,1152]{2,1,0:T(8,128)}, u32[]{:S(2)}) copy-start(f32[2,128,1152]{2,1,0:T(8,128)} %get-tuple-element.27) | copy-start | bytes 3538948

commit v6 on v5

--- a/solution.py
+++ b/solution.py
@@ -332,27 +332,14 @@
     chunk,
     held,
     shared,
-    context,
     w_out,
-    columns_in,
     seg_row,
-    gain_in,
-    gain_post_attn,
-    gain_pre_ffn,
-    gain_post_ffn,
-    gain_query,
-    gain_key,
+    gains_in,
     hidden_all,
     cotangent_all,
     w_gate_all,
     w_up_all,
     w_down_all,
-    normed_all,
-    queries_all,
-    keys_all,
-    values_all,
-    query_raw_all,
-    key_raw_all,
     cosine_all,
     sine_all,
     w_query_all,
@@ -371,6 +358,9 @@
     chosen_out,
     mid_pair,
     d_mlp_pair,
+    normed_keep,
+    qkv_keep,
+    context,
     a1,
     b1,
     a2,
@@ -466,6 +456,26 @@
     def pairq(k, base=0):
         return span(base, k, 2 * r)
 
+    gain_in, gain_post_attn, gain_pre_ffn, gain_post_ffn = [gains_in.at[pl.ds(i, 1)] for i in range(4)]
+    gain_query, gain_key = [gains_in.at[pl.ds(4, 1), pl.ds(i * HD, HD)] for i in range(2)]
+
+    def halves(ref, base, cols):
+        return [ref.at[:, pl.ds(base + i * cols, cols)] for i in range(2)]
+
+    def half_copies(src, dst, first):
+        return [
+            pltpu.make_async_copy(src.at[pl.ds(i * half, half)], dst[i], late_sems.at[first + i]) for i in range(2)
+        ]
+
+    def weight_copies(dst, first):
+        return [
+            pltpu.make_async_copy(src, dst.at[:, pl.ds(i * HD, HD)], late_sems.at[first + i])
+            for i, src in enumerate((w_query_all, w_key_all, w_value_all))
+        ]
+
+    cosine, sine = halves(l1, 0, HD // 2), halves(l1, HD, HD // 2)
+    rope_copies = half_copies(cosine_all, cosine, 7) + half_copies(sine_all, sine, 9)
+
     fetch = [
         (hidden_all.at[span(0, at.core, half)], hidden),
         (w_gate_all, w_gate),
@@ -474,8 +484,62 @@
         (cotangent_all.at[span(0, at.core, half)], cotangent),
     ]
     fetch = [pltpu.make_async_copy(src, dst, in_sems.at[i]) for i, (src, dst) in enumerate(fetch)]
-    for copy in fetch:
+    normed_rows = slope.at[:, pl.ds(0, width)]
+    qkv = gelu.at[:, pl.ds(0, 3 * HD)]
+    w_start = d_mlp.at[pl.ds(0, width), pl.ds(0, 3 * HD)]
+    ready = [pltpu.make_async_copy(hidden_all, normed_rows, late_sems.at[0])] + weight_copies(w_start, 1) + rope_copies
+    for copy in ready + fetch:
         copy.start()
+    for copy in ready:
+        copy.wait()
+
+    def rope(raw, gain, cos_rows, sin_rows):
+        turned = raw * rms_scale(raw) * gain[...]
+        first, second = turned[:, : HD // 2], turned[:, HD // 2 :]
+        return jnp.concatenate([first * cos_rows - second * sin_rows, second * cos_rows + first * sin_rows], axis=-1)
+
+    def project(part, k):
+        rows, inside = span(part * half, k, wide), span(0, k, wide)
+        start = normed_rows[rows, :].astype(f32)
+        low = (start * rms_scale(start) * gain_in[...]).astype(bf16)
+        normed_rows[rows, :] = low
+        raw = dot(low, w_start[...])
+        cos_rows, sin_rows = cosine[part][inside, :], sine[part][inside, :]
+        qkv[rows, :HD] = rope(raw[:, :HD], gain_query, cos_rows, sin_rows).astype(bf16)
+        qkv[rows, HD : 2 * HD] = rope(raw[:, HD : 2 * HD], gain_key, cos_rows, sin_rows).astype(bf16)
+        qkv[rows, 2 * HD :] = raw[:, 2 * HD :].astype(bf16)
+
+    for part in range(2):
+
+        def project_rows(k, _, part=part):
+            project(part, k)
+            return 0
+
+        lax.fori_loop(0, half // wide, project_rows, 0)
+    keep_copies = [
+        pltpu.make_async_copy(normed_rows, normed_keep, late_sems.at[4]),
+        pltpu.make_async_copy(qkv, qkv_keep, late_sems.at[5]),
+    ]
+    for copy in keep_copies:
+        copy.start()
+
+    def softmax_block(query_rows, key_rows, start, size):
+        stop = start + size
+        scores = right_dot(query_rows, key_rows) * score_scale
+        row_at = start + lax.broadcasted_iota(jnp.int32, (size, stop), 0)
+        key_at = lax.broadcasted_iota(jnp.int32, (size, stop), 1)
+        segments = seg_row[...].astype(f32)
+        own = jnp.broadcast_to(segments[:, start:stop], (size, size)).T[:, 0:1]
+        allowed = (own == segments[:, :stop]) & (key_at <= row_at)
+        scores = jnp.where(allowed, scores, masked_value)
+        powers = jnp.exp(scores - jnp.max(scores, axis=-1, keepdims=True))
+        return powers / jnp.sum(powers, axis=-1, keepdims=True)
+
+    for start in range(0, rows_all, wide):
+        rows = slice(start, start + wide)
+        probs = softmax_block(qkv[rows, :HD], qkv[: start + wide, HD : 2 * HD], start, wide)
+        context[rows, :] = dot(probs.astype(bf16), qkv[: start + wide, 2 * HD :]).astype(bf16)
+
     greet(
         [
             (None, at.dp, at.sibling),
@@ -500,7 +564,7 @@
     lax.fori_loop(0, n, give1, 0)
     lax.fori_loop(0, n, first1, 0)
     one.drain()
-    for copy in fetch:
+    for copy in fetch + keep_copies:
         copy.wait()
 
     gain_hops[0] = jnp.zeros(gain_hops.shape[1:], f32)
@@ -725,44 +789,21 @@
     mid_copy(n - 1, rows_all).wait()
 
     normed = w_gate.at[pl.ds(0, rows_all)]
-    w_query = w_gate.at[pl.ds(rows_all, HD)]
-    w_key = w_gate.at[pl.ds(rows_all + HD, HD)]
+    w_qkv = w_down.at[pl.ds(0, width), pl.ds(0, 3 * HD)]
     d_attn = w_up.at[pl.ds(0, rows_all)]
-    w_value = w_up.at[pl.ds(rows_all, HD)]
-    queries = slope.at[:, pl.ds(0, HD)]
-    keys = slope.at[:, pl.ds(HD, HD)]
-    values = slope.at[:, pl.ds(2 * HD, HD)]
+    qkv = slope.at[:, pl.ds(0, 3 * HD)]
+    queries, keys, values = [slope.at[:, pl.ds(i * HD, HD)] for i in range(3)]
     d_context = slope.at[:, pl.ds(3 * HD, HD)]
     d_raw = gelu.at[:, pl.ds(0, 3 * HD)]
 
-    def halves(ref, base, cols):
-        return [ref.at[:, pl.ds(base + i * cols, cols)] for i in range(2)]
-
-    cosine, sine = halves(l1, 0, HD // 2), halves(l1, HD, HD // 2)
-    raws = halves(l1, 2 * HD, HD)
     d_keys, d_values = halves(b1, 0, HD), halves(b1, 2 * HD, HD)
     own_out = b3.at[pl.ds(0, HD)]
     own_query = l1.at[pl.ds(0, HD)]
     own_kv = b1
 
-    def half_copies(src, dst, first):
-        return [
-            pltpu.make_async_copy(src.at[pl.ds(i * half, half)], dst[i], late_sems.at[first + i]) for i in range(2)
-        ]
-
-    early = [
-        (normed_all, normed),
-        (w_query_all, w_query),
-        (w_key_all, w_key),
-        (w_value_all, w_value),
-        (queries_all, queries),
-        (keys_all, keys),
-        (values_all, values),
-    ]
+    early = [(normed_keep, normed), (qkv_keep, qkv)]
     early = [pltpu.make_async_copy(src, dst, late_sems.at[i]) for i, (src, dst) in enumerate(early)]
-    rope_copies = half_copies(cosine_all, cosine, 7) + half_copies(sine_all, sine, 9)
-    rope_copies += half_copies(query_raw_all, raws, 11)
-    key_copies = half_copies(key_raw_all, raws, 13)
+    weights = weight_copies(w_qkv, 2)
     mid_load = pltpu.make_async_copy(mid_low, d_mlp, late_sems.at[15])
 
     per = group.shape[0] // chunk
@@ -851,8 +892,7 @@
         first, second = grad[:, : HD // 2], grad[:, HD // 2 :]
         return jnp.concatenate([first * cos_rows + second * sin_rows, second * cos_rows - first * sin_rows], axis=-1)
 
-    def head_back(grad, gain, row, column, part, rows):
-        raw = raws[part][rows, :]
+    def head_back(grad, raw, gain, row, column, part, rows):
         back = rope_back(grad, cosine[part][rows, :], sine[part][rows, :])
         scale = rms_scale(raw)
         share = jnp.sum(back * (raw * scale), axis=0, keepdims=True)
@@ -871,16 +911,13 @@
         part, inside = start // half, slice(start % half, start % half + size)
         rows = slice(start, stop)
         qi, ki, vi, dc = queries[rows, :], keys[:stop, :], values[:stop, :], d_context[rows, :]
-        scores = right_dot(qi, ki) * score_scale
-        row_at = start + lax.broadcasted_iota(jnp.int32, (size, stop), 0)
-        key_at = lax.broadcasted_iota(jnp.int32, (size, stop), 1)
-        allowed = (columns_in[rows, 1:2] == seg_row[:, :stop]) & (key_at <= row_at)
-        probs = jnp.exp(jnp.where(allowed, scores, masked_value) - columns_in[rows, 0:1])
+        probs = softmax_block(qi, ki, start, size)
         d_probs = right_dot(dc, vi)
         inner = jnp.sum(probs * d_probs, axis=-1, keepdims=True)
         d_scores = (probs * (d_probs - inner)).astype(bf16)
         d_query = dot(d_scores, ki) * score_scale
-        d_raw[rows, :HD] = head_back(d_query, gain_query, 4, 0, part, inside)
+        raw = dot(normed[rows, :], w_qkv[:, :HD])
+        d_raw[rows, :HD] = head_back(d_query, raw, gain_query, 4, 0, part, inside)
         add_rows(d_keys, stop, turn_dot(d_scores, qi) * score_scale)
         add_rows(d_values, stop, turn_dot(probs.astype(bf16), dc))
 
@@ -888,14 +925,13 @@
         start = i * size
         part, inside = start // half, slice(start % half, start % half + size)
         rows = slice(start, start + size)
-        d_raw[rows, HD : 2 * HD] = head_back(d_keys[part][inside, :], gain_key, 4, HD, part, inside)
+        raw = dot(normed[rows, :], w_qkv[:, HD : 2 * HD])
+        d_raw[rows, HD : 2 * HD] = head_back(d_keys[part][inside, :], raw, gain_key, 4, HD, part, inside)
         d_raw[rows, 2 * HD :] = d_values[part][inside, :].astype(bf16)
 
     def in_block(k):
         low = jnp.concatenate([d_raw[span(mine, k, r), :], d_raw[span(theirs, k, r), :]], axis=0)
-        part = (
-            dot(low[:, :HD], w_query[...]) + dot(low[:, HD : 2 * HD], w_key[...]) + dot(low[:, 2 * HD :], w_value[...])
-        )
+        part = right_dot(low, w_qkv[...])
         two.give(k, part[r:])
         mine_stage[lax.rem(k, 2)] = part[:r]
 
@@ -1044,15 +1080,14 @@
         alternate(t, 1, pair_backward)
         alternate(t, 2, second3)
         alternate(t, 3, take_attn)
-        at_step(t, t_attn, start_all(rope_copies), clear)
+        at_step(t, t_attn, start_all(rope_copies + weights), clear)
         within(t - t_attn, 2, out_block)
-        at_step(t, t_attn + 2, wait_all(rope_copies), wait_all(early))
+        at_step(t, t_attn + 2, wait_all(rope_copies + weights), wait_all(early))
         within(t - both_one.begin, part_out.count, functools.partial(stream.give, part_out))
         within(t - both_two.begin, part_kv.count, functools.partial(stream.give, part_kv))
         within(t - both_two.begin - part_kv.count, part_query.count, functools.partial(stream.give, part_query))
         for i in range(blocks):
             at_step(t, t_attn + 2 + i, functools.partial(attention_block, i, size))
-        at_step(t, t_raw, start_all(key_copies), wait_all(key_copies))
         for i in range(4):
             at_step(t, t_raw + i, functools.partial(raw_block, i, rows_all // 4))
         within(t - t_in, n, in_block)
@@ -1126,7 +1161,7 @@
     def vm(*shape, dtype=f32):
         return pltpu.VMEM(shape, dtype)
 
-    scratch = [vm(half, width)] * 6
+    scratch = [vm(rows, HD, dtype=bf16)] + [vm(half, width)] * 6
     scratch += [vm(2, r, width), vm(2, r, width), vm(2, 2 * r, width)]
     scratch += [vm(2, 2 * r, width, dtype=bf16), vm(units + shared * chunk, 2 * r, dtype=bf16), vm(12, 8, width)]
     scratch += [vm(half, width, dtype=bf16)] * 2
@@ -1158,6 +1193,8 @@
         shape((units + shared * chunk, 2 * rows), bf16),
         shape((rows, width), f32),
         shape((rows, width), f32),
+        shape((rows, width), bf16),
+        shape((rows, 3 * HD), bf16),
     ]
     return pl.pallas_call(
         functools.partial(layer_kernel, n, r, chunk, held, shared),
@@ -1225,90 +1262,28 @@
 ):
     row_total, width = hidden.shape
     head_local = w_query.shape[1] // HD
-    y = lax.rem(lax.axis_index("dp"), 2)
+    units = w_down.shape[0]
     segment_row = segment_ids[0]
     cosine, sine_table = rope_tables(segment_row)
-    hidden_full = hidden.astype(jnp.float32)
-    normed_full, norm_in_back = jax.vjp(rms_norm, hidden_full, gain_in)
-    normed_in = normed_full.astype(jnp.bfloat16)
-    query_raw = matmul(normed_in, w_query)
-    key_raw = matmul(normed_in, w_key)
-    value_raw = matmul(normed_in, w_value)
-
-    def query_path(raw_rows, gain_vec):
-        shaped = raw_rows.reshape(row_total, head_local, HD)
-        return rotate(rms_norm(shaped, gain_vec), cosine[:, None, :], sine_table[:, None, :])
-
-    def key_path(raw_rows, gain_vec):
-        return rotate(rms_norm(raw_rows, gain_vec), cosine, sine_table)
-
-    query_rot, query_back = jax.vjp(query_path, query_raw, gain_query)
-    key_rot, key_back = jax.vjp(key_path, key_raw, gain_key)
-    queries = query_rot.astype(jnp.bfloat16)
-    key_rows = key_rot.astype(jnp.bfloat16)
-    value_rows = value_raw.astype(jnp.bfloat16)
-    positions_all = jnp.arange(row_total, dtype=jnp.int32)
-    block_count = row_total // BLOCK
-
-    def block_scores(block_index):
-        start = block_index * BLOCK
-        stop = start + BLOCK
-        raw_scores = (
-            jnp.einsum("rhd,kd->hrk", queries[start:stop], key_rows[:stop], preferred_element_type=jnp.float32)
-            * score_scale
-        )
-        allowed = (segment_row[start:stop, None] == segment_row[None, :stop]) & (
-            positions_all[None, :stop] <= positions_all[start:stop, None]
-        )
-        return (jnp.where(allowed[None], raw_scores, masked_value), start, stop)
-
-    context_blocks = []
-    log_totals = []
-    for block_index in range(block_count):
-        scores, start, stop = block_scores(block_index)
-        peak = jnp.max(scores, axis=-1, keepdims=True)
-        expo_scores = jnp.exp(scores - peak)
-        row_totals = jnp.sum(expo_scores, axis=-1, keepdims=True)
-        probs = expo_scores / row_totals
-        log_totals.append(peak + jnp.log(row_totals))
-        context_blocks.append(
-            jnp.einsum(
-                "hrk,kd->rhd", probs.astype(jnp.bfloat16), value_rows[:stop], preferred_element_type=jnp.float32
-            )
-        )
-    context = jnp.concatenate(context_blocks, axis=0).reshape(row_total, head_local * HD).astype(jnp.bfloat16)
-    units = w_down.shape[0]
+    head_gains = jnp.concatenate([gain_query, gain_key, jnp.zeros(width - 2 * HD, jnp.float32)])
+    gains = jnp.zeros((8, width), jnp.float32)
+    row = lax.broadcasted_iota(jnp.int32, gains.shape, 0)
+    for i, gain in enumerate((gain_in, gain_post_attn, gain_pre_ffn, gain_post_ffn, head_gains)):
+        gains = jnp.where(row == i, gain[None, :], gains)
     (output, grad_hidden, grad_down, grad_chosen, grad_out_w, grad_query, _, grad_kv, gains, *_) = layer_call(
         1,
-        (
-            context,
-            w_out,
-            jnp.concatenate([jnp.concatenate(log_totals, axis=1)[0], segment_row[:, None].astype(jnp.float32)], axis=1),
-            segment_row[None, :].astype(jnp.float32),
-            gain_in[None],
-            gain_post_attn[None],
-            gain_pre_ffn[None],
-            gain_post_ffn[None],
-            gain_query[None],
-            gain_key[None],
-        ),
+        (w_out, segment_ids, gains),
         (
             hidden,
             cotangent,
             w_gate.T,
             w_up.T,
             w_down,
-            normed_in,
-            queries.reshape(row_total, HD),
-            key_rows,
-            value_rows,
-            query_raw,
-            key_raw,
             cosine,
             sine_table,
-            w_query.T,
-            w_key.T,
-            w_value.T,
+            w_query,
+            w_key,
+            w_value,
         ),
         64,
         32,

time: 551 us -> 540 us (0.980)
  Pallas kernels: 484 us -> 499 us
  local copies, waits for them, and re-layouts: 35 us -> 24.9 us
  other arithmetic: 24.3 us -> 14.7 us
  matrix products: 6.45 us -> 0 us
    pallas_call x1, Pallas kernels: 484 us -> 499 us  [layer_call(): pl.pallas_call(functools.partial(layer_kernel, n, r, chunk, held, shared)...]
    dot_general x7 -> x0, matrix products: 6.45 us -> none  [the longest x3 4.41 us: matmul(): return jnp.dot(left, right, preferred_element_type=jnp.float32)]
    another operation x2 -> x0, other arithmetic: 5.51 us -> none
    unnamed x61 -> x12, local copies, waits for them, and re-layouts: 14.5 us -> 10.8 us
where the time goes in v6:
time: 540 us
  Pallas kernels  499 us (92%)
  local copies, waits for them, and re-layouts  24.9 us (5%)
  other arithmetic  14.7 us (3%)
    pallas_call x1, Pallas kernels, layer_call(): pl.pallas_call(functools.partial(layer_kernel, n, r, chunk, held, shared)...  499 us
    transpose x1, local copies, waits for them, and re-layouts, per_device(): grad_chosen[1]  11.3 us
    unnamed x12, local copies, waits for them, and re-layouts  10.8 us

profile of v6, /device:TPU:0, one launch (start us, length us, event | category | flops | bytes accessed | tf_op | source)
XLA Modules:
  0.0 539.8 jit_solution(12468029216192636147)
XLA Ops:
  0.7 1.3 convert_reduce_fusion
  2.0 0.7 pad_maximum_fusion
  2.7 1.4 select_select_fusion.gains_in
  4.2 3.0 multiply_sine_fusion
  7.2 499.5 %layer.1 = (f32[1024,1152]{1,0:T(8,128)}, f32[1024,1152]{1,0:T(8,128)}, f32[2,864,1152]{2,1,0:T(8,128)}, f32[2,1728,1152]{2,1,0:T(8,128)}, f32[2,128,1152]{2,1,0...) custom-call(bf16[256,1152]{1,0:T(8,128)(2,1)} %w_out.1, ...), custom_call_target="tpu_custom_call" | custom-call | tf_op jit(solution)/shard_map/layer/pallas_call | solution.py:1199
  506.7 0.0 copy-start.3
  506.7 0.0 copy-start.2
  506.7 4.1 convert_element_type.18
  510.8 0.0 copy-done.3
  510.8 0.6 fusion
  511.3 0.6 slice_reduce_fusion
  512.0 0.0 copy-done.2
  512.0 1.4 copy.34
  513.4 0.0 copy-start
  513.4 4.1 convert_element_type.19
  517.5 0.0 copy-done
  517.5 0.2 slice_bitcast_fusion.2
  517.7 1.4 copy.36
  519.1 1.4 copy.35
  520.4 0.0 copy-start.1
  520.4 11.3 %slice_bitcast_fusion = (f32[1152,1728]{0,1:T(8,128)}, f32[1152,1728]{0,1:T(8,128)}) fusion(f32[2,1728,1152]{2,1,0:T(8,128)} %get-tuple-element.28), kind=kLoop, calls=%fused_computation | loop fusion | bytes 31850496 | tf_op jit(solution)/shard_map/transpose | solution.py:1304
  531.7 0.0 copy-done.1
  531.7 1.0 copy.39
  532.8 7.0 %copy.40 = f32[1728,1152]{1,0:T(8,128)} copy(f32[1728,1152]{1,0:T(8,128)} %bitcast.21) | data formatting | bytes 15925248
  (6 shorter events, 0.0 us)
Async XLA Ops:
  506.7 4.1 copy-start.3
  506.7 5.3 copy-start.2
  513.4 4.1 copy-start
  520.4 11.3 %copy-start.1 = (f32[2,128,1152]{2,1,0:T(8,128)S(1)}, f32[2,128,1152]{2,1,0:T(8,128)}, u32[]{:S(2)}) copy-start(f32[2,128,1152]{2,1,0:T(8,128)} %get-tuple-element.27) | copy-start | bytes 3538948

commit v7 on v6

--- a/solution.py
+++ b/solution.py
@@ -101,7 +101,7 @@
 
 
 class Stream:
-    lag_mid, lag_end, keep = 2, 5, 9
+    lag_mid, lag_end, keep = 2, 6, 9
 
     def __init__(self, at, r, r1, r2, group, sems, credits, sections):
         self.at, self.r, self.r1, self.r2, self.group = at, r, r1, r2, group
@@ -255,13 +255,15 @@
         def _():
             within(t, self.n, self.first)
             within(t - self.lag_mid, self.n, self.second)
-            within(t - self.lag_mid - 1, self.n, self.forward)
 
         @pl.when(self.at.end)
         def _():
             within(t, self.n, self.outer)
             within(t - self.lag_end, self.n, self.last)
-            within(t - self.lag_end - 1, self.n, self.forward)
+
+    def step_end(self, t):
+        lag = jnp.where(self.at.mid, self.lag_mid, self.lag_end)
+        within(t - lag, self.n, self.forward)
 
     def collect(self, section):
         other = section.out.at[1 - self.at.y, pl.ds(section.base, section.count * self.r)]
@@ -488,10 +490,12 @@
     qkv = gelu.at[:, pl.ds(0, 3 * HD)]
     w_start = d_mlp.at[pl.ds(0, width), pl.ds(0, 3 * HD)]
     ready = [pltpu.make_async_copy(hidden_all, normed_rows, late_sems.at[0])] + weight_copies(w_start, 1) + rope_copies
-    for copy in ready + fetch:
+    for copy in ready:
         copy.start()
     for copy in ready:
         copy.wait()
+    for copy in fetch:
+        copy.start()
 
     def rope(raw, gain, cos_rows, sin_rows):
         turned = raw * rms_scale(raw) * gain[...]
@@ -534,11 +538,6 @@
         scores = jnp.where(allowed, scores, masked_value)
         powers = jnp.exp(scores - jnp.max(scores, axis=-1, keepdims=True))
         return powers / jnp.sum(powers, axis=-1, keepdims=True)
-
-    for start in range(0, rows_all, wide):
-        rows = slice(start, start + wide)
-        probs = softmax_block(qkv[rows, :HD], qkv[: start + wide, HD : 2 * HD], start, wide)
-        context[rows, :] = dot(probs.astype(bf16), qkv[: start + wide, 2 * HD :]).astype(bf16)
 
     greet(
         [
@@ -561,8 +560,18 @@
         one.first(k, dot(context[span(mine, k, r), :], w_out[...]))
         return 0
 
-    lax.fori_loop(0, n, give1, 0)
-    lax.fori_loop(0, n, first1, 0)
+    def context_block(start):
+        rows = slice(start, start + wide)
+        probs = softmax_block(qkv[rows, :HD], qkv[: start + wide, HD : 2 * HD], start, wide)
+        context[rows, :] = dot(probs.astype(bf16), qkv[: start + wide, 2 * HD :]).astype(bf16)
+
+    for k in range(0, n, 2):
+        context_block(k * r)
+        context_block(half + k * r)
+        lax.fori_loop(k, k + 2, give1, 0)
+        if k:
+            lax.fori_loop(k - 2, k, first1, 0)
+    lax.fori_loop(n - 2, n, first1, 0)
     one.drain()
     for copy in fetch + keep_copies:
         copy.wait()
@@ -1112,6 +1121,7 @@
             mid_load.start()
             chosen_copy(0).start()
 
+        stream.step_end(t)
         return 0
 
     lax.fori_loop(0, stream.steps, step, 0)

time: 540 us -> 527 us (0.976)
  Pallas kernels: 499 us -> 486 us
    pallas_call x1, Pallas kernels: 499 us -> 486 us  [layer_call(): pl.pallas_call(functools.partial(layer_kernel, n, r, chunk, held, shared)...]
where the time goes in v7:
time: 527 us
  Pallas kernels  486 us (92%)
  local copies, waits for them, and re-layouts  24.9 us (5%)
  other arithmetic  14.7 us (3%)
    pallas_call x1, Pallas kernels, layer_call(): pl.pallas_call(functools.partial(layer_kernel, n, r, chunk, held, shared)...  486 us
    transpose x1, local copies, waits for them, and re-layouts, per_device(): grad_chosen[1]  11.3 us
    unnamed x12, local copies, waits for them, and re-layouts  10.8 us

profile of v7, /device:TPU:0, one launch (start us, length us, event | category | flops | bytes accessed | tf_op | source)
XLA Modules:
  0.0 526.6 jit_solution(6035032041302570502)
XLA Ops:
  0.7 1.3 convert_reduce_fusion
  2.0 0.7 pad_maximum_fusion
  2.7 1.4 select_select_fusion.gains_in
  4.2 3.0 multiply_sine_fusion
  7.2 486.3 %layer.1 = (f32[1024,1152]{1,0:T(8,128)}, f32[1024,1152]{1,0:T(8,128)}, f32[2,864,1152]{2,1,0:T(8,128)}, f32[2,1728,1152]{2,1,0:T(8,128)}, f32[2,128,1152]{2,1,0...) custom-call(bf16[256,1152]{1,0:T(8,128)(2,1)} %w_out.1, ...), custom_call_target="tpu_custom_call" | custom-call | tf_op jit(solution)/shard_map/layer/pallas_call | solution.py:1209
  493.5 0.0 copy-start.3
  493.5 0.0 copy-start.2
  493.5 4.1 convert_element_type.18
  497.6 0.0 copy-done.3
  497.6 0.6 fusion
  498.2 0.6 slice_reduce_fusion
  498.8 0.0 copy-done.2
  498.8 1.4 copy.34
  500.2 0.0 copy-start
  500.2 4.1 convert_element_type.19
  504.4 0.0 copy-done
  504.4 0.2 slice_bitcast_fusion.2
  504.5 1.4 copy.36
  505.9 1.4 copy.35
  507.3 0.0 copy-start.1
  507.3 11.3 %slice_bitcast_fusion = (f32[1152,1728]{0,1:T(8,128)}, f32[1152,1728]{0,1:T(8,128)}) fusion(f32[2,1728,1152]{2,1,0:T(8,128)} %get-tuple-element.28), kind=kLoop, calls=%fused_computation | loop fusion | bytes 31850496 | tf_op jit(solution)/shard_map/transpose | solution.py:1314
  518.6 0.0 copy-done.1
  518.6 1.0 copy.39
  519.6 7.0 %copy.40 = f32[1728,1152]{1,0:T(8,128)} copy(f32[1728,1152]{1,0:T(8,128)} %bitcast.21) | data formatting | bytes 15925248
  (6 shorter events, 0.0 us)
Async XLA Ops:
  493.5 4.1 copy-start.3
  493.5 5.3 %copy-start.2 = (f32[2,128,1152]{2,1,0:T(8,128)S(1)}, f32[2,128,1152]{2,1,0:T(8,128)}, u32[]{:S(2)}) copy-start(f32[2,128,1152]{2,1,0:T(8,128)} %get-tuple-element.25) | copy-start | bytes 3538948
  500.2 4.1 copy-start
  507.3 11.3 %copy-start.1 = (f32[2,128,1152]{2,1,0:T(8,128)S(1)}, f32[2,128,1152]{2,1,0:T(8,128)}, u32[]{:S(2)}) copy-start(f32[2,128,1152]{2,1,0:T(8,128)} %get-tuple-element.27) | copy-start | bytes 3538948

commit v8 on v7

--- a/solution.py
+++ b/solution.py
@@ -1299,8 +1299,8 @@
         32,
         3,
         16,
-        (4, 3),
-        6,
+        (5, 3),
+        3,
     )
     output = output.astype(jnp.bfloat16)
     grad_hidden = grad_hidden.astype(jnp.bfloat16)

time: 527 us -> 529 us (level)
  no operation moved by 1% of the time
where the time goes in v8:
time: 529 us; the launch traced here: 528 us
  Pallas kernels  487 us (92%)
  local copies, waits for them, and re-layouts  24.9 us (5%)
  other arithmetic  14.7 us (3%)
    pallas_call x1, Pallas kernels, layer_call(): pl.pallas_call(functools.partial(layer_kernel, n, r, chunk, held, shared)...  487 us
    transpose x1, local copies, waits for them, and re-layouts, per_device(): grad_chosen[1]  11.3 us
    unnamed x12, local copies, waits for them, and re-layouts  10.8 us

profile of v8, /device:TPU:0, one launch (start us, length us, event | category | flops | bytes accessed | tf_op | source)
XLA Modules:
  0.0 527.7 jit_solution(10367660258502390535)
XLA Ops:
  0.7 1.3 convert_reduce_fusion
  2.0 0.7 pad_maximum_fusion
  2.7 1.4 select_select_fusion.gains_in
  4.2 3.0 multiply_sine_fusion
  7.2 487.3 %layer.1 = (f32[1024,1152]{1,0:T(8,128)}, f32[1024,1152]{1,0:T(8,128)}, f32[2,864,1152]{2,1,0:T(8,128)}, f32[2,1728,1152]{2,1,0:T(8,128)}, f32[2,128,1152]{2,1,0...) custom-call(bf16[256,1152]{1,0:T(8,128)(2,1)} %w_out.1, ...), custom_call_target="tpu_custom_call" | custom-call | tf_op jit(solution)/shard_map/layer/pallas_call | solution.py:1209
  494.6 0.0 copy-start.3
  494.6 0.0 copy-start.2
  494.6 4.1 convert_element_type.18
  498.7 0.0 copy-done.3
  498.7 0.6 fusion
  499.2 0.6 slice_reduce_fusion
  499.9 0.0 copy-done.2
  499.9 1.4 copy.34
  501.3 0.0 copy-start
  501.3 4.1 convert_element_type.19
  505.4 0.0 copy-done
  505.4 0.2 slice_bitcast_fusion.2
  505.6 1.4 copy.36
  506.9 1.4 copy.35
  508.3 0.0 copy-start.1
  508.3 11.3 %slice_bitcast_fusion = (f32[1152,1728]{0,1:T(8,128)}, f32[1152,1728]{0,1:T(8,128)}) fusion(f32[2,1728,1152]{2,1,0:T(8,128)} %get-tuple-element.28), kind=kLoop, calls=%fused_computation | loop fusion | bytes 31850496 | tf_op jit(solution)/shard_map/transpose | solution.py:1314
  519.6 0.0 copy-done.1
  519.6 1.0 copy.39
  520.6 7.0 %copy.40 = f32[1728,1152]{1,0:T(8,128)} copy(f32[1728,1152]{1,0:T(8,128)} %bitcast.21) | data formatting | bytes 15925248
  (6 shorter events, 0.0 us)
Async XLA Ops:
  494.6 4.1 copy-start.3
  494.6 5.3 %copy-start.2 = (f32[2,128,1152]{2,1,0:T(8,128)S(1)}, f32[2,128,1152]{2,1,0:T(8,128)}, u32[]{:S(2)}) copy-start(f32[2,128,1152]{2,1,0:T(8,128)} %get-tuple-element.25) | copy-start | bytes 3538948
  501.3 4.1 copy-start
  508.3 11.3 %copy-start.1 = (f32[2,128,1152]{2,1,0:T(8,128)S(1)}, f32[2,128,1152]{2,1,0:T(8,128)}, u32[]{:S(2)}) copy-start(f32[2,128,1152]{2,1,0:T(8,128)} %get-tuple-element.27) | copy-start | bytes 3538948
